TPU v7x, 32 devices: a whole 2x2x4 slice. The times are simulated.
32 devices in a mesh: wide: 8 (over y, x, core), narrow: 4 (over z).
Axes of the slice: x: 2, y: 2, z: 4, core: 2. Of those that a mesh axis runs over, the one named last changes fastest.
Arguments:
- tokens: bfloat16 [32, 128, 2048], P(('wide', 'narrow')), may hold values from -6 to 6
- lengths: int32 [32, 5], P(('wide', 'narrow')), may hold values from 1 to 96, as said below
- gain: bfloat16 [2048], P(('wide', 'narrow')), may hold values from 0.5 to 1.5
- w_in: bfloat16 [2048, 8192], P(('wide', 'narrow')), may hold values from -0.125 to 0.125
- conv_w: bfloat16 [4096, 4], P(('wide', 'narrow')), may hold values from -3 to 3
- conv_b: bfloat16 [4096], P(('wide', 'narrow')), may hold values from -3 to 3
- w_x: bfloat16 [4096, 160], P(('wide', 'narrow')), may hold values from -0.09375 to 0.09375
- w_dt: bfloat16 [4096, 128], P(('wide', 'narrow')), may hold values from -0.5 to 0.5
- dt_bias: bfloat16 [4096], P(('wide', 'narrow')), may hold values from -4 to 1
- skip: bfloat16 [4096], P(('wide', 'narrow')), may hold values from 0.099609375 to 1.8984375
- w_out: bfloat16 [4096, 2048], P(('wide', 'narrow')), may hold values from -0.09375 to 0.09375
- grad_out: bfloat16 [32, 128, 2048], P(('wide', 'narrow')), may hold values from -6 to 6
Outputs:
- block_out: bfloat16 [32, 128, 2048], P(('wide', 'narrow'))
- grad_tokens: bfloat16 [32, 128, 2048], P(('wide', 'narrow'))
- grad_gain: float32 [2048], P(('wide', 'narrow'))
- grad_w_in: float32 [2048, 8192], P(('wide', 'narrow'))
- grad_conv_w: float32 [4096, 4], P(('wide', 'narrow'))
- grad_conv_b: float32 [4096], P(('wide', 'narrow'))
- grad_w_x: float32 [4096, 160], P(('wide', 'narrow'))
- grad_w_dt: float32 [4096, 128], P(('wide', 'narrow'))
- grad_dt_bias: float32 [4096], P(('wide', 'narrow'))
- grad_skip: float32 [4096], P(('wide', 'narrow'))
- grad_w_out: float32 [4096, 2048], P(('wide', 'narrow'))
- beta_mean: float32 [], replicated
- beta_max: float32 [], replicated
Inputs may be any that keep to these rules, and one draw needn't show every extreme that they name: Each row's entries sum to 128; the first 4 are its documents' lengths, the last the length of its padding at the row's end.
All inputs are finite; a program needn't handle non-finite values.
Results may differ from a plain program's by a relative error of at most 0.0096.
Values may be sent and summed in bfloat16 or wider, within the bound.
A program may use at most 384 MiB of HBM per device.

v0:
```python
import jax
import jax.numpy as jnp
from jax import lax
from jax.sharding import PartitionSpec as P

DOCS = 4


highest = lax.Precision.HIGHEST
norm_eps = 1e-05


def segment_ids(lengths_row, count):
    ends = jnp.cumsum(lengths_row)
    places = jnp.arange(count, dtype=jnp.int32)
    return jnp.sum((places[:, None] >= ends[None, :]).astype(jnp.int32), axis=1)


def keep_flags(segment):
    earlier = jnp.concatenate([jnp.full((1,), -1, jnp.int32), segment[:-1]])
    return (earlier == segment).astype(jnp.float32)


def convolve(inputs, conv_w, conv_b, segment):
    count = inputs.shape[0]
    width = conv_w.shape[1]
    total = conv_b[None, :] + conv_w[:, width - 1][None, :] * inputs
    for offset in range(1, width):
        earlier = jnp.pad(inputs, ((offset, 0), (0, 0)))[:count]
        before = jnp.pad(segment, (offset, 0), constant_values=-1)[:count]
        same = (before == segment).astype(jnp.float32)
        total = total + conv_w[:, width - 1 - offset][None, :] * earlier * same[:, None]
    return total


def normalize(inputs, gain_full):
    scale = lax.rsqrt(jnp.mean(inputs * inputs, axis=1, keepdims=True) + norm_eps)
    return inputs * scale * gain_full


def combine_steps(left, right):
    return (left[0] * right[0], right[0] * left[1] + right[1])


def mix_piece(pre, keys, queries, inputs, gate, skip_full, keep, live):
    beta = jax.nn.sigmoid(pre)
    squares = keys * keys
    rates = beta / (1.0 + beta * jnp.sum(squares, axis=1, keepdims=True))
    length = pre.shape[0]
    block = min(32, length)
    blocks = length // block
    channels = pre.shape[1]
    states = keys.shape[1]

    def shaped(array):
        return array.reshape((blocks, block) + array.shape[1:])

    def advance(state, item):
        rate, square, key, query, value, held = item
        decay = held[:, None, None] * (1.0 - rate[:, :, None] * square[:, None, :])
        update = (rate * value)[:, :, None] * key[:, None, :]
        first = update[0] + decay[0] * state
        update = jnp.concatenate([first[None], update[1:]], axis=0)
        _, trail = lax.associative_scan(combine_steps, (decay, update))
        reads = jnp.einsum("ten,tn->te", trail, query, precision=highest)
        return (trail[-1], reads)

    start = jnp.zeros((channels, states), jnp.float32)
    items = tuple((shaped(member) for member in (rates, squares, keys, queries, inputs, keep)))
    _, reads = lax.scan(jax.checkpoint(advance), start, items)
    mixed_out = reads.reshape(length, channels) + skip_full * inputs
    return mixed_out * jax.nn.silu(gate) * live[:, None]


def on_device(
    tokens, lengths, gain, w_in, conv_w, conv_b, w_x, w_dt, dt_bias, skip, w_out, grad_out
):
    whole = (
        lax.all_gather(gain, ("wide", "narrow"), axis=0, tiled=True),
        lax.all_gather(w_in, ("wide", "narrow"), axis=0, tiled=True),
        lax.all_gather(conv_w, ("wide", "narrow"), axis=0, tiled=True),
        lax.all_gather(conv_b, ("wide", "narrow"), axis=0, tiled=True),
        lax.all_gather(w_x, ("wide", "narrow"), axis=0, tiled=True),
        lax.all_gather(w_dt, ("wide", "narrow"), axis=0, tiled=True),
        lax.all_gather(dt_bias, ("wide", "narrow"), axis=0, tiled=True),
        lax.all_gather(skip, ("wide", "narrow"), axis=0, tiled=True),
        lax.all_gather(w_out, ("wide", "narrow"), axis=0, tiled=True),
    )
    full_gain, full_in, full_conv, full_bias, full_x, full_dt, full_dtb, full_skip, full_out = whole
    inputs = tokens[0].astype(jnp.float32)
    length = inputs.shape[0]
    inner = full_in.shape[1] // 2
    rank = full_dt.shape[1]
    states = (full_x.shape[1] - rank) // 2
    segment = segment_ids(lengths[0], length)
    keep = keep_flags(segment)
    live = (segment < DOCS).astype(jnp.float32)
    dims_rows = (((0,), (0,)), ((), ()))
    dims_cols = (((1,), (1,)), ((), ()))
    normed, norm_back = jax.vjp(normalize, inputs, full_gain.astype(jnp.float32))
    normed_low = normed.astype(jnp.bfloat16)
    mixed_in = jnp.dot(normed_low, full_in, preferred_element_type=jnp.float32)
    conv_in = mixed_in[:, :inner]
    gate = mixed_in[:, inner:]

    def conv_local(values, taps, offsets):
        return jax.nn.silu(convolve(values, taps, offsets, segment))

    activated, conv_back = jax.vjp(
        conv_local, conv_in, full_conv.astype(jnp.float32), full_bias.astype(jnp.float32)
    )
    act_low = activated.astype(jnp.bfloat16)
    projected = jnp.dot(act_low, full_x, preferred_element_type=jnp.float32)
    delta_low = projected[:, :rank].astype(jnp.bfloat16)
    keys = projected[:, rank : rank + states]
    queries = projected[:, rank + states :]
    pre = lax.dot_general(
        delta_low, full_dt, dims_cols, preferred_element_type=jnp.float32
    ) + full_dtb.astype(jnp.float32)

    def mix_local(pre_in, key_in, query_in, value_in, gate_in, skip_in):
        return mix_piece(pre_in, key_in, query_in, value_in, gate_in, skip_in, keep, live)

    mixed, mix_back = jax.vjp(
        mix_local,
        pre,
        keys,
        queries,
        act_low.astype(jnp.float32),
        gate,
        full_skip.astype(jnp.float32),
    )
    mixed_low = mixed.astype(jnp.bfloat16)
    result = inputs + jnp.dot(mixed_low, full_out, preferred_element_type=jnp.float32)
    live_beta = jax.nn.sigmoid(pre) * live[:, None]
    local_sum = jnp.sum(live_beta)
    local_peak = jnp.max(live_beta)
    total = lax.psum(local_sum, ("wide", "narrow"))
    peak = lax.pmax(local_peak, ("wide", "narrow"))
    row_count = lax.axis_size("wide") * lax.axis_size("narrow")
    beta_mean = total / float(row_count * length * inner)
    back_in, back_x, back_dt, back_out = (
        lax.all_gather(w_in, ("wide", "narrow"), axis=0, tiled=True),
        lax.all_gather(w_x, ("wide", "narrow"), axis=0, tiled=True),
        lax.all_gather(w_dt, ("wide", "narrow"), axis=0, tiled=True),
        lax.all_gather(w_out, ("wide", "narrow"), axis=0, tiled=True),
    )
    upstream = grad_out[0]
    grad_wout = lax.dot_general(mixed_low, upstream, dims_rows, preferred_element_type=jnp.float32)
    grad_mixed = lax.dot_general(upstream, back_out, dims_cols, preferred_element_type=jnp.float32)
    grad_pre, grad_keys, grad_queries, grad_act_mix, grad_gate, grad_skip = mix_back(grad_mixed)
    grad_pre_low = grad_pre.astype(jnp.bfloat16)
    grad_dtb = jnp.sum(grad_pre_low.astype(jnp.float32), axis=0)
    grad_wdt = lax.dot_general(
        grad_pre_low, delta_low, dims_rows, preferred_element_type=jnp.float32
    )
    grad_delta = jnp.dot(grad_pre_low, back_dt, preferred_element_type=jnp.float32)
    grad_proj_low = jnp.concatenate([grad_delta, grad_keys, grad_queries], axis=1).astype(
        jnp.bfloat16
    )
    grad_wx = lax.dot_general(act_low, grad_proj_low, dims_rows, preferred_element_type=jnp.float32)
    grad_act = grad_act_mix + lax.dot_general(
        grad_proj_low, back_x, dims_cols, preferred_element_type=jnp.float32
    )
    grad_conv_in, grad_taps, grad_offsets = conv_back(grad_act)
    grad_zz_low = jnp.concatenate([grad_conv_in, grad_gate], axis=1).astype(jnp.bfloat16)
    grad_win = lax.dot_general(
        normed_low, grad_zz_low, dims_rows, preferred_element_type=jnp.float32
    )
    grad_normed = lax.dot_general(
        grad_zz_low, back_in, dims_cols, preferred_element_type=jnp.float32
    )
    grad_inputs_norm, grad_gain_full = norm_back(grad_normed)
    grad_inputs = upstream.astype(jnp.float32) + grad_inputs_norm
    partials = (
        grad_gain_full,
        grad_win,
        grad_taps,
        grad_offsets,
        grad_wx,
        grad_wdt,
        grad_dtb,
        grad_skip,
        grad_wout,
    )
    summed = (
        lax.psum_scatter(partials[0], ("wide", "narrow"), scatter_dimension=0, tiled=True),
        lax.psum_scatter(partials[1], ("wide", "narrow"), scatter_dimension=0, tiled=True),
        lax.psum_scatter(partials[2], ("wide", "narrow"), scatter_dimension=0, tiled=True),
        lax.psum_scatter(partials[3], ("wide", "narrow"), scatter_dimension=0, tiled=True),
        lax.psum_scatter(partials[4], ("wide", "narrow"), scatter_dimension=0, tiled=True),
        lax.psum_scatter(partials[5], ("wide", "narrow"), scatter_dimension=0, tiled=True),
        lax.psum_scatter(partials[6], ("wide", "narrow"), scatter_dimension=0, tiled=True),
        lax.psum_scatter(partials[7], ("wide", "narrow"), scatter_dimension=0, tiled=True),
        lax.psum_scatter(partials[8], ("wide", "narrow"), scatter_dimension=0, tiled=True),
    )
    return (
        result.astype(jnp.bfloat16)[None],
        grad_inputs.astype(jnp.bfloat16)[None],
        summed[0],
        summed[1],
        summed[2],
        summed[3],
        summed[4],
        summed[5],
        summed[6],
        summed[7],
        summed[8],
        beta_mean,
        peak,
    )


def solution(mesh):
    in_specs = (
        P(("wide", "narrow"), None, None),
        P(("wide", "narrow"), None),
        P(("wide", "narrow")),
        P(("wide", "narrow"), None),
        P(("wide", "narrow"), None),
        P(("wide", "narrow")),
        P(("wide", "narrow"), None),
        P(("wide", "narrow"), None),
        P(("wide", "narrow")),
        P(("wide", "narrow")),
        P(("wide", "narrow"), None),
        P(("wide", "narrow"), None, None),
    )
    out_specs = (
        P(("wide", "narrow"), None, None),
        P(("wide", "narrow"), None, None),
        P(("wide", "narrow")),
        P(("wide", "narrow"), None),
        P(("wide", "narrow"), None),
        P(("wide", "narrow")),
        P(("wide", "narrow"), None),
        P(("wide", "narrow"), None),
        P(("wide", "narrow")),
        P(("wide", "narrow")),
        P(("wide", "narrow"), None),
        P(),
        P(),
    )
    return jax.shard_map(
        on_device, mesh=mesh, in_specs=in_specs, out_specs=out_specs, check_vma=False
    )
```

profile of v0, /device:TPU:8, one launch (start us, length us, event | category | flops | bytes accessed | tf_op | source)
XLA Modules:
  0.0 5142.3 jit_solution(17524743733423154765)
XLA Ops:
  11.0 42.5 all-reduce.71
  55.1 65.5 %all_gather.32 = bf16[4096,4]{0,1:T(4,128)(2,1)S(1)} all-gather(bf16[128,4]{0,1:T(4,128)(2,1)S(1)} %copy-done.95), channel_id=1, replica_groups=mesh['wide'=8,'narrow'=4] {'wide','narrow'}, dimensions={0}, use_global_device_ids=true | all-gather | bytes 33792 | tf_op jit(solution)/shard_map/all_gather | solution.py:81
  120.7 66.0 %all-gather = bf16[32,1,128]{2,1,0:T(2,128)(2,1)S(1)} all-gather(bf16[1,1,128]{2,1,0:T(2,128)(2,1)S(1)} %bitcast.266), channel_id=1, replica_groups=mesh['wide'=8,'narrow'=4] {'wide','narrow'}, dimensions={0}, use_global_device_ids=true | all-gather | bytes 8448 | tf_op jit(solution)/shard_map/all_gather | solution.py:82
  186.8 63.9 %all-gather.2 = bf16[32,1,128]{2,1,0:T(2,128)(2,1)S(1)} all-gather(bf16[1,1,128]{2,1,0:T(2,128)(2,1)S(1)} %bitcast.267), channel_id=1, replica_groups=mesh['wide'=8,'narrow'=4] {'wide','narrow'}, dimensions={0}, use_global_device_ids=true | all-gather | bytes 8448 | tf_op jit(solution)/shard_map/all_gather | solution.py:86
  251.3 66.0 %all-gather.1 = bf16[32,1,128]{2,1,0:T(2,128)(2,1)S(1)} all-gather(bf16[1,1,128]{2,1,0:T(2,128)(2,1)S(1)} %bitcast.268), channel_id=1, replica_groups=mesh['wide'=8,'narrow'=4] {'wide','narrow'}, dimensions={0}, use_global_device_ids=true | all-gather | bytes 8448 | tf_op jit(solution)/shard_map/all_gather | solution.py:85
  317.6 13.6 fusion.66
  334.7 15.7 multiply_reduce_fusion.4
  352.1 23.6 all-gather.10.cloned.1.call-done
  378.5 52.4 %all-gather.12.cloned.1.call-done = bf16[4096,128]{1,0:T(8,128)(2,1)} async-done(((bf16[128,128]{1,0:T(8,128)(2,1)}), bf16[4096,128]{1,0:T(8,128)(2,1)}) %all-gather.12.cloned.1.call-update) | async-done | bytes 1048592 | tf_op jit(solution)/shard_map/all_gather | solution.py:84
  436.8 500.5 %while.39 = (s32[]{:T(128)}, f32[4096,16]{0,1:T(8,128)S(1)}, f32[4,32,4096]{2,1,0:T(8,128)}, f32[4,4096,16]{1,2,0:T(8,128)}, f32[4,32,4096]{2,1,0:T(8,128)}, /*i...) while((s32[]{:T(128)}, f32[4096,16]{0,1:T(8,128)S(1)}, ...), condition=%wide.region_5.6_spmd, body=%wide.region_4.5_spmd.sunk | while | flops 53084160 | bytes 348936896 | solution.py:70
  537.9 13.6 pad.982
  942.3 1631.2 %while.40 = (s32[]{:T(128)}, f32[4096,16]{0,1:T(8,128)}, f32[4,32,4096]{2,1,0:T(8,128)}, f32[4,32,16]{2,1,0:T(8,128)}, f32[4,32,16]{2,1,0:T(8,128)}, /*index=5*/...) while((s32[]{:T(128)}, f32[4096,16]{0,1:T(8,128)}, ...), condition=%wide.region_11.12_spmd.clone, body=%wide.region_6.11_spmd.clone.sunk | while | flops 121109504 | bytes 1010287296 | solution.py:70
  1182.7 17.6 multiply_add_fusion.15
  1583.8 17.6 multiply_add_fusion.15
  1984.9 17.6 multiply_add_fusion.15
  2385.9 17.6 multiply_add_fusion.15
  2617.0 23.5 fusion.50
  2640.6 40.0 pmax.7
  2680.5 17.4 fusion.55
  2698.0 41.2 all-reduce.76
  2755.0 113.5 %reduce-scatter.12.cloned.1.call-done = f32[128,128]{1,0:T(8,128)} async-done(((f32[4096,128]{1,0:T(8,128)}), f32[128,128]{1,0:T(8,128)}) %reduce-scatter.12.cloned.1.call-update) | async-done | bytes 65552 | tf_op jit(solution)/shard_map/reduce_scatter | solution.py:192
  2868.5 141.0 %reduce-scatter.10.cloned.1.call-done = f32[128,160]{0,1:T(8,128)} async-done(((f32[4096,160]{0,1:T(8,128)}), f32[128,160]{0,1:T(8,128)}) %reduce-scatter.10.cloned.1.call-update) | async-done | bytes 81936 | tf_op jit(solution)/shard_map/reduce_scatter | solution.py:191
  3009.6 710.7 %reduce-scatter.14.cloned.1.call-done = f32[128,2048]{1,0:T(8,128)} async-done(((f32[4096,2048]{1,0:T(8,128)}), f32[128,2048]{1,0:T(8,128)}) %reduce-scatter.14.cloned.1.call-update) | async-done | bytes 1048592 | tf_op jit(solution)/shard_map/reduce_scatter | solution.py:195
  3720.3 1414.1 %reduce-scatter.8.cloned.1.call-done = f32[64,8192]{1,0:T(8,128)} async-done(((f32[2048,8192]{1,0:T(8,128)}), f32[64,8192]{1,0:T(8,128)}) %reduce-scatter.8.cloned.1.call-update) | async-done | bytes 2097168 | tf_op jit(solution)/shard_map/reduce_scatter | solution.py:188
  (1239 shorter events, 2100.0 us)
Async XLA Ops:
  7.2 310.4 %copy-start.47 = (bf16[1,128,2048]{2,1,0:T(8,128)(2,1)S(1)}, bf16[1,128,2048]{2,1,0:T(8,128)(2,1)}, u32[]{:S(2)}) copy-start(bf16[1,128,2048]{2,1,0:T(8,128)(2,1)} %param.16) | copy-start | bytes 1572868
  7.2 47.9 copy-start.95
  7.2 113.5 %copy-start.98 = (bf16[128]{0:T(256)(128)(2,1)S(1)}, bf16[128]{0:T(256)(128)(2,1)}, u32[]{:S(2)}) copy-start(bf16[128]{0:T(256)(128)(2,1)} %param.21) | copy-start | bytes 772
  7.2 179.6 %copy-start.99 = (bf16[128]{0:T(256)(128)(2,1)S(1)}, bf16[128]{0:T(256)(128)(2,1)}, u32[]{:S(2)}) copy-start(bf16[128]{0:T(256)(128)(2,1)} %param.25) | copy-start | bytes 772
  7.2 244.1 %copy-start.100 = (bf16[128]{0:T(256)(128)(2,1)S(1)}, bf16[128]{0:T(256)(128)(2,1)}, u32[]{:S(2)}) copy-start(bf16[128]{0:T(256)(128)(2,1)} %param.24) | copy-start | bytes 772
  7.2 310.3 %all-gather.8.cloned.1.call-start = ((), (), s32[]{:S(2)}) async-start(), calls=%async_computation.5 | async-start | bytes 34603008 | tf_op jit(solution)/shard_map/all_gather | solution.py:80
  8.0 326.6 %all-gather.14.cloned.1.call-start = ((), (), s32[]{:S(2)}) async-start(), calls=%async_computation.8 | async-start | bytes 17301504 | tf_op jit(solution)/shard_map/all_gather | solution.py:87
  8.7 367.0 %all-gather.10.cloned.1.call-start = ((), (), s32[]{:S(2)}) async-start(), calls=%async_computation.6 | async-start | bytes 1351680 | tf_op jit(solution)/shard_map/all_gather | solution.py:83
  9.5 421.4 %all-gather.12.cloned.1.call-start = ((), (), s32[]{:S(2)}) async-start(), calls=%async_computation.7 | async-start | bytes 1081344 | tf_op jit(solution)/shard_map/all_gather | solution.py:84
  10.0 2743.5 %reduce-scatter.16.cloned.1.call-start = ((), (), s32[]{:S(2)}) async-start(), calls=%async_computation.13 | async-start | bytes 2162688
  53.4 277.7 %copy-start.68 = (f32[2048]{0:T(1024)}, f32[2048]{0:T(1024)S(1)}, u32[]{:S(2)}) copy-start(f32[2048]{0:T(1024)S(1)} %convert_element_type.87) | copy-start | bytes 24580
  54.8 65.8 %copy-start.96 = (f32[128]{0:T(128)}, f32[128]{0:T(128)S(1)}, u32[]{:S(2)}) copy-start(f32[128]{0:T(128)S(1)} %fusion.58) | copy-start | bytes 1540
  54.8 276.3 %copy-start.79 = (f32[128]{0:T(128)}, f32[128]{0:T(128)S(1)}, u32[]{:S(2)}) copy-start(f32[128]{0:T(128)S(1)} %fusion.71) | copy-start | bytes 1540
  120.7 213.9 %copy-start.75 = (f32[4096,1]{0,1:T(1,128)}, f32[4096,1]{0,1:T(1,128)S(1)}, u32[]{:S(2)}) copy-start(f32[4096,1]{0,1:T(1,128)S(1)} %get-tuple-element.673) | copy-start | bytes 49156
  120.7 213.9 %copy-start.82 = (f32[4096,1]{0,1:T(1,128)}, f32[4096,1]{0,1:T(1,128)S(1)}, u32[]{:S(2)}) copy-start(f32[4096,1]{0,1:T(1,128)S(1)} %get-tuple-element.674) | copy-start | bytes 49156
  120.7 213.9 %copy-start.84 = (f32[4096,1]{0,1:T(1,128)}, f32[4096,1]{0,1:T(1,128)S(1)}, u32[]{:S(2)}) copy-start(f32[4096,1]{0,1:T(1,128)S(1)} %get-tuple-element.675) | copy-start | bytes 49156
  120.7 213.9 %copy-start.86 = (f32[4096,1]{0,1:T(1,128)}, f32[4096,1]{0,1:T(1,128)S(1)}, u32[]{:S(2)}) copy-start(f32[4096,1]{0,1:T(1,128)S(1)} %get-tuple-element.676) | copy-start | bytes 49156
  377.5 57.7 %copy-start.72 = (f32[128,160]{0,1:T(8,128)}, f32[128,160]{0,1:T(8,128)S(1)}, u32[]{:S(2)}) copy-start(f32[128,160]{0,1:T(8,128)S(1)} %fusion.96) | copy-start | bytes 245764
  377.6 57.7 %copy-start.91 = (f32[128]{0:T(128)}, f32[128]{0:T(128)S(1)}, u32[]{:S(2)}) copy-start(f32[128]{0:T(128)S(1)} %get-tuple-element.671) | copy-start | bytes 1540
  2593.5 275.1 %reduce-scatter.12.cloned.1.call-start = ((), (), s32[]{:S(2)}) async-start(), calls=%async_computation.11 | async-start | bytes 2162688 | tf_op jit(solution)/shard_map/reduce_scatter | solution.py:192
  2595.4 414.2 %reduce-scatter.10.cloned.1.call-start = ((), (), s32[]{:S(2)}) async-start(), calls=%async_computation.10 | async-start | bytes 2703360 | tf_op jit(solution)/shard_map/reduce_scatter | solution.py:191
  2597.5 1122.8 %reduce-scatter.14.cloned.1.call-start = ((), (), s32[]{:S(2)}) async-start(), calls=%async_computation.12 | async-start | bytes 34603008 | tf_op jit(solution)/shard_map/reduce_scatter | solution.py:195
  2611.8 2522.6 %reduce-scatter.8.cloned.1.call-start = ((), (), s32[]{:S(2)}) async-start(), calls=%async_computation.9 | async-start | bytes 69206016 | tf_op jit(solution)/shard_map/reduce_scatter | solution.py:188
  2680.5 61.6 %copy-start.97 = (f32[128]{0:T(128)S(1)}, f32[128]{0:T(128)}, u32[]{:S(2)}) copy-start(f32[128]{0:T(128)} %copy-done.96) | copy-start | bytes 1540
  (288 other events, 1575.6 us)
Sparse Core Ops, SparseCore 0:
  11.0 195.5 all-gather.7
  209.6 114.1 all-gather.13
  326.8 48.8 all-gather.9
  378.5 52.3 all-gather.11
  2593.6 135.5 reduce-scatter.15
  2732.0 136.5 reduce-scatter.11
  2871.4 138.1 reduce-scatter.9
  3012.5 707.7 reduce-scatter.13
  3723.2 1411.1 reduce-scatter.7
where the time goes:
time: 5170 us; the launch traced here: 5140 us
  waiting for transfers between devices  2460 us (48%)
  local copies, waits for them, and re-layouts  1260 us (24%)
  other arithmetic  794 us (15%)
  blocking collectives  385 us (7%)
  matrix products  198 us (4%)
    reduce_scatter x1, waiting for transfers between devices, on_device(): lax.psum_scatter(partials[1], ('wide', 'narrow'), scatter_dimension=0, ti...  1410 us
    pad x168, local copies, waits for them, and re-layouts, advance(): _, trail = lax.associative_scan(combine_steps, (decay, update))  1050 us
    reduce_scatter x1, waiting for transfers between devices, on_device(): lax.psum_scatter(partials[8], ('wide', 'narrow'), scatter_dimension=0, ti...  711 us
    add x32, other arithmetic, combine_steps(): return (left[0] * right[0], right[0] * left[1] + right[1])  161 us
    reduce_scatter x1, waiting for transfers between devices, on_device(): lax.psum_scatter(partials[4], ('wide', 'narrow'), scatter_dimension=0, ti...  141 us
    add_any x16, other arithmetic, combine_steps(): return (left[0] * right[0], right[0] * left[1] + right[1])  138 us
    reduce_scatter x1, waiting for transfers between devices, on_device(): lax.psum_scatter(partials[5], ('wide', 'narrow'), scatter_dimension=0, ti...  114 us
    mul x32, other arithmetic, combine_steps(): return (left[0] * right[0], right[0] * left[1] + right[1])  106 us
  transfers between devices with their start and end apart: 9, of which 6 were waited for; matrix products, arithmetic and copies ran while one was open for 2% of the time, Pallas kernels for 0%

commit v1 on v0

v1 whole, which is shorter than its diff:
```python
import functools
import jax, jax.numpy as jnp
from jax import lax
from jax.experimental import pallas as pl
from jax.experimental.pallas import tpu as pltpu
from jax.sharding import Mesh, PartitionSpec as P

DOCS = 4
EPS = 1e-05
ALL = ("dp", "core", "z")
TP = ("core", "z")

f32 = jnp.float32
bf16 = jnp.bfloat16

def fold(x):
    total = x[:, :128]
    for at in range(128, x.shape[1], 128):
        total = total + x[:, at:at+128]
    return total

def mixer_kernel(states, unroll, chunk, flags_ref, kq3_ref, sk_ref, pre_ref, v_ref, g_ref, dm_ref, skip_ref,
                 m_ref, dg_ref, dpre_ref, dv_ref, dkq_ref, stat_ref, s_ref, h_ref, rate_ref, rv_ref, kb_ref, drr_ref):
    rows = pre_ref.shape[0]
    width = pre_ref.shape[1]
    steps = rows // 8
    wide = states * 128
    spread_rows = kq3_ref.shape[1]
    def spread(i, c):
        r = pl.ds(pl.multiple_of(i * chunk, chunk), chunk)
        left = kq3_ref[r, :]
        for part in range(0, 2 * wide, 512):
            ids = lax.broadcasted_iota(jnp.int32, (spread_rows, 512), 0) % (2 * states)
            col = lax.broadcasted_iota(jnp.int32, (spread_rows, 512), 1) // 128 + part // 128
            hot = jnp.where(ids == col, 1.0, 0.0).astype(bf16)
            kb_ref[r, part:part+512] = jnp.dot(left, hot, preferred_element_type=f32)
        return c
    lax.fori_loop(0, rows // chunk, spread, 0)

    def before(i, c):
        r = pl.ds(pl.multiple_of(i * 64, 64), 64)
        live = flags_ref[r, 1:2]
        beta = jax.nn.sigmoid(pre_ref[r, :])
        part = 1.0 / (1.0 + beta * sk_ref[r, 0:1])
        rate = beta * part
        rate_ref[r, :] = rate
        v = v_ref[r, :]
        rv_ref[r, :] = rate * v
        dpre_ref[r, :] = part * part * beta * (1.0 - beta)
        g = g_ref[r, :]
        sg = jax.nn.sigmoid(g)
        dm = dm_ref[r, :] * live
        dv_ref[r, :] = dm * (g * sg)
        dg_ref[r, :] = dm * (sg * (1.0 + g * (1.0 - sg)))
        return c
    lax.fori_loop(0, rows // 64, before, 0)

    s_ref[0, 0] = jnp.zeros(s_ref.shape[2:], f32)

    group = unroll
    tile = lambda x: jnp.concatenate([x] * (width // 128), axis=1)
    span = group * 8
    at = [slice(j * 8, j * 8 + 8) for j in range(group)]
    def view(ref, i):
        return ref.at[pl.ds(pl.multiple_of(i * span, span), span)]

    def forward(i, carry):
        flags, rates, rvs, vs, kbs, ms = [view(x, i) for x in (flags_ref, rate_ref, rv_ref, v_ref, kb_ref, m_ref)]
        keep = [jnp.broadcast_to(flags[r, 0:1], (8, 128)) for r in at]
        rate = [rates[r, :] for r in at]
        rv = [rvs[r, :] for r in at]
        y = [skip_ref[...] * vs[r, :] for r in at]
        for n in range(states):
            state = s_ref[i, 0, n]
            for j, r in enumerate(at):
                kb = kbs[r, n*128:(n+1)*128]
                qb = kbs[r, wide+n*128:wide+(n+1)*128]
                state = (tile(keep[j]) - rate[j] * tile(kb * kb * keep[j])) * state + rv[j] * tile(kb)
                if j < group - 1:
                    s_ref[i, j + 1, n] = state
                else:
                    s_ref[i + 1, 0, n] = state
                y[j] = y[j] + state * tile(qb)
        for j, r in enumerate(at):
            ms[r, :] = y[j]
        return carry

    lax.fori_loop(0, steps // group, forward, 0)
    h_ref[...] = jnp.zeros_like(h_ref)

    def backward(step, carry):
        i = steps // group - 1 - step
        flags, rates, rvs, vs, kbs, dvs, dpres, drrs = [view(x, i) for x in (flags_ref, rate_ref, rv_ref, v_ref, kb_ref, dv_ref, dpre_ref, drr_ref)]
        keep = [jnp.broadcast_to(flags[r, 0:1], (8, 128)) for r in at]
        rate = [rates[r, :] for r in at]
        rv = [rvs[r, :] for r in at]
        dy = [dvs[r, :] for r in at]
        hk = [jnp.zeros((8, width), f32) for r in at]
        hs2 = [jnp.zeros((8, width), f32) for r in at]
        for n in range(states):
            ah = h_ref[n]
            after_ = s_ref[i + 1, 0, n]
            for j in range(group - 1, -1, -1):
                r = at[j]
                kb = kbs[r, n*128:(n+1)*128]
                qb = kbs[r, wide+n*128:wide+(n+1)*128]
                kk = kb * keep[j]
                held = tile(kb * kk)
                h = dy[j] * tile(qb) + ah
                prior = s_ref[i, j, n]
                hs = h * prior
                hk[j] = hk[j] + h * tile(kb)
                hs2[j] = hs2[j] + hs * held
                kbs[r, n*128:(n+1)*128] = fold(h * rv[j]) - 2.0 * kk * fold(hs * rate[j])
                kbs[r, wide+n*128:wide+(n+1)*128] = fold(dy[j] * after_)
                after_ = prior
                ah = (tile(keep[j]) - rate[j] * held) * h
            h_ref[n] = ah
        for j, r in enumerate(at):
            v = vs[r, :]
            drate = v * hk[j] - hs2[j]
            drrs[r, :] = fold(drate * rate[j] * rate[j]) * (-2.0)
            dpres[r, :] = drate * dpres[r, :]
            dvs[r, :] = rate[j] * hk[j] + skip_ref[...] * dy[j]
            stat_ref[0, 0] += dy[j] * v
        return carry

    stat_ref[...] = jnp.zeros_like(stat_ref)
    lax.fori_loop(0, steps // group, backward, 0)

    first = pl.program_id(0) == 0
    def gather(i, c):
        r = pl.ds(pl.multiple_of(i * chunk, chunk), chunk)
        total = jnp.zeros((chunk, 128), f32)
        for part in range(0, 2 * wide, 512):
            row = lax.broadcasted_iota(jnp.int32, (512, 128), 0) // 128 + part // 128
            col = lax.broadcasted_iota(jnp.int32, (512, 128), 1)
            hot = jnp.where(row == col, 1.0, 0.0).astype(bf16)
            total += jnp.dot(kb_ref[r, part:part+512].astype(bf16), hot, preferred_element_type=f32)
        col = lax.broadcasted_iota(jnp.int32, (128, 128), 1)
        hot = jnp.where(col == 2 * states, 1.0, 0.0).astype(bf16)
        total += jnp.dot(drr_ref[r, :].astype(bf16), hot, preferred_element_type=f32)
        dkq_ref[r, :] = jnp.where(first, total, dkq_ref[r, :] + total)
        return c
    lax.fori_loop(0, rows // chunk, gather, 0)

    def after(i, c):
        r = pl.ds(pl.multiple_of(i * 64, 64), 64)
        live = flags_ref[r, 1:2]
        y = m_ref[r, :]
        g = g_ref[r, :]
        m_ref[r, :] = y * (g * jax.nn.sigmoid(g)) * live
        dg_ref[r, :] = y * dg_ref[r, :]
        shown = (jax.nn.sigmoid(pre_ref[r, :]) * live).reshape(8, 8, width)
        stat_ref[0, 1] += jnp.sum(shown, axis=0)
        stat_ref[0, 2] = jnp.maximum(stat_ref[0, 2], jnp.max(shown, axis=0))
        return c
    lax.fori_loop(0, rows // 64, after, 0)

def mixer(flags, kq3, sk, pre, v, g, dm, skip, states=16, width=256, unroll=1):
    rows, total = pre.shape
    steps = rows // 8
    tiles = total // width
    big = jax.ShapeDtypeStruct((rows, total), f32)
    cut = pl.BlockSpec((rows, width), lambda h: (0, h))
    whole = lambda a: pl.BlockSpec(a.shape, lambda h: (0,) * a.ndim)
    return pl.pallas_call(
        functools.partial(mixer_kernel, states, unroll, min(256, rows)),
        grid=(tiles,),
        out_shape=(big, big, big, big, jax.ShapeDtypeStruct((rows, 128), f32), jax.ShapeDtypeStruct((tiles, 3, 8, width), f32)),
        in_specs=[whole(flags), whole(kq3), whole(sk), cut, cut, cut, cut, pl.BlockSpec((1, width), lambda h: (0, h))],
        out_specs=(cut, cut, cut, cut, pl.BlockSpec((rows, 128), lambda h: (0, 0)), pl.BlockSpec((1, 3, 8, width), lambda h: (h, 0, 0, 0))),
        scratch_shapes=[pltpu.VMEM((steps//unroll+1, unroll, states, 8, width), f32), pltpu.VMEM((states, 8, width), f32)] + [pltpu.VMEM((rows, width), f32)]*2
          + [pltpu.VMEM((rows, 2*states*128), f32), pltpu.VMEM((rows, 128), f32)],
        compiler_params=pltpu.CompilerParams(vmem_limit_bytes=60*1024*1024),
    )(flags, kq3, sk, pre, v, g, dm, skip)


def masks(lengths, count):
    ends = jnp.cumsum(lengths, axis=1)
    places = jnp.arange(count, dtype=jnp.int32)
    segment = jnp.sum((places[:, None, None] >= ends[None, :, :]).astype(jnp.int32), axis=2)
    same = []
    for offset in range(1, 4):
        before = jnp.pad(segment, ((offset, 0), (0, 0)), constant_values=-1)[:count]
        same.append((before == segment).astype(f32))
    return same, (segment < DOCS).astype(f32)


def columns(weights, ways):
    rows, total = weights.shape
    return weights.reshape(rows, 2, total // (2 * ways * 128), ways, 128)


def on_device(tokens, lengths, gain, w_in, conv_w, conv_b, w_x, w_dt, dt_bias, skip, w_out, grad_out):
    ways = lax.axis_size("core") * lax.axis_size("z")
    groups = lax.axis_size("dp")
    length, model = tokens.shape[1:]
    own_d = w_in.shape[0]
    own_e = conv_w.shape[0]
    inner = w_in.shape[1] // 2
    channels = inner // ways
    rank = w_dt.shape[1]
    states = (w_x.shape[1] - rank) // 2
    cols = w_in.reshape(own_d, 2, groups, ways, own_e).transpose(3, 0, 1, 2, 4).reshape(ways, own_d, 2 * channels)
    cols = lax.all_to_all(cols, TP, split_axis=0, concat_axis=0, tiled=True)
    win = lax.all_gather(cols, "dp", axis=0, tiled=True).reshape(model, 2 * channels)
    small = jnp.concatenate([w_x, w_dt, conv_w, conv_b[:, None], dt_bias[:, None], skip[:, None]], axis=1)
    small_width = small.shape[1]
    small = lax.all_gather(small, "dp", axis=0, tiled=True)
    wx = small[:, :rank + 2 * states]
    wdt = small[:, rank + 2 * states:2 * rank + 2 * states]
    rest = small[:, 2 * rank + 2 * states:].astype(f32)
    taps, bias, dtb, skips = rest[:, :4], rest[:, 4], rest[:, 5], rest[:, 6]
    wout = lax.all_gather(w_out, "dp", axis=0, tiled=True)
    gains = lax.all_gather(gain, ALL, axis=0, tiled=True).astype(f32)
    x = tokens[0].astype(f32)
    scale = lax.rsqrt(jnp.mean(x * x, axis=1, keepdims=True) + EPS)
    xn = (x * scale * gains).astype(bf16)
    xns = lax.all_gather(xn, TP, axis=0, tiled=True)
    ups = lax.all_gather(grad_out[0], TP, axis=0, tiled=True)
    lens = lax.all_gather(lengths, TP, axis=0, tiled=True)
    rows = lens.shape[0]
    tall = rows * length

    def time_major(a):
        return a.reshape(rows, length, -1).transpose(1, 0, 2).reshape(tall, -1)

    def row_major(a):
        return a.reshape(length, rows, -1).transpose(1, 0, 2).reshape(tall, -1)

    same, live = masks(lens, length)
    zz = time_major(jnp.dot(xns, win, preferred_element_type=f32))
    u = zz[:, :channels].reshape(length, rows, channels)
    g = zz[:, channels:]
    c = bias + taps[:, 3] * u
    shifted = []
    for offset in range(1, 4):
        earlier = jnp.pad(u, ((offset, 0), (0, 0), (0, 0)))[:length] * same[offset - 1][:, :, None]
        shifted.append(earlier)
        c = c + taps[:, 3 - offset] * earlier
    sig = jax.nn.sigmoid(c)
    v16 = (c * sig).astype(bf16).reshape(tall, channels)
    v = v16.astype(f32)
    p = lax.psum(jnp.dot(v16, wx, preferred_element_type=f32), TP)
    dl = p[:, :rank].astype(bf16)
    kq = p[:, rank:]
    dims_cols = (((1,), (1,)), ((), ()))
    dims_rows = (((0,), (0,)), ((), ()))
    pre = lax.dot_general(dl, wdt, dims_cols, preferred_element_type=f32) + dtb
    dm = time_major(lax.dot_general(ups, wout, dims_cols, preferred_element_type=f32))
    flags = jnp.pad(jnp.stack([same[0].reshape(tall), live.reshape(tall)], axis=1), ((0, 0), (0, 126)))
    hi = kq.astype(bf16)
    mid = (kq - hi.astype(f32)).astype(bf16)
    low = (kq - hi.astype(f32) - mid.astype(f32)).astype(bf16)
    kq3 = jnp.concatenate([hi, mid, low], axis=1)
    keys = kq[:, :states]
    sk = jnp.broadcast_to(jnp.sum(keys * keys, axis=1, keepdims=True), (tall, 8))
    m, dg, dpre, dv, dkq, stats = mixer(flags, kq3, sk, pre, v, g, dm, skips[None], states=states, width=256, unroll=4)
    stats = stats.transpose(1, 2, 0, 3).reshape(3, 8, channels)
    dskip = jnp.sum(stats[0], axis=0)
    total = lax.psum(jnp.sum(stats[1]), ALL)
    peak = lax.pmax(jnp.max(stats[2]), ALL)
    beta_mean = total / float(groups * ways * length * inner)
    m16 = row_major(m).astype(bf16)
    out = jnp.dot(m16, wout, preferred_element_type=f32).astype(bf16)
    out = lax.psum_scatter(out, TP, scatter_dimension=0, tiled=True)
    block_out = (x + out.astype(f32)).astype(bf16)
    grad_wout = lax.dot_general(m16, ups, dims_rows, preferred_element_type=f32).astype(bf16)
    grad_wout = lax.psum_scatter(grad_wout, "dp", scatter_dimension=0, tiled=True)
    dpre16 = dpre.astype(bf16)
    grad_dtb = jnp.sum(dpre16.astype(f32), axis=0)
    grad_wdt = lax.dot_general(dpre16, dl, dims_rows, preferred_element_type=f32)
    ddl = jnp.dot(dpre16, wdt, preferred_element_type=f32)
    dkq = dkq[:, :2 * states] + dkq[:, 2 * states:2 * states + 1] * jnp.pad(keys, ((0, 0), (0, states)))
    dp16 = lax.psum(jnp.concatenate([ddl, dkq], axis=1), TP).astype(bf16)
    grad_wx = lax.dot_general(v16, dp16, dims_rows, preferred_element_type=f32)
    dvt = dv + lax.dot_general(dp16, wx, dims_cols, preferred_element_type=f32)
    dc = (dvt * (sig.reshape(tall, channels) * (1.0 + c.reshape(tall, channels) * (1.0 - sig.reshape(tall, channels))))).reshape(length, rows, channels)
    du = taps[:, 3] * dc
    grad_taps = [jnp.sum(dc * u, axis=(0, 1))]
    for offset in range(1, 4):
        grad_taps.append(jnp.sum(dc * shifted[offset - 1], axis=(0, 1)))
        du = du + taps[:, 3 - offset] * jnp.pad((dc * same[offset - 1][:, :, None])[offset:], ((0, offset), (0, 0), (0, 0)))
    grad_conv = jnp.stack(grad_taps[::-1] + [jnp.sum(dc, axis=(0, 1)), grad_dtb, dskip], axis=1)
    dz = row_major(jnp.concatenate([du.reshape(tall, channels), dg], axis=1)).astype(bf16)
    gwin = lax.dot_general(xns, dz, dims_rows, preferred_element_type=f32).astype(bf16)
    gwin = lax.psum_scatter(gwin, "dp", scatter_dimension=0, tiled=True)
    gwin = lax.all_to_all(gwin.reshape(ways, own_d, 2 * channels), TP, split_axis=0, concat_axis=0, tiled=True)
    grad_win = gwin.reshape(ways, own_d, 2, groups, own_e).transpose(1, 2, 3, 0, 4).reshape(own_d, 2 * inner).astype(f32)
    dxn = lax.dot_general(dz, win, dims_cols, preferred_element_type=f32).astype(bf16)
    dxn = lax.psum_scatter(dxn, TP, scatter_dimension=0, tiled=True).astype(f32)
    small_grad = lax.psum_scatter(jnp.concatenate([grad_wx, grad_wdt, grad_conv], axis=1), "dp", scatter_dimension=0, tiled=True)
    inner_grad = dxn * gains
    dxx = scale * inner_grad - x * (scale * scale * scale) * (jnp.sum(inner_grad * x, axis=1, keepdims=True) / model)
    grad_tokens = (grad_out[0].astype(f32) + dxx).astype(bf16)
    grad_gain = lax.psum_scatter(jnp.sum(dxn * x * scale, axis=0), ALL, scatter_dimension=0, tiled=True)
    at = rank + 2 * states
    return (
        block_out[None],
        grad_tokens[None],
        grad_gain,
        grad_win,
        small_grad[:, at + rank:at + rank + 4],
        small_grad[:, at + rank + 4],
        small_grad[:, :at],
        small_grad[:, at:at + rank],
        small_grad[:, at + rank + 5],
        small_grad[:, at + rank + 6],
        grad_wout.astype(f32),
        beta_mean,
        peak,
    )


def solution(mesh):
    wide, narrow = mesh.devices.shape
    fine = Mesh(mesh.devices.reshape(wide // 2, 2, narrow), ALL)
    cut = (P(ALL, None), P(ALL))
    in_specs = (P(ALL, None, None), cut[0], cut[1], cut[0], cut[0], cut[1], cut[0], cut[0], cut[1], cut[1], cut[0], P(ALL, None, None))
    out_specs = (P(ALL, None, None), P(ALL, None, None), cut[1], cut[0], cut[0], cut[1], cut[0], cut[0], cut[1], cut[1], cut[0], P(), P())
    return jax.shard_map(on_device, mesh=fine, in_specs=in_specs, out_specs=out_specs, check_vma=False)
```

time: 5170 us -> 788 us (0.15)
  waiting for transfers between devices: 2460 us -> 320 us
  local copies, waits for them, and re-layouts: 1260 us -> 41.7 us
  other arithmetic: 794 us -> 29.4 us
  matrix products: 198 us -> 48.7 us
  blocking collectives: 385 us -> 254 us
  Pallas kernels: 0 us -> 58.3 us
    reduce_scatter x4 -> x5, waiting for transfers between devices: 2380 us -> 167 us  [the longest x1 86.8 us: on_device(): dxn = lax.psum_scatter(dxn, TP, scatter_dimension=0, tiled=True).astype(f32)]
    pad x168 -> x1, local copies, waits for them, and re-layouts: 1050 us -> 0.84 us  [on_device(): jnp.pad(jnp.stack([same[0].reshape(tall), live.reshape(tall)], axis=1), (...]
    add x64 -> x2, other arithmetic: 253 us -> 4 us  [the longest x1 2.04 us: on_device(): dkq[:, :2 * states]]
    all_gather x4 -> x2, blocking collectives: 261 us -> 28.2 us  [the longest x1 14.4 us: on_device(): lens = lax.all_gather(lengths, TP, axis=0, tiled=True)]
    add_any x42 -> x0, other arithmetic: 198 us -> none  [the longest x16 138 us: combine_steps(): return (left[0] * right[0], right[0] * left[1] + right[1])]
    dot_general x20 -> x12, matrix products: 198 us -> 48.7 us  [the longest x1 8.55 us: on_device(): lax.dot_general(dz, win, dims_cols, preferred_element_type=f32).astype(bf16)]
    mul x56 -> x4, other arithmetic: 148 us -> 1.48 us  [the longest x3 0.89 us: on_device(): dc * same[offset - 1][:, :, None]]
    while x490 -> x0, local copies, waits for them, and re-layouts: 88.2 us -> none
  transfers between devices with their start and end apart: 9 -> 11, of which waited for: 6 -> 8; matrix products, arithmetic and copies ran while one was open for 2% -> 9% of each run, Pallas kernels for 0% -> 0%
where the time goes in v1:
time: 788 us; the launch traced here: 775 us
  waiting for transfers between devices  320 us (41%)
  blocking collectives  254 us (32%)
  Pallas kernels  58.3 us (7%)
  matrix products  48.7 us (6%)
  local copies, waits for them, and re-layouts  41.7 us (5%)
  other arithmetic  29.4 us (4%)
  between operations  16.6 us (2%)
    reduce_scatter x1, waiting for transfers between devices, on_device(): dxn = lax.psum_scatter(dxn, TP, scatter_dimension=0, tiled=True).astype(f32)  86.8 us
    unnamed x2, blocking collectives  86.2 us
    pallas_call x1, Pallas kernels, mixer(): pl.pallas_call(functools.partial(mixer_kernel, states, unroll, min(256, r...  58.3 us
    all_to_all x1, blocking collectives, on_device(): cols = lax.all_to_all(cols, TP, split_axis=0, concat_axis=0, tiled=True)  52.2 us
    psum x1, waiting for transfers between devices, on_device(): p = lax.psum(jnp.dot(v16, wx, preferred_element_type=f32), TP)  51.4 us
    all_gather x1, waiting for transfers between devices, on_device(): ups = lax.all_gather(grad_out[0], TP, axis=0, tiled=True)  47.1 us
    pmax x1, blocking collectives, on_device(): peak = lax.pmax(jnp.max(stats[2]), ALL)  44.1 us
    reduce_scatter x1, waiting for transfers between devices, on_device(): out = lax.psum_scatter(out, TP, scatter_dimension=0, tiled=True)  43.7 us
  transfers between devices with their start and end apart: 11, of which 8 were waited for; matrix products, arithmetic and copies ran while one was open for 9% of the time, Pallas kernels for 0%

profile of v1, /device:TPU:8, one launch (start us, length us, event | category | flops | bytes accessed | tf_op | source)
XLA Modules:
  0.0 774.7 jit_solution(3487173911650360798)
XLA Ops:
  10.0 40.5 %all-reduce.11 = bf16[2048]{0:T(1024)(128)(2,1)S(1)} all-reduce(bf16[2048]{0:T(1024)(128)(2,1)S(1)} %dynamic-update-slice), channel_id=1, replica_groups=mesh['dp'=4,'core'=2,'z'=4] {'dp','core','z'}, use_global_device_ids=true, to_apply=%add.11 | all-reduce | flops 2048 | bytes 8192
  54.1 52.2 %all_to_all.10 = bf16[8,64,1024]{2,1,0:T(8,128)(2,1)} all-to-all(bf16[8,64,1024]{2,1,0:T(8,128)(2,1)S(1)} %reshape.144), channel_id=1, replica_groups=mesh['dp'=4,'core'=2,'z'=4] {'core','z'}, dimensions={0} | all-to-all | bytes 2097152 | tf_op jit(solution)/shard_map/all_to_all | solution.py:206
  107.7 14.4 %all-gather.1 = s32[8,1,5]{2,1,0:T(1,128)S(1)} all-gather(s32[1,1,5]{2,1,0:T(1,128)S(1)} %bitcast.163), channel_id=1, replica_groups=mesh['dp'=4,'core'=2,'z'=4] {'core','z'}, dimensions={0}, use_global_device_ids=true | all-gather | bytes 180 | tf_op jit(solution)/shard_map/all_gather | solution.py:222
  124.4 13.8 %all_gather.22 = bf16[512,295]{0,1:T(8,128)(2,1)S(1)} all-gather(bf16[128,295]{0,1:T(8,128)(2,1)S(1)} %concatenate.18), channel_id=1, replica_groups=mesh['dp'=4,'core'=2,'z'=4] {'dp'}, dimensions={0}, use_global_device_ids=true | all-gather | bytes 377600 | tf_op jit(solution)/shard_map/all_gather | solution.py:210
  138.8 35.0 %all-gather.9.cloned.1.call-done = bf16[32,64,1024]{2,1,0:T(8,128)(2,1)} async-done(((bf16[8,64,1024]{2,1,0:T(8,128)(2,1)}), bf16[32,64,1024]{2,1,0:T(8,128)(2,1)}) %all-gather.9.cloned.1.call-update) | async-done | bytes 4194320 | tf_op jit(solution)/shard_map/all_gather | solution.py:207
  173.8 7.5 convolution_bitcast_fusion
  192.8 18.2 %all-gather.11.cloned.1.call-done = bf16[512,2048]{1,0:T(8,128)(2,1)} async-done(((bf16[128,2048]{1,0:T(8,128)(2,1)}), bf16[512,2048]{1,0:T(8,128)(2,1)}) %all-gather.11.cloned.1.call-update) | async-done | bytes 2097168 | tf_op jit(solution)/shard_map/all_gather | solution.py:215
  211.0 47.1 %all-gather.13.cloned.1.call-done = bf16[1,1024,2048]{2,1,0:T(8,128)(2,1)} async-done(((bf16[1,128,2048]{2,1,0:T(8,128)(2,1)}), bf16[1,1024,2048]{2,1,0:T(8,128)(2,1)}) %all-gather.13.cloned.1.call-update) | async-done | bytes 4194320 | tf_op jit(solution)/shard_map/all_gather | solution.py:221
  258.1 5.2 fusion.2
  267.9 51.4 %all-reduce.17.cloned.1.call-done = f32[1024,160]{1,0:T(8,128)} async-done(((f32[1024,160]{1,0:T(8,128)}), f32[1024,160]{1,0:T(8,128)}) %all-reduce.17.cloned.1.call-update) | async-done | bytes 655376 | tf_op jit(solution)/shard_map/psum | solution.py:245
  324.7 58.3 %shard_map.219 = (f32[1024,512]{1,0:T(8,128)}, f32[1024,512]{1,0:T(8,128)}, f32[1024,512]{1,0:T(8,128)}, f32[1024,512]{1,0:T(8,128)}, f32[1024,128]{1,0:T(8,128)}, /*index=5*/f32[2,3,8,256]{3,2,1,0:T(8,128)}) custom-call(f32[1024,128]{1,0:T(8,128)} %pad.45.flags_ref, bf16[1024,96]{1,0:T(8,128)(2,1)} %pad_maximum_fusion.1.kq3_ref, ...), custom_call_target="tpu_custom_call" | custom-call | tf_op jit(solution)/shard_map/pallas_call | solution.py:167
  391.3 43.6 %all-reduce.18 = bf16[1024,160]{0,1:T(8,128)(2,1)} all-reduce(f32[1024,160]{0,1:T(8,128)} %pad_maximum_fusion), channel_id=1, replica_groups=mesh['dp'=4,'core'=2,'z'=4] {'core','z'}, use_global_device_ids=true, to_apply=%region_6.7 | all-reduce | flops 163840 | bytes 983040 | tf_op jit(solution)/shard_map/psum | solution.py:276
  434.9 5.8 fusion.50
  450.9 6.2 convolution_convert_fusion.1
  467.1 3.8 fusion.4
  472.5 8.6 %convolution_convert_fusion.2 = bf16[1024,2048]{1,0:T(8,128)(2,1)} fusion(bf16[1024,1024]{1,0:T(8,128)(2,1)S(1)} %bitcast.133, bf16[2048,1024]{1,0:T(8,128)(2,1)} %bitcast.165), kind=kOutput, calls=%fused_computation.8 | convolution fusion | flops 4297064448 | bytes 10485760 | tf_op jit(solution)/shard_map/dot_general | solution.py:291
  482.7 4.3 convolution_convert_fusion
  487.0 23.2 %reduce-scatter.10.cloned.1.call-done = bf16[512,1024]{1,0:T(8,128)(2,1)} async-done(((bf16[2048,1024]{1,0:T(8,128)(2,1)}), bf16[512,1024]{1,0:T(8,128)(2,1)}) %reduce-scatter.10.cloned.1.call-update) | async-done | bytes 1048592 | tf_op jit(solution)/shard_map/reduce_scatter | solution.py:288
  510.2 5.3 all-to-all-start.1
  515.5 44.1 %pmax.7 = f32[]{:T(128)} all-reduce(f32[]{:T(128)} %get-tuple-element.97), channel_id=1, replica_groups=mesh['dp'=4,'core'=2,'z'=4] {'dp','core','z'}, use_global_device_ids=true, to_apply=%region_24.25 | all-reduce | flops 1 | bytes 8 | tf_op jit(solution)/shard_map/pmax | solution.py:263
  565.3 13.0 %reduce-scatter.14.cloned.1.call-done = bf16[128,2048]{1,0:T(8,128)(2,1)} async-done(((bf16[512,2048]{1,0:T(8,128)(2,1)}), bf16[128,2048]{1,0:T(8,128)(2,1)}) %reduce-scatter.14.cloned.1.call-update) | async-done | bytes 524304 | tf_op jit(solution)/shard_map/reduce_scatter | solution.py:270
  580.3 86.8 %reduce-scatter.8.cloned.1.call-done = bf16[128,2048]{1,0:T(8,128)(2,1)} async-done(((bf16[1024,2048]{1,0:T(8,128)(2,1)}), bf16[128,2048]{1,0:T(8,128)(2,1)}) %reduce-scatter.8.cloned.1.call-update) | async-done | bytes 524304 | tf_op jit(solution)/shard_map/reduce_scatter | solution.py:292
  668.5 45.7 %all-reduce.13 = (f32[2048]{0:T(1024)S(1)}, f32[]{:T(128)}) all-reduce(f32[2048]{0:T(1024)S(1)} %get-tuple-element.95, f32[]{:T(128)} %get-tuple-element.98), channel_id=5, replica_groups=mesh['dp'=4,'core'=2,'z'=4] {'dp','core','z'}, use_global_device_ids=true, to_apply=%region_10.11.clone | all-reduce | flops 2049 | bytes 16392
  715.4 43.7 %reduce-scatter.6.cloned.1.call-done = bf16[128,2048]{1,0:T(8,128)(2,1)} async-done(((bf16[1024,2048]{1,0:T(8,128)(2,1)}), bf16[128,2048]{1,0:T(8,128)(2,1)}) %reduce-scatter.6.cloned.1.call-update) | async-done | bytes 524304 | tf_op jit(solution)/shard_map/reduce_scatter | solution.py:267
  (150 shorter events, 80.6 us)
Async XLA Ops:
  7.2 45.4 %copy-start.12 = (bf16[64,8192]{1,0:T(8,128)(2,1)S(1)}, bf16[64,8192]{1,0:T(8,128)(2,1)}, u32[]{:S(2)}) copy-start(bf16[64,8192]{1,0:T(8,128)(2,1)} %param.15) | copy-start | bytes 3145732
  7.2 131.6 %all-gather.7.cloned.1.call-start = ((), (), s32[]{:S(2)}) async-start(), calls=%async_computation.7 | async-start | bytes 4718592 | tf_op jit(solution)/shard_map/all_gather | solution.py:220
  52.5 121.3 %all-gather.9.cloned.1.call-start = ((), (), s32[]{:S(2)}) async-start(), calls=%async_computation.8 | async-start | bytes 5242880 | tf_op jit(solution)/shard_map/all_gather | solution.py:207
  54.1 53.7 %copy-start.23 = (s32[1,5]{1,0:T(1,128)S(1)}, s32[1,5]{1,0:T(1,128)}, u32[]{:S(2)}) copy-start(s32[1,5]{1,0:T(1,128)} %param.13) | copy-start | bytes 64
  54.1 68.6 %copy-start.17 = (bf16[128,128]{1,0:T(8,128)(2,1)S(1)}, bf16[128,128]{1,0:T(8,128)(2,1)}, u32[]{:S(2)}) copy-start(bf16[128,128]{1,0:T(8,128)(2,1)} %param.19) | copy-start | bytes 98308
  106.3 18.0 %copy-start.16 = (bf16[128,160]{0,1:T(8,128)(2,1)S(1)}, bf16[128,160]{0,1:T(8,128)(2,1)}, u32[]{:S(2)}) copy-start(bf16[128,160]{0,1:T(8,128)(2,1)} %param.18) | copy-start | bytes 122884
  106.3 18.0 %copy-start.18 = (bf16[128,4]{0,1:T(4,128)(2,1)S(1)}, bf16[128,4]{0,1:T(4,128)(2,1)}, u32[]{:S(2)}) copy-start(bf16[128,4]{0,1:T(4,128)(2,1)} %param.16) | copy-start | bytes 3076
  106.3 18.0 %copy-start.19 = (bf16[128]{0:T(256)(128)(2,1)S(1)}, bf16[128]{0:T(256)(128)(2,1)}, u32[]{:S(2)}) copy-start(bf16[128]{0:T(256)(128)(2,1)} %param.17) | copy-start | bytes 772
  106.3 18.0 %copy-start.20 = (bf16[128]{0:T(256)(128)(2,1)S(1)}, bf16[128]{0:T(256)(128)(2,1)}, u32[]{:S(2)}) copy-start(bf16[128]{0:T(256)(128)(2,1)} %param.20) | copy-start | bytes 772
  106.3 18.0 %copy-start.21 = (bf16[128]{0:T(256)(128)(2,1)S(1)}, bf16[128]{0:T(256)(128)(2,1)}, u32[]{:S(2)}) copy-start(bf16[128]{0:T(256)(128)(2,1)} %param.21) | copy-start | bytes 772
  106.4 104.7 %all-gather.11.cloned.1.call-start = ((), (), s32[]{:S(2)}) async-start(), calls=%async_computation.10 | async-start | bytes 2621440 | tf_op jit(solution)/shard_map/all_gather | solution.py:215
  107.1 151.0 %all-gather.13.cloned.1.call-start = ((), (), s32[]{:S(2)}) async-start(), calls=%async_computation.16 | async-start | bytes 4718592 | tf_op jit(solution)/shard_map/all_gather | solution.py:221
  107.7 211.5 %all-reduce.17.cloned.1.call-start = ((), (), s32[]{:S(2)}) async-start(), calls=%async_computation.9 | async-start | bytes 2097152 | tf_op jit(solution)/shard_map/psum | solution.py:245
  192.6 317.6 %reduce-scatter.10.cloned.1.call-start = ((), (), s32[]{:S(2)}) async-start(), calls=%async_computation.13 | async-start | bytes 5242880 | tf_op jit(solution)/shard_map/reduce_scatter | solution.py:288
  434.9 5.8 copy-start.2
  457.1 102.5 %reduce-scatter.12.cloned.1.call-start = ((), (), s32[]{:S(2)}) async-start(), calls=%async_computation.14 | async-start | bytes 757760 | tf_op jit(solution)/shard_map/reduce_scatter | solution.py:293
  463.5 114.7 %reduce-scatter.14.cloned.1.call-start = ((), (), s32[]{:S(2)}) async-start(), calls=%async_computation.15 | async-start | bytes 2621440 | tf_op jit(solution)/shard_map/reduce_scatter | solution.py:270
  463.7 3.4 copy-start.24
  470.9 196.2 %reduce-scatter.8.cloned.1.call-start = ((), (), s32[]{:S(2)}) async-start(), calls=%async_computation.12 | async-start | bytes 4718592 | tf_op jit(solution)/shard_map/reduce_scatter | solution.py:292
  481.1 278.1 %reduce-scatter.6.cloned.1.call-start = ((), (), s32[]{:S(2)}) async-start(), calls=%async_computation.11 | async-start | bytes 4718592 | tf_op jit(solution)/shard_map/reduce_scatter | solution.py:267
  487.0 180.1 %copy-start.4 = (bf16[1,128,2048]{2,1,0:T(8,128)(2,1)S(1)}, bf16[1,128,2048]{2,1,0:T(8,128)(2,1)}, u32[]{:S(2)}) copy-start(bf16[1,128,2048]{2,1,0:T(8,128)(2,1)} %param.12) | copy-start | bytes 1572868
  510.2 248.9 %copy-start.7 = (bf16[1,128,2048]{2,1,0:T(8,128)(2,1)S(1)}, bf16[1,128,2048]{2,1,0:T(8,128)(2,1)}, u32[]{:S(2)}) copy-start(bf16[1,128,2048]{2,1,0:T(8,128)(2,1)} %param.23) | copy-start | bytes 1572868
  510.2 248.9 %copy-start.22 = (f32[128]{0:T(128)S(1)}, f32[128]{0:T(128)}, u32[]{:S(2)}) copy-start(f32[128]{0:T(128)} %get-tuple-element.128) | copy-start | bytes 1540
  510.2 251.6 %all-to-all-start.1 = ((bf16[8,64,1024]{2,1,0:T(8,128)(2,1)}), bf16[8,64,1024]{2,1,0:T(8,128)(2,1)S(1)}, u32[]{:S(2)}, u32[]{:S(2)}) async-start(bf16[8,64,1024]{2,1,0:T(8,128)(2,1)} %bitcast.137), calls=%async_computation.4 | async-start | bytes 2097152 | tf_op jit(solution)/shard_map/all_to_all | solution.py:289
  (14 other events, 27.4 us)
Sparse Core Ops, SparseCore 0:
  52.7 64.2 all-gather.6
  118.8 54.9 all-gather.8
  175.7 35.3 all-gather.10
  212.5 45.5 all-gather.12
  260.9 58.2 all-reduce.16
  457.2 52.9 reduce-scatter.9
  514.0 25.4 reduce-scatter.11
  542.4 35.8 reduce-scatter.13
  580.6 86.4 reduce-scatter.7
  669.3 89.7 reduce-scatter.5

commit v2 on v1

--- a/solution.py
+++ b/solution.py
@@ -176,6 +176,586 @@
     )(flags, kq3, sk, pre, v, g, dm, skip)
 
 
+MESH = pl.DeviceIdType.MESH
+
+
+def flip(value, bit):
+    return value + bit * (1 - 2 * ((value // bit) % 2))
+
+
+def place():
+    d, c, z = lax.axis_index("dp"), lax.axis_index("core"), lax.axis_index("z")
+    return d, c, z
+
+
+def put(src, dst, send, recv, device):
+    copy = pltpu.make_async_remote_copy(src_ref=src, dst_ref=dst, send_sem=send, recv_sem=recv, device_id=device, device_id_type=MESH)
+    copy.start()
+    return copy
+
+
+def landed(slot, sem, device):
+    pltpu.make_async_remote_copy(src_ref=slot, dst_ref=slot, send_sem=sem, recv_sem=sem, device_id=device, device_id_type=MESH).wait_recv()
+
+
+def sent(slot, sem, device):
+    pltpu.make_async_remote_copy(src_ref=slot, dst_ref=slot, send_sem=sem, recv_sem=sem, device_id=device, device_id_type=MESH).wait_send()
+
+
+def greet(devices):
+    barrier = pltpu.get_barrier_semaphore()
+    for device in devices:
+        pl.semaphore_signal(barrier, inc=1, device_id=device, device_id_type=MESH)
+    pl.semaphore_wait(barrier, len(devices))
+
+
+def mates():
+    return [(a, k) for k in (0, 1, 3, 2) for a in (1, 0) if (a, k) != (0, 0)]
+
+
+def mate(step, sign=1):
+    d, c, z = place()
+    a, k = step
+    return d, (flip(c, 1) if a else c), lax.rem(z + sign * k + 4, 4)
+
+
+def rank_of(device):
+    return device[1] * 4 + device[2]
+
+
+def front_kernel(tok_ref, up_ref, cols_ref, wout_ref, small_ref, meta_ref,
+                 xs_ref, ups_ref, win_ref, wouts_ref, smalls_ref, metas_ref,
+                 own_sem, ms, mr, qs, qr, xls, xlr, xrs, xrr, xcs, xcr, as_, ar, ps, pr, rs, rr, ws, wr):
+    d, c, z = place()
+    j = c * 4 + z
+    me = (d, c, z)
+    dx, dy, dd = flip(d, 1), flip(d, 2), flip(flip(d, 1), 2)
+    xn, yn, dn = (dx, c, z), (dy, c, z), (dd, c, z)
+    sib = (d, flip(c, 1), z)
+    left = (d, c, lax.rem(z + 3, 4))
+    right = (d, c, lax.rem(z + 1, 4))
+    steps = mates()
+    greet([mate(s) for s in steps] + [xn, yn, dn])
+    half = cols_ref.shape[1]
+    own = [
+        pltpu.make_async_copy(tok_ref.at[0], xs_ref.at[j], own_sem.at[0]),
+        pltpu.make_async_copy(up_ref.at[0], ups_ref.at[j], own_sem.at[1]),
+        pltpu.make_async_copy(cols_ref.at[j], win_ref.at[d, j], own_sem.at[2]),
+        pltpu.make_async_copy(wout_ref, wouts_ref.at[d], own_sem.at[3]),
+        pltpu.make_async_copy(small_ref, smalls_ref.at[d], own_sem.at[4]),
+        pltpu.make_async_copy(meta_ref, metas_ref.at[d, j], own_sem.at[5]),
+    ]
+    for copy in own:
+        copy.start()
+    pending = []
+    for i, s in enumerate(steps):
+        to = mate(s)
+        pending.append(put(meta_ref, metas_ref.at[d, j], ms.at[i], mr.at[i], to))
+    for i, to in enumerate((xn, yn, dn)):
+        pending.append(put(small_ref, smalls_ref.at[d], ps.at[16 + i], pr.at[16 + i], to))
+    for i, s in enumerate(steps):
+        to = mate(s)
+        pending.append(put(cols_ref.at[rank_of(to)], win_ref.at[d, j], as_.at[i], ar.at[i], to))
+    own[2].wait()
+    pending.append(put(win_ref.at[d, j], win_ref.at[d, j], ps.at[7], pr.at[7], xn))
+    pending.append(put(win_ref.at[d, j], win_ref.at[d, j], ps.at[15], pr.at[15], yn))
+
+    def row_start(ref, out, base):
+        pending.append(put(ref.at[0], out.at[j], xcs.at[base + z], xcr.at[base + z], sib))
+
+        @pl.when(z < 3)
+        def _():
+            put(ref.at[0], out.at[j], xls.at[base], xlr.at[base], right)
+
+        @pl.when(z > 0)
+        def _():
+            put(ref.at[0], out.at[j], xrs.at[base], xrr.at[base], left)
+
+    def row_hop(out, base, i):
+        @pl.when(z > i)
+        def _():
+            at = z - 1 - i
+            slot = out.at[c * 4 + at]
+            landed(slot, xlr.at[base + i], left)
+            if i < 2:
+                @pl.when(z < 3)
+                def _():
+                    put(slot, slot, xls.at[base + i + 1], xlr.at[base + i + 1], right)
+            put(slot, slot, xcs.at[base + at], xcr.at[base + at], sib)
+
+        @pl.when(z < 3 - i)
+        def _():
+            at = z + 1 + i
+            slot = out.at[c * 4 + at]
+            landed(slot, xrr.at[base + i], right)
+            if i < 2:
+                @pl.when(z > 0)
+                def _():
+                    put(slot, slot, xrs.at[base + i + 1], xrr.at[base + i + 1], left)
+            put(slot, slot, xcs.at[base + at], xcr.at[base + at], sib)
+
+    def row_end(out, base):
+        for i in range(3):
+            @pl.when((z < 3) & (z >= i))
+            def _():
+                sent(out.at[j], xls.at[base + i], right)
+
+            @pl.when((z > 0) & (z <= 3 - i))
+            def _():
+                sent(out.at[j], xrs.at[base + i], left)
+        for at in range(4):
+            landed(out.at[flip(c, 1) * 4 + at], xcr.at[base + at], sib)
+
+            @pl.when(z != at)
+            def _():
+                sent(out.at[j], xcs.at[base + at], sib)
+
+    row_start(tok_ref, xs_ref, 0)
+    own[5].wait()
+    for i, s in enumerate(steps):
+        landed(metas_ref.at[d, rank_of(mate(s, -1))], mr.at[i], xn)
+    for i, to in enumerate((xn, yn, dn)):
+        pending.append(put(metas_ref.at[d], metas_ref.at[d], qs.at[i], qr.at[i], to))
+    for i, s in enumerate(steps):
+        src = mate(s, -1)
+        slot = win_ref.at[d, rank_of(src)]
+        landed(slot, ar.at[i], src)
+        pending.append(put(slot, slot, ps.at[i], pr.at[i], xn))
+        pending.append(put(slot, slot, ps.at[8 + i], pr.at[8 + i], yn))
+    row_hop(xs_ref, 0, 0)
+    row_start(up_ref, ups_ref, 4)
+    halves = wout_ref.shape[0] // 2
+    pending.append(put(wout_ref, wouts_ref.at[d], ws.at[0], wr.at[0], xn))
+    pending.append(put(wout_ref, wouts_ref.at[d], ws.at[1], wr.at[1], yn))
+    order = [7] + list(range(7))
+    slots = {7: j}
+    for i, s in enumerate(steps):
+        slots[i] = rank_of(mate(s, -1))
+    for k, i in enumerate(order):
+        slot = win_ref.at[dx, slots[i]]
+        landed(slot, pr.at[i], xn)
+        if k % 2 == 0:
+            pending.append(put(slot, slot, rs.at[k // 2], rr.at[k // 2], yn))
+        slot = win_ref.at[dy, slots[i]]
+        landed(slot, pr.at[8 + i], yn)
+        if k % 2 == 1:
+            pending.append(put(slot, slot, rs.at[4 + k // 2], rr.at[4 + k // 2], xn))
+        if k == 3:
+            row_hop(xs_ref, 0, 1)
+            row_hop(ups_ref, 4, 0)
+    row_hop(xs_ref, 0, 2)
+    row_hop(ups_ref, 4, 1)
+    slot = wouts_ref.at[dx]
+    landed(slot, wr.at[0], xn)
+    slot = wouts_ref.at[dx, pl.ds(0, halves)]
+    pending.append(put(slot, slot, ws.at[2], wr.at[2], yn))
+    slot = wouts_ref.at[dy]
+    landed(slot, wr.at[1], yn)
+    slot = wouts_ref.at[dy, pl.ds(halves, halves)]
+    pending.append(put(slot, slot, ws.at[3], wr.at[3], xn))
+    row_hop(ups_ref, 4, 2)
+    for k, i in enumerate(order):
+        slot = win_ref.at[dd, slots[i]]
+        if k % 2 == 0:
+            landed(slot, rr.at[k // 2], yn)
+        else:
+            landed(slot, rr.at[4 + k // 2], xn)
+    landed(wouts_ref.at[dd, pl.ds(0, halves)], wr.at[2], yn)
+    landed(wouts_ref.at[dd, pl.ds(halves, halves)], wr.at[3], xn)
+    for i, (to, at) in enumerate(((xn, dx), (yn, dy), (dn, dd))):
+        landed(smalls_ref.at[at], pr.at[16 + i], to)
+        landed(metas_ref.at[at], qr.at[i], to)
+    row_end(xs_ref, 0)
+    row_end(ups_ref, 4)
+    for copy in own[:2] + own[3:5]:
+        copy.wait()
+    for copy in pending:
+        copy.wait_send()
+
+
+def front(tokens, upstream, cols, w_out, small, meta):
+    groups, ways = lax.axis_size("dp"), cols.shape[0]
+    like = jax.ShapeDtypeStruct
+    length, model = tokens.shape[1:]
+    dma = lambda n: pltpu.SemaphoreType.DMA((n,))
+    some = pl.BlockSpec(memory_space=pl.ANY)
+    return pl.pallas_call(
+        front_kernel,
+        out_shape=(
+            like((ways, length, model), bf16),
+            like((ways, length, model), bf16),
+            like((groups,) + cols.shape, bf16),
+            like((groups,) + w_out.shape, bf16),
+            like((groups,) + small.shape, bf16),
+            like((groups, ways) + meta.shape, bf16),
+        ),
+        in_specs=[some] * 6,
+        out_specs=(some,) * 6,
+        scratch_shapes=[dma(6), dma(7), dma(7), dma(3), dma(3), dma(8), dma(8), dma(8), dma(8), dma(8), dma(8), dma(7), dma(7), dma(19), dma(19), dma(8), dma(8), dma(4), dma(4)],
+        compiler_params=pltpu.CompilerParams(collective_id=0, has_side_effects=True, vmem_limit_bytes=16 * 1024 * 1024),
+    )(tokens, upstream, cols, w_out, small, meta)
+
+
+PIECES = 4
+
+
+def total_kernel(part_ref, out_ref, sib_ref, base_ref, left_ref, right_ref, tor_ref, tol_ref, ss, sr, ls, lr, rs, rr, os_, or_):
+    d, c, z = place()
+    sib = (d, flip(c, 1), z)
+    left = (d, c, lax.rem(z + 3, 4))
+    right = (d, c, lax.rem(z + 1, 4))
+    rows = part_ref.shape[0] // 2
+    piece = rows // PIECES
+    mine, theirs = c * rows, flip(c, 1) * rows
+    barrier = pltpu.get_barrier_semaphore()
+    pl.semaphore_signal(barrier, inc=1, device_id=sib, device_id_type=MESH)
+    pl.semaphore_signal(barrier, inc=1, device_id=left, device_id_type=MESH)
+    pl.semaphore_signal(barrier, inc=1, device_id=right, device_id_type=MESH)
+    pl.semaphore_wait(barrier, 3)
+
+    def cut(p):
+        return pl.ds(p * piece, piece)
+
+    def far(base, p):
+        return pl.ds(pl.multiple_of(base + p * piece, 8), piece)
+
+    for p in range(PIECES):
+        put(part_ref.at[far(theirs, p)], sib_ref.at[cut(p)], ss.at[p], sr.at[p], sib)
+    for p in range(PIECES):
+        landed(sib_ref.at[cut(p)], sr.at[p], sib)
+        base_ref[cut(p), :] = part_ref[far(mine, p), :] + sib_ref[cut(p), :]
+
+        @pl.when(z == 0)
+        def _():
+            put(base_ref.at[cut(p)], left_ref.at[cut(p)], rs.at[p], lr.at[p], right)
+
+        @pl.when(z == 3)
+        def _():
+            put(base_ref.at[cut(p)], right_ref.at[cut(p)], ls.at[p], rr.at[p], left)
+
+    def from_left(p):
+        landed(left_ref.at[cut(p)], lr.at[p], left)
+
+        @pl.when(z < 3)
+        def _():
+            tor_ref[cut(p), :] = base_ref[cut(p), :] + left_ref[cut(p), :]
+            put(tor_ref.at[cut(p)], left_ref.at[cut(p)], rs.at[p], lr.at[p], right)
+
+    def from_right(p):
+        landed(right_ref.at[cut(p)], rr.at[p], right)
+
+        @pl.when(z > 0)
+        def _():
+            tol_ref[cut(p), :] = base_ref[cut(p), :] + right_ref[cut(p), :]
+            put(tol_ref.at[cut(p)], right_ref.at[cut(p)], ls.at[p], rr.at[p], left)
+
+    def finish(p):
+        value = base_ref[cut(p), :]
+        out_ref[far(mine, p), :] = value
+
+        @pl.when(z > 0)
+        def _():
+            out_ref[far(mine, p), :] += left_ref[cut(p), :]
+
+        @pl.when(z < 3)
+        def _():
+            out_ref[far(mine, p), :] += right_ref[cut(p), :]
+
+        put(out_ref.at[far(mine, p)], out_ref.at[far(mine, p)], os_.at[p], or_.at[p], sib)
+
+    @pl.when(z == 1)
+    def _():
+        for p in range(PIECES):
+            from_left(p)
+
+    @pl.when(z < 3)
+    def _():
+        for p in range(PIECES):
+            from_right(p)
+
+    @pl.when(z >= 2)
+    def _():
+        for p in range(PIECES):
+            from_left(p)
+
+    for p in range(PIECES):
+        finish(p)
+    for p in range(PIECES):
+        landed(out_ref.at[far(theirs, p)], or_.at[p], sib)
+        sent(out_ref.at[far(mine, p)], os_.at[p], sib)
+        sent(part_ref.at[far(theirs, p)], ss.at[p], sib)
+
+        @pl.when(z < 3)
+        def _():
+            sent(base_ref.at[cut(p)], rs.at[p], right)
+
+        @pl.when(z > 0)
+        def _():
+            sent(base_ref.at[cut(p)], ls.at[p], left)
+
+
+def group_total(part, which):
+    rows = part.shape[0] // 2
+    dma = lambda: pltpu.SemaphoreType.DMA((PIECES,))
+    here = pl.BlockSpec(memory_space=pltpu.VMEM)
+    return pl.pallas_call(
+        total_kernel,
+        out_shape=jax.ShapeDtypeStruct(part.shape, f32),
+        in_specs=[here],
+        out_specs=here,
+        scratch_shapes=[pltpu.VMEM((rows, 128), f32)] * 6 + [dma() for _ in range(8)],
+        compiler_params=pltpu.CompilerParams(collective_id=which, has_side_effects=True, vmem_limit_bytes=16 * 1024 * 1024),
+    )(part)
+
+
+def add_rows(dst, sources):
+    rows = dst.shape[0]
+    step = 16
+
+    def body(i, carry):
+        r = pl.ds(pl.multiple_of(i * step, step), step)
+        value = sources[0][r, :].astype(f32)
+        for more in sources[1:]:
+            value = value + more[r, :].astype(f32)
+        dst[r, :] = value.astype(dst.dtype)
+        return carry
+
+    lax.fori_loop(0, rows // step, body, 0)
+
+
+class Line:
+    def __init__(self, part, out, sib, send, left, right, sems):
+        self.part, self.out, self.sib, self.send, self.left, self.right = part, out, sib, send, left, right
+        self.ss, self.sr, self.gs, self.lr, self.rr = sems
+        d, c, z = place()
+        self.c = c
+        self.other = (d, flip(c, 1), z)
+        self.to_left = (d, c, lax.rem(z + 3, 4))
+        self.to_right = (d, c, lax.rem(z + 1, 4))
+
+    def start(self):
+        for zp in (3, 0, 2, 1):
+            put(self.part.at[flip(self.c, 1), zp], self.sib.at[zp], self.ss.at[zp], self.sr.at[zp], self.other)
+
+    def step(self, zs, k):
+        for zp in range(4):
+            if zp > zs and k == 3 - zp + zs:
+                landed(self.sib.at[zp], self.sr.at[zp], self.other)
+                terms = [self.part.at[self.c, zp], self.sib.at[zp]]
+                if zs > 0:
+                    landed(self.left.at[zp], self.lr.at[zp], self.to_left)
+                    terms.append(self.left.at[zp])
+                add_rows(self.send.at[zp], terms)
+                put(self.send.at[zp], self.left.at[zp], self.gs.at[zp], self.lr.at[zp], self.to_right)
+            if zp < zs and k == zp + 3 - zs:
+                landed(self.sib.at[zp], self.sr.at[zp], self.other)
+                terms = [self.part.at[self.c, zp], self.sib.at[zp]]
+                if zs < 3:
+                    landed(self.right.at[zp], self.rr.at[zp], self.to_right)
+                    terms.append(self.right.at[zp])
+                add_rows(self.send.at[zp], terms)
+                put(self.send.at[zp], self.right.at[zp], self.gs.at[zp], self.rr.at[zp], self.to_left)
+
+    def finish(self, zs):
+        landed(self.sib.at[zs], self.sr.at[zs], self.other)
+        terms = [self.part.at[self.c, zs], self.sib.at[zs]]
+        if zs > 0:
+            landed(self.left.at[zs], self.lr.at[zs], self.to_left)
+            terms.append(self.left.at[zs])
+        if zs < 3:
+            landed(self.right.at[zs], self.rr.at[zs], self.to_right)
+            terms.append(self.right.at[zs])
+        add_rows(self.out, terms)
+
+    def close(self, zs):
+        for zp in range(4):
+            sent(self.sib.at[zp], self.ss.at[zp], self.other)
+            if zp != zs:
+                sent(self.send.at[zp], self.gs.at[zp], self.other)
+
+
+class Plane:
+    def __init__(self, part, out, xa, yb, sx, sy, rx, ry, sems):
+        self.part, self.out, self.xa, self.yb, self.sx, self.sy, self.rx, self.ry = part, out, xa, yb, sx, sy, rx, ry
+        self.ss, self.rs = sems
+        d, c, z = place()
+        self.d, self.dx, self.dy, self.dd = d, flip(d, 1), flip(d, 2), flip(flip(d, 1), 2)
+        self.xn, self.yn = (self.dx, c, z), (self.dy, c, z)
+        half = part.shape[1] // 2
+        self.a, self.b = pl.ds(0, half), pl.ds(half, half)
+
+    def start(self):
+        p = self.part
+        self.sends = [
+            put(p.at[self.dd, self.a], self.xa, self.ss.at[0], self.rs.at[0], self.xn),
+            put(p.at[self.dd, self.b], self.yb, self.ss.at[1], self.rs.at[1], self.yn),
+            put(p.at[self.dx, self.a], self.rx.at[self.a], self.ss.at[2], self.rs.at[2], self.xn),
+            put(p.at[self.dy, self.b], self.ry.at[self.b], self.ss.at[3], self.rs.at[3], self.yn),
+        ]
+
+    def middle(self):
+        p = self.part
+        landed(self.xa, self.rs.at[0], self.xn)
+        add_rows(self.sy, [p.at[self.dy, self.a], self.xa])
+        self.sends.append(put(self.sy, self.ry.at[self.a], self.ss.at[4], self.rs.at[4], self.yn))
+        landed(self.yb, self.rs.at[1], self.yn)
+        add_rows(self.sx, [p.at[self.dx, self.b], self.yb])
+        self.sends.append(put(self.sx, self.rx.at[self.b], self.ss.at[5], self.rs.at[5], self.xn))
+
+    def finish(self):
+        landed(self.rx.at[self.a], self.rs.at[2], self.xn)
+        landed(self.ry.at[self.b], self.rs.at[3], self.yn)
+        landed(self.ry.at[self.a], self.rs.at[4], self.yn)
+        landed(self.rx.at[self.b], self.rs.at[5], self.xn)
+        add_rows(self.out, [self.part.at[self.d], self.rx, self.ry])
+
+    def close(self):
+        for copy in self.sends:
+            copy.wait_send()
+
+
+def plane_scratch(rows, columns, dtype):
+    half = pltpu.VMEM((rows // 2, columns), dtype)
+    full = pltpu.VMEM((rows, columns), dtype)
+    return [half, half, half, half, full, full, pltpu.SemaphoreType.DMA((6,)), pltpu.SemaphoreType.DMA((6,))]
+
+
+def line_scratch(rows, columns, dtype):
+    four = pltpu.VMEM((4, rows, columns), dtype)
+    return [four] * 4 + [pltpu.SemaphoreType.DMA((4,))] * 5
+
+
+def back_kernel(dxn_ref, outp_ref, gwin_ref, gwout_ref, small_ref,
+                dxns_ref, outs_ref, gwins_ref, gwouts_ref, smalls_ref, *scratch):
+    lines = [Line(dxn_ref, dxns_ref, *scratch[0:4], scratch[4:9]), Line(outp_ref, outs_ref, *scratch[9:13], scratch[13:18])]
+    scratch = scratch[18:]
+    fin, own, as_, ar = scratch[:4]
+    scratch = scratch[4:]
+    planes = []
+    for part, out in ((gwin_ref, fin), (gwout_ref, gwouts_ref), (small_ref, smalls_ref)):
+        planes.append(Plane(part, out, *scratch[:6], scratch[6:8]))
+        scratch = scratch[8:]
+    d, c, z = place()
+    j = c * 4 + z
+    steps = mates()
+    greet([mate(s) for s in steps] + [planes[0].xn, planes[0].yn])
+    lines[0].start()
+    planes[0].start()
+    lines[1].start()
+
+    def along(line, k):
+        for zs in range(4):
+            @pl.when(z == zs)
+            def _():
+                if k < 3:
+                    line.step(zs, k)
+                else:
+                    line.finish(zs)
+                    line.close(zs)
+
+    along(lines[0], 0)
+    along(lines[1], 0)
+    planes[1].start()
+    planes[2].start()
+    along(lines[0], 1)
+    planes[0].middle()
+    along(lines[0], 2)
+    planes[0].finish()
+    block = fin.shape[0] // 8
+    def rows_of(rank):
+        return fin.at[pl.ds(pl.multiple_of(rank * block, 16), block)]
+    keep = pltpu.make_async_copy(rows_of(j), gwins_ref.at[j], own)
+    keep.start()
+    pending = []
+    for i, s in enumerate(steps):
+        to = mate(s)
+        pending.append(put(rows_of(rank_of(to)), gwins_ref.at[j], as_.at[i], ar.at[i], to))
+    along(lines[0], 3)
+    planes[1].middle()
+    planes[2].middle()
+    along(lines[1], 1)
+    planes[1].finish()
+    planes[2].finish()
+    along(lines[1], 2)
+    for i, s in enumerate(steps):
+        src = mate(s, -1)
+        landed(gwins_ref.at[rank_of(src)], ar.at[i], src)
+    along(lines[1], 3)
+    keep.wait()
+    for copy in pending:
+        copy.wait_send()
+    for plane in planes:
+        plane.close()
+
+
+def back(dxn, outp, gwin, gwout, small):
+    like = jax.ShapeDtypeStruct
+    here = pl.BlockSpec(memory_space=pltpu.VMEM)
+    rows, columns = dxn.shape[2:]
+    return pl.pallas_call(
+        back_kernel,
+        out_shape=(
+            like((rows, columns), f32),
+            like((rows, columns), f32),
+            like((8, gwin.shape[1] // 8, gwin.shape[2]), bf16),
+            like(gwout.shape[1:], f32),
+            like(small.shape[1:], f32),
+        ),
+        in_specs=[here] * 5,
+        out_specs=(here,) * 5,
+        scratch_shapes=line_scratch(rows, columns, bf16) + line_scratch(rows, columns, bf16)
+        + [pltpu.VMEM(gwin.shape[1:], bf16), pltpu.SemaphoreType.DMA(()), pltpu.SemaphoreType.DMA((7,)), pltpu.SemaphoreType.DMA((7,))]
+        + plane_scratch(*gwin.shape[1:], bf16) + plane_scratch(*gwout.shape[1:], bf16) + plane_scratch(*small.shape[1:], f32),
+        compiler_params=pltpu.CompilerParams(collective_id=3, has_side_effects=True, vmem_limit_bytes=60 * 1024 * 1024),
+    )(dxn, outp, gwin, gwout, small)
+
+
+def tiny_kernel(part_ref, out_ref, near_ref, sum_ref, far_ref, ns, nr, fs, fr):
+    d, c, z = place()
+    j = c * 4 + z
+    steps = mates()
+    planes = [(flip(d, 1), c, z), (flip(d, 2), c, z), (flip(flip(d, 1), 2), c, z)]
+    greet([mate(s) for s in steps] + planes)
+    for i, s in enumerate(steps):
+        to = mate(s)
+        put(part_ref.at[rank_of(to)], near_ref.at[i], ns.at[i], nr.at[i], to)
+    row = lax.broadcasted_iota(jnp.int32, (8, 128), 0)
+    lane = lax.broadcasted_iota(jnp.int32, (8, 128), 1)
+    peak = (row == 4) & (lane == 1)
+
+    def join(a, b):
+        return jnp.where(peak, jnp.maximum(a, b), a + b)
+
+    value = part_ref[j]
+    for i, s in enumerate(steps):
+        landed(near_ref.at[i], nr.at[i], mate(s, -1))
+        value = join(value, near_ref[i])
+    sum_ref[...] = value
+    for i, to in enumerate(planes):
+        put(sum_ref, far_ref.at[i], fs.at[i], fr.at[i], to)
+    for i, to in enumerate(planes):
+        landed(far_ref.at[i], fr.at[i], to)
+        value = join(value, far_ref[i])
+    out_ref[...] = value
+    for i, to in enumerate(planes):
+        sent(sum_ref, fs.at[i], to)
+    for i, s in enumerate(steps):
+        sent(near_ref.at[i], ns.at[i], mate(s))
+
+
+def tiny(part):
+    here = pl.BlockSpec(memory_space=pltpu.VMEM)
+    dma = lambda n: pltpu.SemaphoreType.DMA((n,))
+    return pl.pallas_call(
+        tiny_kernel,
+        out_shape=jax.ShapeDtypeStruct((8, 128), f32),
+        in_specs=[here],
+        out_specs=here,
+        scratch_shapes=[pltpu.VMEM((7, 8, 128), f32), pltpu.VMEM((8, 128), f32), pltpu.VMEM((3, 8, 128), f32), dma(7), dma(7), dma(3), dma(3)],
+        compiler_params=pltpu.CompilerParams(collective_id=4, has_side_effects=True),
+    )(part)
+
+
 def masks(lengths, count):
     ends = jnp.cumsum(lengths, axis=1)
     places = jnp.arange(count, dtype=jnp.int32)
@@ -190,6 +770,15 @@
 def columns(weights, ways):
     rows, total = weights.shape
     return weights.reshape(rows, 2, total // (2 * ways * 128), ways, 128)
+
+
+def group_sum(part, rank, direct, which):
+    if not direct:
+        return lax.psum(part, TP)
+    count, rest = part.shape[0], part.shape[1] - rank
+    packed = jnp.concatenate([part[:, :rank], part[:, rank:].T.reshape(-1, rank)], axis=0)
+    packed = group_total(packed, which)
+    return jnp.concatenate([packed[:count], packed[count:].reshape(rest, count).T], axis=1)
 
 
 def on_device(tokens, lengths, gain, w_in, conv_w, conv_b, w_x, w_dt, dt_bias, skip, w_out, grad_out):
@@ -203,25 +792,38 @@
     rank = w_dt.shape[1]
     states = (w_x.shape[1] - rank) // 2
     cols = w_in.reshape(own_d, 2, groups, ways, own_e).transpose(3, 0, 1, 2, 4).reshape(ways, own_d, 2 * channels)
-    cols = lax.all_to_all(cols, TP, split_axis=0, concat_axis=0, tiled=True)
-    win = lax.all_gather(cols, "dp", axis=0, tiled=True).reshape(model, 2 * channels)
     small = jnp.concatenate([w_x, w_dt, conv_w, conv_b[:, None], dt_bias[:, None], skip[:, None]], axis=1)
     small_width = small.shape[1]
-    small = lax.all_gather(small, "dp", axis=0, tiled=True)
+    direct = groups == 4 and lax.axis_size("z") == 4
+    x = tokens[0].astype(f32)
+    scale = lax.rsqrt(jnp.mean(x * x, axis=1, keepdims=True) + EPS)
+    if direct:
+        padded = -small_width % 128
+        meta = jnp.zeros((16, 128), bf16).at[0, :own_d].set(gain).at[1, :5].set(lengths[0].astype(bf16))
+        xs, ups, win, wout, small, metas = front(tokens, grad_out, cols, w_out, jnp.pad(small, ((0, 0), (0, padded))), meta)
+        gains = metas[:, :, 0, :own_d].reshape(model).astype(f32)
+        lens = lax.dynamic_index_in_dim(metas, lax.axis_index("dp"), keepdims=False)[:, 1, :5].astype(jnp.int32)
+    else:
+        cols = lax.all_to_all(cols, TP, split_axis=0, concat_axis=0, tiled=True)
+        win = lax.all_gather(cols, "dp", axis=0, tiled=True)
+        small = lax.all_gather(small, "dp", axis=0, tiled=True)
+        wout = lax.all_gather(w_out, "dp", axis=0, tiled=True)
+        gains = lax.all_gather(gain, ALL, axis=0, tiled=True).astype(f32)
+        xs = lax.all_gather(tokens, TP, axis=0, tiled=True)
+        ups = lax.all_gather(grad_out, TP, axis=0, tiled=True)
+        lens = lax.all_gather(lengths, TP, axis=0, tiled=True)
+    rows = lens.shape[0]
+    tall = rows * length
+    win = win.reshape(model, 2 * channels)
+    wout = wout.reshape(channels, model)
+    small = small.reshape(channels, -1)
+    ups = ups.reshape(tall, model)
+    wide_x = xs.reshape(tall, model).astype(f32)
+    xns = (wide_x * lax.rsqrt(jnp.mean(wide_x * wide_x, axis=1, keepdims=True) + EPS) * gains).astype(bf16)
     wx = small[:, :rank + 2 * states]
     wdt = small[:, rank + 2 * states:2 * rank + 2 * states]
-    rest = small[:, 2 * rank + 2 * states:].astype(f32)
+    rest = small[:, 2 * rank + 2 * states:small_width].astype(f32)
     taps, bias, dtb, skips = rest[:, :4], rest[:, 4], rest[:, 5], rest[:, 6]
-    wout = lax.all_gather(w_out, "dp", axis=0, tiled=True)
-    gains = lax.all_gather(gain, ALL, axis=0, tiled=True).astype(f32)
-    x = tokens[0].astype(f32)
-    scale = lax.rsqrt(jnp.mean(x * x, axis=1, keepdims=True) + EPS)
-    xn = (x * scale * gains).astype(bf16)
-    xns = lax.all_gather(xn, TP, axis=0, tiled=True)
-    ups = lax.all_gather(grad_out[0], TP, axis=0, tiled=True)
-    lens = lax.all_gather(lengths, TP, axis=0, tiled=True)
-    rows = lens.shape[0]
-    tall = rows * length
 
     def time_major(a):
         return a.reshape(rows, length, -1).transpose(1, 0, 2).reshape(tall, -1)
@@ -242,7 +844,8 @@
     sig = jax.nn.sigmoid(c)
     v16 = (c * sig).astype(bf16).reshape(tall, channels)
     v = v16.astype(f32)
-    p = lax.psum(jnp.dot(v16, wx, preferred_element_type=f32), TP)
+    whole = group_sum(jnp.dot(v16, wx, preferred_element_type=f32), rank, direct, 1)
+    p = whole
     dl = p[:, :rank].astype(bf16)
     kq = p[:, rank:]
     dims_cols = (((1,), (1,)), ((), ()))
@@ -259,21 +862,15 @@
     m, dg, dpre, dv, dkq, stats = mixer(flags, kq3, sk, pre, v, g, dm, skips[None], states=states, width=256, unroll=4)
     stats = stats.transpose(1, 2, 0, 3).reshape(3, 8, channels)
     dskip = jnp.sum(stats[0], axis=0)
-    total = lax.psum(jnp.sum(stats[1]), ALL)
-    peak = lax.pmax(jnp.max(stats[2]), ALL)
-    beta_mean = total / float(groups * ways * length * inner)
     m16 = row_major(m).astype(bf16)
     out = jnp.dot(m16, wout, preferred_element_type=f32).astype(bf16)
-    out = lax.psum_scatter(out, TP, scatter_dimension=0, tiled=True)
-    block_out = (x + out.astype(f32)).astype(bf16)
     grad_wout = lax.dot_general(m16, ups, dims_rows, preferred_element_type=f32).astype(bf16)
-    grad_wout = lax.psum_scatter(grad_wout, "dp", scatter_dimension=0, tiled=True)
     dpre16 = dpre.astype(bf16)
     grad_dtb = jnp.sum(dpre16.astype(f32), axis=0)
     grad_wdt = lax.dot_general(dpre16, dl, dims_rows, preferred_element_type=f32)
     ddl = jnp.dot(dpre16, wdt, preferred_element_type=f32)
     dkq = dkq[:, :2 * states] + dkq[:, 2 * states:2 * states + 1] * jnp.pad(keys, ((0, 0), (0, states)))
-    dp16 = lax.psum(jnp.concatenate([ddl, dkq], axis=1), TP).astype(bf16)
+    dp16 = group_sum(jnp.concatenate([ddl, dkq], axis=1), rank, direct, 2).astype(bf16)
     grad_wx = lax.dot_general(v16, dp16, dims_rows, preferred_element_type=f32)
     dvt = dv + lax.dot_general(dp16, wx, dims_cols, preferred_element_type=f32)
     dc = (dvt * (sig.reshape(tall, channels) * (1.0 + c.reshape(tall, channels) * (1.0 - sig.reshape(tall, channels))))).reshape(length, rows, channels)
@@ -285,16 +882,38 @@
     grad_conv = jnp.stack(grad_taps[::-1] + [jnp.sum(dc, axis=(0, 1)), grad_dtb, dskip], axis=1)
     dz = row_major(jnp.concatenate([du.reshape(tall, channels), dg], axis=1)).astype(bf16)
     gwin = lax.dot_general(xns, dz, dims_rows, preferred_element_type=f32).astype(bf16)
-    gwin = lax.psum_scatter(gwin, "dp", scatter_dimension=0, tiled=True)
-    gwin = lax.all_to_all(gwin.reshape(ways, own_d, 2 * channels), TP, split_axis=0, concat_axis=0, tiled=True)
+    dxn = lax.dot_general(dz, win, dims_cols, preferred_element_type=f32).astype(bf16)
+    small_grad = jnp.concatenate([grad_wx, grad_wdt, grad_conv], axis=1)
+    if direct:
+        small_grad = jnp.pad(small_grad, ((0, 0), (0, padded)))
+        dxn, out, gwin, grad_wout, small_grad = back(
+            dxn.reshape(2, 4, length, model), out.reshape(2, 4, length, model), gwin.reshape(groups, ways * own_d, 2 * channels),
+            grad_wout.reshape(groups, own_e, model), small_grad.reshape(groups, own_e, -1))
+    else:
+        out = lax.psum_scatter(out, TP, scatter_dimension=0, tiled=True).astype(f32)
+        grad_wout = lax.psum_scatter(grad_wout, "dp", scatter_dimension=0, tiled=True).astype(f32)
+        gwin = lax.psum_scatter(gwin, "dp", scatter_dimension=0, tiled=True)
+        gwin = lax.all_to_all(gwin.reshape(ways, own_d, 2 * channels), TP, split_axis=0, concat_axis=0, tiled=True)
+        dxn = lax.psum_scatter(dxn, TP, scatter_dimension=0, tiled=True).astype(f32)
+        small_grad = lax.psum_scatter(small_grad, "dp", scatter_dimension=0, tiled=True)
+    block_out = (x + out).astype(bf16)
     grad_win = gwin.reshape(ways, own_d, 2, groups, own_e).transpose(1, 2, 3, 0, 4).reshape(own_d, 2 * inner).astype(f32)
-    dxn = lax.dot_general(dz, win, dims_cols, preferred_element_type=f32).astype(bf16)
-    dxn = lax.psum_scatter(dxn, TP, scatter_dimension=0, tiled=True).astype(f32)
-    small_grad = lax.psum_scatter(jnp.concatenate([grad_wx, grad_wdt, grad_conv], axis=1), "dp", scatter_dimension=0, tiled=True)
     inner_grad = dxn * gains
     dxx = scale * inner_grad - x * (scale * scale * scale) * (jnp.sum(inner_grad * x, axis=1, keepdims=True) / model)
     grad_tokens = (grad_out[0].astype(f32) + dxx).astype(bf16)
-    grad_gain = lax.psum_scatter(jnp.sum(dxn * x * scale, axis=0), ALL, scatter_dimension=0, tiled=True)
+    grad_gain = jnp.sum(dxn * x * scale, axis=0)
+    seen, peak = jnp.sum(stats[1]), jnp.max(stats[2])
+    if direct:
+        part = grad_gain.reshape(groups, ways, own_d).transpose(1, 0, 2)
+        part = jnp.pad(part, ((0, 0), (0, 8 - groups), (0, 128 - own_d)))
+        part = part.at[:, 4, 0].set(seen).at[:, 4, 1].set(peak)
+        part = tiny(part)
+        grad_gain = lax.dynamic_index_in_dim(part, lax.axis_index("dp"), keepdims=False)[:own_d]
+        seen, peak = part[4, 0], part[4, 1]
+    else:
+        grad_gain = lax.psum_scatter(grad_gain, ALL, scatter_dimension=0, tiled=True)
+        seen, peak = lax.psum(seen, ALL), lax.pmax(peak, ALL)
+    beta_mean = seen / float(groups * ways * length * inner)
     at = rank + 2 * states
     return (
         block_out[None],
@@ -307,7 +926,7 @@
         small_grad[:, at:at + rank],
         small_grad[:, at + rank + 5],
         small_grad[:, at + rank + 6],
-        grad_wout.astype(f32),
+        grad_wout,
         beta_mean,
         peak,
     )

time: 788 us -> 474 us (0.60)
  waiting for transfers between devices: 320 us -> 0 us
  Pallas kernels: 58.3 us -> 323 us
  blocking collectives: 254 us -> 0 us
  local copies, waits for them, and re-layouts: 41.7 us -> 60.2 us
  between operations: 16.6 us -> 3.53 us
    pallas_call x0 -> x5, Pallas kernels: none -> 265 us  [the longest x1 112 us: back(): pl.pallas_call(back_kernel, out_shape=(like((rows, columns), f32), like((...]
    reduce_scatter x5 -> x0, waiting for transfers between devices: 167 us -> none  [the longest x1 86.8 us: on_device(): dxn = lax.psum_scatter(dxn, TP, scatter_dimension=0, tiled=True).astype(f32)]
    all_gather x4 -> x0, waiting for transfers between devices: 100 us -> none  [the longest x1 47.1 us: on_device(): ups = lax.all_gather(grad_out[0], TP, axis=0, tiled=True)]
    unnamed x2 -> x0, blocking collectives: 86.2 us -> none
    all_to_all x1 -> x0, blocking collectives: 52.2 us -> none  [on_device(): cols = lax.all_to_all(cols, TP, split_axis=0, concat_axis=0, tiled=True)]
    psum x1 -> x0, waiting for transfers between devices: 51.4 us -> none  [on_device(): p = lax.psum(jnp.dot(v16, wx, preferred_element_type=f32), TP)]
    pmax x1 -> x0, blocking collectives: 44.1 us -> none  [on_device(): peak = lax.pmax(jnp.max(stats[2]), ALL)]
    psum x1 -> x0, blocking collectives: 43.6 us -> none  [on_device(): dp16 = lax.psum(jnp.concatenate([ddl, dkq], axis=1), TP).astype(bf16)]
  transfers between devices with their start and end apart: 11 -> 0, of which waited for: 8 -> 0; matrix products, arithmetic and copies ran while one was open for 9% -> 0% of each run, Pallas kernels for 0% -> 0%
where the time goes in v2:
time: 474 us; the launch traced here: 467 us
  Pallas kernels  323 us (68%)
  local copies, waits for them, and re-layouts  60.2 us (13%)
  matrix products  47.6 us (10%)
  other arithmetic  32.5 us (7%)
    pallas_call x1, Pallas kernels, back(): pl.pallas_call(back_kernel, out_shape=(like((rows, columns), f32), like((...  112 us
    pallas_call x1, Pallas kernels, front(): pl.pallas_call(front_kernel, out_shape=(like((ways, length, model), bf16)...  96.5 us
    pallas_call x1, Pallas kernels, mixer(): pl.pallas_call(functools.partial(mixer_kernel, states, unroll, min(256, r...  58.3 us
    pallas_call x2, Pallas kernels, group_total(): pl.pallas_call(total_kernel, out_shape=jax.ShapeDtypeStruct(part.shape, f...  45.2 us
    unnamed x117, local copies, waits for them, and re-layouts  25 us
    pallas_call x1, Pallas kernels, tiny(): pl.pallas_call(tiny_kernel, out_shape=jax.ShapeDtypeStruct((8, 128), f32)...  11.2 us
    reduce_sum x1, other arithmetic, on_device(): grad_taps.append(jnp.sum(dc * shifted[offset - 1], axis=(0, 1)))  11.2 us

profile of v2, /device:TPU:8, one launch (start us, length us, event | category | flops | bytes accessed | tf_op | source)
XLA Modules:
  0.0 466.9 jit_solution(609889558711057879)
XLA Ops:
  6.6 96.5 %shard_map.219 = (bf16[8,128,2048]{2,1,0:T(8,128)(2,1)S(1)}, bf16[8,128,2048]{2,1,0:T(8,128)(2,1)S(1)}, bf16[4,8,64,1024]{3,2,1,0:T(8,128)(2,1)S(1)}, bf16[4,128...) custom-call(bf16[1,128,2048]{2,1,0:T(8,128)(2,1)S(1)} %copy-done, ...), custom_call_target="tpu_custom_call" | custom-call | tf_op jit(solution)/shard_map/pallas_call | solution.py:382
  110.4 3.2 fusion
  113.9 6.4 %fusion.6 = f32[128,8,1024]{2,0,1:T(8,128)S(1)} fusion(bf16[2048,1024,1]{1,0,2:T(8,128)(2,1)} %bitcast.145, bf16[8,128,2048]{2,1,0:T(8,128)(2,1)S(1)} %copy-done.2, f32[2048]{0:T(1024)S(1)} %reshape.367, f32[8,128]{1,0:T(8,128)S(1)} %add_rsqrt_fusion), kind=kOutput, calls=%fused_computation.14 | convolution fusion | flops 4303355904 | bytes 12595200 | tf_op jit(solution)/shard_map/dot_general | solution.py:835
  120.3 2.4 copy.257
  125.3 2.5 copy.195
  128.5 7.0 %add_divide_fusion = (f32[128,8,512]{2,0,1:T(8,128)}, f32[128,8,512]{2,0,1:T(8,128)S(1)}) fusion(f32[128,8]{0,1:T(8,128)S(1)} %get-tuple-element.195, f32[128,8,512]{2,0,1:T(8,128)} %copy.195, f32[512]{0:T(512)S(1)} %bitcast.178, f32[128,8]{0,1:T(8,128)S(1)} %get-tuple-element.192, f32[512]{0:T(512)S(1)} %bitcast.176, f32[128,8]{0,1:T(8,128)S(1)} %get-tuple-element.194, ...), kind=kLoop, calls=%fused_computation.42 | loop fusion | flops 7340032 | bytes 6313984 | tf_op jit(solution)/shard_map/div | solution.py:844
  138.4 23.4 %shard_map.220 = f32[1280,128]{1,0:T(8,128)S(1)} custom-call(f32[1280,128]{1,0:T(8,128)S(1)} %pad_maximum_fusion.1.part_ref), custom_call_target="tpu_custom_call" | custom-call | tf_op jit(solution)/shard_map/pallas_call | solution.py:501
  169.6 5.2 %convolution_bitcast_fusion = f32[128,8,512]{2,0,1:T(8,128)S(1)} fusion(bf16[8,128,2048]{2,1,0:T(8,128)(2,1)} %copy-done.6, bf16[512,2048,1]{1,0,2:T(8,128)(2,1)} %bitcast.147), kind=kOutput, calls=%fused_computation.45 | convolution fusion | flops 2147483648 | bytes 8388608 | tf_op jit(solution)/shard_map/dot_general | solution.py:854
  174.9 2.5 copy.259
  178.0 58.3 %shard_map.221 = (f32[1024,512]{1,0:T(8,128)}, f32[1024,512]{1,0:T(8,128)}, f32[1024,512]{1,0:T(8,128)}, f32[1024,512]{1,0:T(8,128)}, f32[1024,128]{1,0:T(8,128)}, /*index=5*/f32[2,3,8,256]{3,2,1,0:T(8,128)}) custom-call(f32[1024,128]{1,0:T(8,128)} %pad.72.flags_ref, bf16[1024,96]{1,0:T(8,128)(2,1)} %pad_maximum_fusion.6.kq3_ref, ...), custom_call_target="tpu_custom_call" | custom-call | tf_op jit(solution)/shard_map/pallas_call | solution.py:167
  236.3 2.8 fusion.41
  241.0 21.8 %shard_map.222 = f32[1280,128]{1,0:T(8,128)S(1)} custom-call(f32[1280,128]{1,0:T(8,128)S(1)} %pad_maximum_fusion.2.part_ref), custom_call_target="tpu_custom_call" | custom-call | tf_op jit(solution)/shard_map/pallas_call | solution.py:501
  268.4 2.8 fusion.26
  271.2 6.2 %fusion.52 = (f32[512]{0:T(512)}, f32[512]{0:T(512)}, f32[1024,512]{1,0:T(8,128)S(1)}) fusion(f32[1024,1024]{1,0:T(8,128)} %bitcast.150, f32[128,8,512]{2,0,1:T(8,128)S(1)} %copy-done.14, f32[128,8,512]{2,0,1:T(8,128)} %get-tuple-element.173, f32[1024,512]{1,0:T(8,128)} %get-tuple-element.84, bf16[512,384]{1,0:T(8,128)(2,1)S(1)} %bitcast.144, ...), kind=kOutput, calls=%fused_computation.124 | convolution fusion | flops 173145088 | bytes 11276288 | tf_op jit(solution)/shard_map/dot_general | solution.py:875
  281.5 11.2 %multiply_reduce_fusion.1 = (f32[512]{0:T(512)S(1)}, f32[512]{0:T(512)S(1)}, f32[512]{0:T(512)S(1)}, bf16[128,8,512]{2,0,1:T(8,128)(2,1)S(1)}) fusion(f32[128,8,512]{2,0,1:T(8,128)S(1)} %copy-done.15, f32[128,8]{0,1:T(8,128)S(1)} %get-tuple-element.194, f32[128,8,512]{2,1,0:T(8,128)S(1)} %bitcast.152, f32[128,8]{0,1:T(8,128)S(1)} %copy-done.30, ...), kind=kLoop, calls=%fused_computation.37 | loop fusion | flops 8911360 | bytes 11462656 | tf_op jit(solution)/shard_map/reduce_sum | solution.py:880
  295.1 2.7 convert_bitcast_fusion.1
  298.6 6.6 %bitcast_convert_fusion = bf16[2048,1024]{1,0:T(8,128)(2,1)} fusion(bf16[8,128,2048]{2,1,0:T(8,128)(2,1)S(1)} %copy-done.3, f32[2048]{0:T(1024)S(1)} %reshape.367, f32[8,128]{1,0:T(8,128)S(1)} %copy-done.45, bf16[128,8,512]{2,0,1:T(8,128)(2,1)S(1)} %copy.211, bf16[128,8,512]{2,0,1:T(8,128)(2,1)S(1)} %get-tuple-element.177), kind=kOutput, calls=%fused_computation.5 | convolution fusion | flops 4309647360 | bytes 10498048 | tf_op jit(solution)/shard_map/dot_general | solution.py:884
  306.8 4.3 convolution_convert_fusion
  313.3 6.1 %convolution_convert_fusion.1 = bf16[1024,2048]{1,0:T(8,128)(2,1)} fusion(bf16[1024,1024]{1,0:T(8,128)(2,1)S(1)} %bitcast.164, bf16[2048,1024]{1,0:T(8,128)(2,1)S(1)} %bitcast.146), kind=kOutput, calls=%fused_computation.9 | convolution fusion | flops 4297064448 | bytes 10485760 | tf_op jit(solution)/shard_map/dot_general | solution.py:885
  319.4 4.0 bitcast_convert_fusion.1
  323.4 111.9 %shard_map.223 = (f32[128,2048]{1,0:T(8,128)}, f32[128,2048]{1,0:T(8,128)}, bf16[8,64,1024]{2,1,0:T(8,128)(2,1)}, f32[128,2048]{1,0:T(8,128)}, f32[128,384]{1,0:T(8,128)}) custom-call(bf16[2,4,128,2048]{3,2,1,0:T(8,128)(2,1)} %bitcast.161, bf16[2,4,128,2048]{3,2,1,0:T(8,128)(2,1)} %bitcast.160, bf16[4,512,1024]{2,1,0:T(8,128)(2,1)} %bitcast.159, ...), custom_call_target="tpu_custom_call" | custom-call | tf_op jit(solution)/shard_map/pallas_call | solution.py:695
  438.6 2.5 copy.258
  444.4 11.2 %shard_map.224 = f32[8,128]{1,0:T(8,128)} custom-call(f32[8,8,128]{2,1,0:T(8,128)} %copy-done.28), custom_call_target="tpu_custom_call" | custom-call | tf_op jit(solution)/shard_map/pallas_call | solution.py:749
  463.2 2.3 copy.266
  (208 shorter events, 59.5 us)
Async XLA Ops:
  2.2 3.4 copy-start.46
  2.2 3.6 copy-start.47
  2.2 3.7 copy-start.48
  2.2 3.8 copy-start.49
  2.2 3.9 copy-start.33
  2.2 4.1 copy-start.51
  2.2 4.1 copy-start.52
  2.2 4.3 copy-start
  2.3 4.3 copy-start.4
  2.3 4.3 copy-start.5
  110.4 3.5 copy-start.2
  113.7 6.6 %copy-start.44 = (f32[8,128]{1,0:T(8,128)}, f32[8,128]{1,0:T(8,128)S(1)}, u32[]{:S(2)}) copy-start(f32[8,128]{1,0:T(8,128)S(1)} %add_rsqrt_fusion) | copy-start | bytes 12292
  128.2 7.3 %copy-start.29 = (f32[128,8]{0,1:T(8,128)}, f32[128,8]{0,1:T(8,128)S(1)}, u32[]{:S(2)}) copy-start(f32[128,8]{0,1:T(8,128)S(1)} %get-tuple-element.195) | copy-start | bytes 12292
  128.5 7.0 %copy-start.34 = (f32[512,1]{0,1:T(1,128)}, f32[512,1]{0,1:T(1,128)S(1)}, u32[]{:S(2)}) copy-start(f32[512,1]{0,1:T(1,128)S(1)} %get-tuple-element.185) | copy-start | bytes 6148
  128.5 7.0 %copy-start.36 = (f32[512,1]{0,1:T(1,128)}, f32[512,1]{0,1:T(1,128)S(1)}, u32[]{:S(2)}) copy-start(f32[512,1]{0,1:T(1,128)S(1)} %get-tuple-element.187) | copy-start | bytes 6148
  128.5 7.0 %copy-start.38 = (f32[512,1]{0,1:T(1,128)}, f32[512,1]{0,1:T(1,128)S(1)}, u32[]{:S(2)}) copy-start(f32[512,1]{0,1:T(1,128)S(1)} %get-tuple-element.188) | copy-start | bytes 6148
  128.5 7.0 %copy-start.40 = (f32[512,1]{0,1:T(1,128)}, f32[512,1]{0,1:T(1,128)S(1)}, u32[]{:S(2)}) copy-start(f32[512,1]{0,1:T(1,128)S(1)} %get-tuple-element.189) | copy-start | bytes 6148
  263.5 7.7 %copy-start.14 = (f32[128,8,512]{2,0,1:T(8,128)S(1)}, f32[128,8,512]{2,0,1:T(8,128)}, u32[]{:S(2)}) copy-start(f32[128,8,512]{2,0,1:T(8,128)} %copy-done.13) | copy-start | bytes 6291460
  267.4 3.8 copy-start.25
  281.5 11.2 %copy-start.31 = (f32[2,3,8,256]{3,2,1,0:T(8,128)S(1)}, f32[2,3,8,256]{3,2,1,0:T(8,128)}, u32[]{:S(2)}) copy-start(f32[2,3,8,256]{3,2,1,0:T(8,128)} %get-tuple-element.89) | copy-start | bytes 147460
  281.5 11.9 %copy-start.17 = (f32[1024,512]{1,0:T(8,128)S(1)}, f32[1024,512]{1,0:T(8,128)}, u32[]{:S(2)}) copy-start(f32[1024,512]{1,0:T(8,128)} %get-tuple-element.85) | copy-start | bytes 6291460
  295.1 3.4 copy-start.3
  313.3 6.1 %copy-start.7 = (bf16[8,128,2048]{2,1,0:T(8,128)(2,1)S(1)}, bf16[8,128,2048]{2,1,0:T(8,128)(2,1)}, u32[]{:S(2)}) copy-start(bf16[8,128,2048]{2,1,0:T(8,128)(2,1)} %copy-done.6) | copy-start | bytes 12582916
  441.1 17.7 %copy-start.24 = (f32[128,2048]{1,0:T(8,128)S(1)}, f32[128,2048]{1,0:T(8,128)}, u32[]{:S(2)}) copy-start(f32[128,2048]{1,0:T(8,128)} %get-tuple-element.90) | copy-start | bytes 3145732
  (29 other events, 47.1 us)

commit v3 on v2

--- a/solution.py
+++ b/solution.py
@@ -223,179 +223,6 @@
     return device[1] * 4 + device[2]
 
 
-def front_kernel(tok_ref, up_ref, cols_ref, wout_ref, small_ref, meta_ref,
-                 xs_ref, ups_ref, win_ref, wouts_ref, smalls_ref, metas_ref,
-                 own_sem, ms, mr, qs, qr, xls, xlr, xrs, xrr, xcs, xcr, as_, ar, ps, pr, rs, rr, ws, wr):
-    d, c, z = place()
-    j = c * 4 + z
-    me = (d, c, z)
-    dx, dy, dd = flip(d, 1), flip(d, 2), flip(flip(d, 1), 2)
-    xn, yn, dn = (dx, c, z), (dy, c, z), (dd, c, z)
-    sib = (d, flip(c, 1), z)
-    left = (d, c, lax.rem(z + 3, 4))
-    right = (d, c, lax.rem(z + 1, 4))
-    steps = mates()
-    greet([mate(s) for s in steps] + [xn, yn, dn])
-    half = cols_ref.shape[1]
-    own = [
-        pltpu.make_async_copy(tok_ref.at[0], xs_ref.at[j], own_sem.at[0]),
-        pltpu.make_async_copy(up_ref.at[0], ups_ref.at[j], own_sem.at[1]),
-        pltpu.make_async_copy(cols_ref.at[j], win_ref.at[d, j], own_sem.at[2]),
-        pltpu.make_async_copy(wout_ref, wouts_ref.at[d], own_sem.at[3]),
-        pltpu.make_async_copy(small_ref, smalls_ref.at[d], own_sem.at[4]),
-        pltpu.make_async_copy(meta_ref, metas_ref.at[d, j], own_sem.at[5]),
-    ]
-    for copy in own:
-        copy.start()
-    pending = []
-    for i, s in enumerate(steps):
-        to = mate(s)
-        pending.append(put(meta_ref, metas_ref.at[d, j], ms.at[i], mr.at[i], to))
-    for i, to in enumerate((xn, yn, dn)):
-        pending.append(put(small_ref, smalls_ref.at[d], ps.at[16 + i], pr.at[16 + i], to))
-    for i, s in enumerate(steps):
-        to = mate(s)
-        pending.append(put(cols_ref.at[rank_of(to)], win_ref.at[d, j], as_.at[i], ar.at[i], to))
-    own[2].wait()
-    pending.append(put(win_ref.at[d, j], win_ref.at[d, j], ps.at[7], pr.at[7], xn))
-    pending.append(put(win_ref.at[d, j], win_ref.at[d, j], ps.at[15], pr.at[15], yn))
-
-    def row_start(ref, out, base):
-        pending.append(put(ref.at[0], out.at[j], xcs.at[base + z], xcr.at[base + z], sib))
-
-        @pl.when(z < 3)
-        def _():
-            put(ref.at[0], out.at[j], xls.at[base], xlr.at[base], right)
-
-        @pl.when(z > 0)
-        def _():
-            put(ref.at[0], out.at[j], xrs.at[base], xrr.at[base], left)
-
-    def row_hop(out, base, i):
-        @pl.when(z > i)
-        def _():
-            at = z - 1 - i
-            slot = out.at[c * 4 + at]
-            landed(slot, xlr.at[base + i], left)
-            if i < 2:
-                @pl.when(z < 3)
-                def _():
-                    put(slot, slot, xls.at[base + i + 1], xlr.at[base + i + 1], right)
-            put(slot, slot, xcs.at[base + at], xcr.at[base + at], sib)
-
-        @pl.when(z < 3 - i)
-        def _():
-            at = z + 1 + i
-            slot = out.at[c * 4 + at]
-            landed(slot, xrr.at[base + i], right)
-            if i < 2:
-                @pl.when(z > 0)
-                def _():
-                    put(slot, slot, xrs.at[base + i + 1], xrr.at[base + i + 1], left)
-            put(slot, slot, xcs.at[base + at], xcr.at[base + at], sib)
-
-    def row_end(out, base):
-        for i in range(3):
-            @pl.when((z < 3) & (z >= i))
-            def _():
-                sent(out.at[j], xls.at[base + i], right)
-
-            @pl.when((z > 0) & (z <= 3 - i))
-            def _():
-                sent(out.at[j], xrs.at[base + i], left)
-        for at in range(4):
-            landed(out.at[flip(c, 1) * 4 + at], xcr.at[base + at], sib)
-
-            @pl.when(z != at)
-            def _():
-                sent(out.at[j], xcs.at[base + at], sib)
-
-    row_start(tok_ref, xs_ref, 0)
-    own[5].wait()
-    for i, s in enumerate(steps):
-        landed(metas_ref.at[d, rank_of(mate(s, -1))], mr.at[i], xn)
-    for i, to in enumerate((xn, yn, dn)):
-        pending.append(put(metas_ref.at[d], metas_ref.at[d], qs.at[i], qr.at[i], to))
-    for i, s in enumerate(steps):
-        src = mate(s, -1)
-        slot = win_ref.at[d, rank_of(src)]
-        landed(slot, ar.at[i], src)
-        pending.append(put(slot, slot, ps.at[i], pr.at[i], xn))
-        pending.append(put(slot, slot, ps.at[8 + i], pr.at[8 + i], yn))
-    row_hop(xs_ref, 0, 0)
-    row_start(up_ref, ups_ref, 4)
-    halves = wout_ref.shape[0] // 2
-    pending.append(put(wout_ref, wouts_ref.at[d], ws.at[0], wr.at[0], xn))
-    pending.append(put(wout_ref, wouts_ref.at[d], ws.at[1], wr.at[1], yn))
-    order = [7] + list(range(7))
-    slots = {7: j}
-    for i, s in enumerate(steps):
-        slots[i] = rank_of(mate(s, -1))
-    for k, i in enumerate(order):
-        slot = win_ref.at[dx, slots[i]]
-        landed(slot, pr.at[i], xn)
-        if k % 2 == 0:
-            pending.append(put(slot, slot, rs.at[k // 2], rr.at[k // 2], yn))
-        slot = win_ref.at[dy, slots[i]]
-        landed(slot, pr.at[8 + i], yn)
-        if k % 2 == 1:
-            pending.append(put(slot, slot, rs.at[4 + k // 2], rr.at[4 + k // 2], xn))
-        if k == 3:
-            row_hop(xs_ref, 0, 1)
-            row_hop(ups_ref, 4, 0)
-    row_hop(xs_ref, 0, 2)
-    row_hop(ups_ref, 4, 1)
-    slot = wouts_ref.at[dx]
-    landed(slot, wr.at[0], xn)
-    slot = wouts_ref.at[dx, pl.ds(0, halves)]
-    pending.append(put(slot, slot, ws.at[2], wr.at[2], yn))
-    slot = wouts_ref.at[dy]
-    landed(slot, wr.at[1], yn)
-    slot = wouts_ref.at[dy, pl.ds(halves, halves)]
-    pending.append(put(slot, slot, ws.at[3], wr.at[3], xn))
-    row_hop(ups_ref, 4, 2)
-    for k, i in enumerate(order):
-        slot = win_ref.at[dd, slots[i]]
-        if k % 2 == 0:
-            landed(slot, rr.at[k // 2], yn)
-        else:
-            landed(slot, rr.at[4 + k // 2], xn)
-    landed(wouts_ref.at[dd, pl.ds(0, halves)], wr.at[2], yn)
-    landed(wouts_ref.at[dd, pl.ds(halves, halves)], wr.at[3], xn)
-    for i, (to, at) in enumerate(((xn, dx), (yn, dy), (dn, dd))):
-        landed(smalls_ref.at[at], pr.at[16 + i], to)
-        landed(metas_ref.at[at], qr.at[i], to)
-    row_end(xs_ref, 0)
-    row_end(ups_ref, 4)
-    for copy in own[:2] + own[3:5]:
-        copy.wait()
-    for copy in pending:
-        copy.wait_send()
-
-
-def front(tokens, upstream, cols, w_out, small, meta):
-    groups, ways = lax.axis_size("dp"), cols.shape[0]
-    like = jax.ShapeDtypeStruct
-    length, model = tokens.shape[1:]
-    dma = lambda n: pltpu.SemaphoreType.DMA((n,))
-    some = pl.BlockSpec(memory_space=pl.ANY)
-    return pl.pallas_call(
-        front_kernel,
-        out_shape=(
-            like((ways, length, model), bf16),
-            like((ways, length, model), bf16),
-            like((groups,) + cols.shape, bf16),
-            like((groups,) + w_out.shape, bf16),
-            like((groups,) + small.shape, bf16),
-            like((groups, ways) + meta.shape, bf16),
-        ),
-        in_specs=[some] * 6,
-        out_specs=(some,) * 6,
-        scratch_shapes=[dma(6), dma(7), dma(7), dma(3), dma(3), dma(8), dma(8), dma(8), dma(8), dma(8), dma(8), dma(7), dma(7), dma(19), dma(19), dma(8), dma(8), dma(4), dma(4)],
-        compiler_params=pltpu.CompilerParams(collective_id=0, has_side_effects=True, vmem_limit_bytes=16 * 1024 * 1024),
-    )(tokens, upstream, cols, w_out, small, meta)
-
-
 PIECES = 4
 
 
@@ -506,6 +333,690 @@
         scratch_shapes=[pltpu.VMEM((rows, 128), f32)] * 6 + [dma() for _ in range(8)],
         compiler_params=pltpu.CompilerParams(collective_id=which, has_side_effects=True, vmem_limit_bytes=16 * 1024 * 1024),
     )(part)
+
+
+def k1_kernel(tok_ref, up_ref, cols_ref, wout_ref, small_ref, meta_ref,
+              xn_out, ups_ref, win_out, wouts_ref, smalls_ref, vecs_ref, gains_ref, masks_ref,
+              u_ref, g_ref, v_ref, slope_ref, dl_ref, kq_ref,
+              xs_ref, xn_ref, win_ref, metas_ref, part_ref, out_ref, sib_ref, base_ref, left_ref, right_ref, tor_ref, tol_ref,
+              own_sem, ms, mr, qs, qr, xls, xlr, xrs, xrr, xcs, xcr, as_, ar, ps, pr, rs, rr, ws, wr, ts, tr, tls, tlr, trs, trr, tos, tor):
+    d, c, z = place()
+    j = c * 4 + z
+    dx, dy, dd = flip(d, 1), flip(d, 2), flip(flip(d, 1), 2)
+    xn, yn, dn = (dx, c, z), (dy, c, z), (dd, c, z)
+    sib = (d, flip(c, 1), z)
+    left = (d, c, lax.rem(z + 3, 4))
+    right = (d, c, lax.rem(z + 1, 4))
+    steps = mates()
+    greet([mate(s) for s in steps] + [xn, yn, dn])
+    length = tok_ref.shape[1]
+    model = tok_ref.shape[2]
+    depth = cols_ref.shape[1]
+    tiles = u_ref.shape[0]
+    width = tiles * 128
+    count = g_ref.shape[1]
+
+    def rows(rank):
+        return pl.ds(pl.multiple_of(rank * length, length), length)
+
+    def block(group, rank):
+        return pl.ds(pl.multiple_of((group * 8 + rank) * depth, depth), depth)
+
+    own_e = wout_ref.shape[0]
+
+    def part_e(group, start=0, size=own_e):
+        return pl.ds(pl.multiple_of(group * own_e + start, 16), size)
+
+    own = [
+        pltpu.make_async_copy(tok_ref.at[0], xs_ref.at[rows(j)], own_sem.at[0]),
+        pltpu.make_async_copy(up_ref.at[0], ups_ref.at[rows(j)], own_sem.at[1]),
+        pltpu.make_async_copy(cols_ref.at[j], win_ref.at[block(d, j)], own_sem.at[2]),
+        pltpu.make_async_copy(wout_ref, wouts_ref.at[part_e(d)], own_sem.at[3]),
+        pltpu.make_async_copy(small_ref, smalls_ref.at[part_e(d)], own_sem.at[4]),
+        pltpu.make_async_copy(meta_ref, metas_ref.at[d, j], own_sem.at[5]),
+    ]
+    for copy in own:
+        copy.start()
+    pending = []
+    for i, s in enumerate(steps):
+        to = mate(s)
+        pending.append(put(meta_ref, metas_ref.at[d, j], ms.at[i], mr.at[i], to))
+    for i, s in enumerate(steps):
+        to = mate(s)
+        pending.append(put(cols_ref.at[rank_of(to)], win_ref.at[block(d, j)], as_.at[i], ar.at[i], to))
+    for i, to in enumerate((xn, yn, dn)):
+        pending.append(put(small_ref, smalls_ref.at[part_e(d)], ps.at[16 + i], pr.at[16 + i], to))
+    own[2].wait()
+    slot = win_ref.at[block(d, j)]
+    pending.append(put(slot, slot, ps.at[7], pr.at[7], xn))
+    pending.append(put(slot, slot, ps.at[15], pr.at[15], yn))
+
+    def row_start(ref, out, base):
+        pending.append(put(ref.at[0], out.at[rows(j)], xcs.at[base + z], xcr.at[base + z], sib))
+
+        @pl.when(z < 3)
+        def _():
+            put(ref.at[0], out.at[rows(j)], xls.at[base], xlr.at[base], right)
+
+        @pl.when(z > 0)
+        def _():
+            put(ref.at[0], out.at[rows(j)], xrs.at[base], xrr.at[base], left)
+
+    def row_hop(out, base, i, then=None):
+        @pl.when(z > i)
+        def _():
+            at = z - 1 - i
+            slot = out.at[rows(c * 4 + at)]
+            landed(slot, xlr.at[base + i], left)
+            if i < 2:
+                @pl.when(z < 3)
+                def _():
+                    put(slot, slot, xls.at[base + i + 1], xlr.at[base + i + 1], right)
+            put(slot, slot, xcs.at[base + at], xcr.at[base + at], sib)
+            if then is not None:
+                then(c * 4 + at)
+
+        @pl.when(z < 3 - i)
+        def _():
+            at = z + 1 + i
+            slot = out.at[rows(c * 4 + at)]
+            landed(slot, xrr.at[base + i], right)
+            if i < 2:
+                @pl.when(z > 0)
+                def _():
+                    put(slot, slot, xrs.at[base + i + 1], xrr.at[base + i + 1], left)
+            put(slot, slot, xcs.at[base + at], xcr.at[base + at], sib)
+            if then is not None:
+                then(c * 4 + at)
+
+    def row_end(out, base):
+        for i in range(3):
+            @pl.when((z < 3) & (z >= i))
+            def _():
+                sent(out.at[rows(j)], xls.at[base + i], right)
+
+            @pl.when((z > 0) & (z <= 3 - i))
+            def _():
+                sent(out.at[rows(j)], xrs.at[base + i], left)
+        for at in range(4):
+            @pl.when(z != at)
+            def _():
+                sent(out.at[rows(j)], xcs.at[base + at], sib)
+
+    row_start(tok_ref, xs_ref, 0)
+    own[5].wait()
+    for i, s in enumerate(steps):
+        landed(metas_ref.at[d, rank_of(mate(s, -1))], mr.at[i], xn)
+    for i, to in enumerate((xn, yn, dn)):
+        pending.append(put(metas_ref.at[d], metas_ref.at[d], qs.at[i], qr.at[i], to))
+    slots = {7: j}
+    for i, s in enumerate(steps):
+        slots[i] = rank_of(mate(s, -1))
+    order = [7] + list(range(7))
+
+    def pass_on(i):
+        src = mate(steps[i], -1)
+        slot = win_ref.at[block(d, slots[i])]
+        landed(slot, ar.at[i], src)
+        pending.append(put(slot, slot, ps.at[i], pr.at[i], xn))
+        pending.append(put(slot, slot, ps.at[8 + i], pr.at[8 + i], yn))
+
+    def relay(k):
+        i = order[k]
+        slot = win_ref.at[block(dx, slots[i])]
+        landed(slot, pr.at[i], xn)
+        if k % 2 == 0:
+            pending.append(put(slot, slot, rs.at[k // 2], rr.at[k // 2], yn))
+        slot = win_ref.at[block(dy, slots[i])]
+        landed(slot, pr.at[8 + i], yn)
+        if k % 2 == 1:
+            pending.append(put(slot, slot, rs.at[4 + k // 2], rr.at[4 + k // 2], xn))
+
+    pass_on(0)
+    for i, (to, at) in enumerate(((xn, dx), (yn, dy), (dn, dd))):
+        landed(metas_ref.at[at], qr.at[i], to)
+    lens = jnp.concatenate([metas_ref[d, r, 1:2, :] for r in range(8)], axis=0)
+    ends = []
+    last = jnp.zeros((8, 1), f32)
+    for i in range(5):
+        last = last + lens[:, i:i + 1]
+        ends.append(jnp.broadcast_to(last, (8, 128)))
+
+    def mask_step(t, carry):
+        here = t.astype(f32)
+
+        def segment(at):
+            total = jnp.zeros((8, 128), f32)
+            for end in ends:
+                total = total + jnp.where(end <= at, 1.0, 0.0)
+            return total
+
+        now = segment(here)
+        r = pl.ds(pl.multiple_of(t * 8, 8), 8)
+        for o in range(1, 4):
+            same = jnp.where(segment(here - o) == now, 1.0, 0.0)
+            masks_ref[o - 1, r, :] = jnp.where(here >= o, same, 0.0)
+        masks_ref[3, r, :] = jnp.where(now < DOCS, 1.0, 0.0)
+        return carry
+
+    lax.fori_loop(0, length, mask_step, 0)
+    lane = lax.broadcasted_iota(jnp.int32, (1, 128), 1)
+    for group in range(4):
+        for pair in range(4):
+            at = group * 512 + pair * 128
+            gains_ref[:, at:at + 128] = jnp.where(lane < depth, metas_ref[group, 2 * pair, 0:1, :], metas_ref[group, 2 * pair + 1, 0:1, :])
+        vecs_ref[:, group * own_e:(group + 1) * own_e] = metas_ref[group, j, 8:16, :]
+
+    def normalize(rank):
+        def body(i, carry):
+            r = pl.ds(pl.multiple_of(rank * length + i * 16, 16), 16)
+            x = xs_ref[r, :].astype(f32)
+            scale = lax.rsqrt(jnp.sum(x * x, axis=1, keepdims=True) * (1.0 / model) + EPS)
+            xn_ref[r, :] = (x * scale * gains_ref[...]).astype(bf16)
+            return carry
+
+        lax.fori_loop(0, length // 16, body, 0)
+
+    for i in range(1, 7):
+        pass_on(i)
+    own[0].wait()
+    normalize(j)
+    row_hop(xs_ref, 0, 0, normalize)
+    row_start(up_ref, ups_ref, 4)
+    halves = own_e // 2
+    pending.append(put(wout_ref, wouts_ref.at[part_e(d)], ws.at[0], wr.at[0], xn))
+    pending.append(put(wout_ref, wouts_ref.at[part_e(d)], ws.at[1], wr.at[1], yn))
+    for k in range(4):
+        relay(k)
+    row_hop(xs_ref, 0, 1, normalize)
+    for k in range(4, 8):
+        relay(k)
+    row_hop(xs_ref, 0, 2, normalize)
+    for at in range(4):
+        rank = flip(c, 1) * 4 + at
+        landed(xs_ref.at[rows(rank)], xcr.at[at], sib)
+        normalize(rank)
+    for k, i in enumerate(order):
+        slot = win_ref.at[block(dd, slots[i])]
+        if k % 2 == 0:
+            landed(slot, rr.at[k // 2], yn)
+        else:
+            landed(slot, rr.at[4 + k // 2], xn)
+    own += [pltpu.make_async_copy(xn_ref, xn_out, own_sem.at[6]), pltpu.make_async_copy(win_ref, win_out, own_sem.at[7])]
+    own[6].start()
+    own[7].start()
+    row_hop(ups_ref, 4, 0)
+    lead = u_ref.shape[1] - count
+    u_ref[:, 0:lead, :] = jnp.zeros((tiles, lead, 128), f32)
+
+    tile = 256
+
+    def spread(out, first, start):
+        def body(i, carry):
+            product = jnp.dot(xn_ref[...], win_ref[:, pl.ds(pl.multiple_of(start + i * tile, tile), tile)], preferred_element_type=f32)
+            for r in range(8):
+                for part in range(0, tile, 128):
+                    out[i * (tile // 128) + part // 128, pl.ds(first + r, length, stride=8), :] = product[r * length:(r + 1) * length, part:part + 128]
+            return carry
+
+        lax.fori_loop(0, width // tile, body, 0)
+
+    spread(u_ref, lead, 0)
+    taps = [vecs_ref[o:o + 1, :] for o in range(4)]
+    bias = vecs_ref[4:5, :]
+
+    def conv_step(i, carry):
+        r = pl.ds(pl.multiple_of(i * 32, 32), 32)
+        for n in range(tiles):
+            lanes = slice(n * 128, n * 128 + 128)
+            total = bias[:, lanes] + taps[3][:, lanes] * u_ref[n, pl.ds(pl.multiple_of(lead + i * 32, 8), 32), :]
+            for o in range(1, 4):
+                total = total + taps[3 - o][:, lanes] * (u_ref[n, pl.ds(pl.multiple_of(lead + i * 32 - 8 * o, 8), 32), :] * masks_ref[o - 1, r, :])
+            sig = jax.nn.sigmoid(total)
+            v_ref[n, r, :] = (total * sig).astype(bf16).astype(f32)
+            slope_ref[n, r, :] = sig * (1.0 + total * (1.0 - sig))
+        return carry
+
+    lax.fori_loop(0, count // 32, conv_step, 0)
+    for copy in own[3:5]:
+        copy.wait()
+    for i, (to, at) in enumerate(((xn, dx), (yn, dy), (dn, dd))):
+        landed(smalls_ref.at[part_e(at)], pr.at[16 + i], to)
+    quarter = count // 4
+    narrow = smalls_ref[:, 128:256].astype(f32)
+    packed = jnp.zeros((quarter, 128), f32)
+    for b in range(4):
+        r = slice(b * quarter, (b + 1) * quarter)
+        values = jnp.concatenate([v_ref[n, r, :].astype(bf16) for n in range(tiles)], axis=1)
+        part_ref[r, :] = jnp.dot(values, smalls_ref[:, 0:128], preferred_element_type=f32)
+        turned = pltpu.roll(narrow, 32 * b, 1) if b else narrow
+        packed = packed + jnp.dot(values, turned.astype(bf16), preferred_element_type=f32)
+    part_ref[count:count + quarter, :] = packed
+    slot = wouts_ref.at[part_e(dx)]
+    landed(slot, wr.at[0], xn)
+    slot = wouts_ref.at[part_e(dx, 0, halves)]
+    pending.append(put(slot, slot, ws.at[2], wr.at[2], yn))
+    slot = wouts_ref.at[part_e(dy)]
+    landed(slot, wr.at[1], yn)
+    slot = wouts_ref.at[part_e(dy, halves, halves)]
+    pending.append(put(slot, slot, ws.at[3], wr.at[3], xn))
+
+    def between():
+        spread(g_ref, 0, width)
+        row_hop(ups_ref, 4, 1)
+
+    line_total(part_ref, out_ref, sib_ref, base_ref, left_ref, right_ref, tor_ref, tol_ref, ts, tr, tls, tlr, trs, trr, tos, tor, between)
+    dl_ref[...] = out_ref[0:count, :].astype(bf16)
+    for b in range(4):
+        packed = out_ref[count:count + quarter, :]
+        kq_ref[b * quarter:(b + 1) * quarter, :] = pltpu.roll(packed, 128 - 32 * b, 1) if b else packed
+    row_hop(ups_ref, 4, 2)
+    for at in range(4):
+        landed(ups_ref.at[rows(flip(c, 1) * 4 + at)], xcr.at[4 + at], sib)
+    landed(wouts_ref.at[part_e(dd, 0, halves)], wr.at[2], yn)
+    landed(wouts_ref.at[part_e(dd, halves, halves)], wr.at[3], xn)
+    row_end(xs_ref, 0)
+    row_end(ups_ref, 4)
+    own[1].wait()
+    own[6].wait()
+    own[7].wait()
+    for copy in pending:
+        copy.wait_send()
+
+
+def line_total(part_ref, out_ref, sib_ref, base_ref, left_ref, right_ref, tor_ref, tol_ref, ss, sr, ls, lr, rs, rr, os_, or_, between):
+    d, c, z = place()
+    sib = (d, flip(c, 1), z)
+    left = (d, c, lax.rem(z + 3, 4))
+    right = (d, c, lax.rem(z + 1, 4))
+    rows = part_ref.shape[0] // 2
+    piece = rows // PIECES
+    mine, theirs = c * rows, flip(c, 1) * rows
+
+    def cut(p):
+        return pl.ds(p * piece, piece)
+
+    def far(base, p):
+        return pl.ds(pl.multiple_of(base + p * piece, 8), piece)
+
+    for p in range(PIECES):
+        put(part_ref.at[far(theirs, p)], sib_ref.at[cut(p)], ss.at[p], sr.at[p], sib)
+    for p in range(PIECES):
+        landed(sib_ref.at[cut(p)], sr.at[p], sib)
+        base_ref[cut(p), :] = part_ref[far(mine, p), :] + sib_ref[cut(p), :]
+
+        @pl.when(z == 0)
+        def _():
+            put(base_ref.at[cut(p)], left_ref.at[cut(p)], rs.at[p], lr.at[p], right)
+
+        @pl.when(z == 3)
+        def _():
+            put(base_ref.at[cut(p)], right_ref.at[cut(p)], ls.at[p], rr.at[p], left)
+
+    def from_left(p):
+        landed(left_ref.at[cut(p)], lr.at[p], left)
+
+        @pl.when(z < 3)
+        def _():
+            tor_ref[cut(p), :] = base_ref[cut(p), :] + left_ref[cut(p), :]
+            put(tor_ref.at[cut(p)], left_ref.at[cut(p)], rs.at[p], lr.at[p], right)
+
+    def from_right(p):
+        landed(right_ref.at[cut(p)], rr.at[p], right)
+
+        @pl.when(z > 0)
+        def _():
+            tol_ref[cut(p), :] = base_ref[cut(p), :] + right_ref[cut(p), :]
+            put(tol_ref.at[cut(p)], right_ref.at[cut(p)], ls.at[p], rr.at[p], left)
+
+    @pl.when(z == 1)
+    def _():
+        for p in range(PIECES):
+            from_left(p)
+
+    @pl.when(z == 2)
+    def _():
+        for p in range(PIECES):
+            from_right(p)
+
+    if between is not None:
+        between()
+
+    @pl.when(z < 2)
+    def _():
+        for p in range(PIECES):
+            from_right(p)
+
+    @pl.when(z >= 2)
+    def _():
+        for p in range(PIECES):
+            from_left(p)
+
+    for p in range(PIECES):
+        out_ref[far(mine, p), :] = base_ref[cut(p), :]
+
+        @pl.when(z > 0)
+        def _():
+            out_ref[far(mine, p), :] += left_ref[cut(p), :]
+
+        @pl.when(z < 3)
+        def _():
+            out_ref[far(mine, p), :] += right_ref[cut(p), :]
+
+        put(out_ref.at[far(mine, p)], out_ref.at[far(mine, p)], os_.at[p], or_.at[p], sib)
+    for p in range(PIECES):
+        landed(out_ref.at[far(theirs, p)], or_.at[p], sib)
+        sent(out_ref.at[far(mine, p)], os_.at[p], sib)
+        sent(part_ref.at[far(theirs, p)], ss.at[p], sib)
+
+        @pl.when(z < 3)
+        def _():
+            sent(base_ref.at[cut(p)], rs.at[p], right)
+
+        @pl.when(z > 0)
+        def _():
+            sent(base_ref.at[cut(p)], ls.at[p], left)
+
+
+def k1(tokens, upstream, cols, w_out, small, meta):
+    groups, ways = 4, cols.shape[0]
+    like = jax.ShapeDtypeStruct
+    length, model = tokens.shape[1:]
+    count = ways * length
+    channels = groups * w_out.shape[0]
+    dma = lambda n: pltpu.SemaphoreType.DMA((n,))
+    some = pl.BlockSpec(memory_space=pl.ANY)
+    far = pl.BlockSpec(memory_space=pltpu.HBM)
+    here = pl.BlockSpec(memory_space=pltpu.VMEM)
+    packed = count + count // 4
+    return pl.pallas_call(
+        k1_kernel,
+        out_shape=(
+            like((count, model), bf16),
+            like((count, model), bf16),
+            like((groups * ways * cols.shape[1], cols.shape[2]), bf16),
+            like((channels, model), bf16),
+            like((channels, small.shape[1]), bf16),
+            like((8, channels), f32),
+            like((1, model), f32),
+            like((4, count, 128), f32),
+            like((channels // 128, count + 24, 128), f32),
+            like((channels // 128, count, 128), f32),
+            like((channels // 128, count, 128), f32),
+            like((channels // 128, count, 128), f32),
+            like((count, 128), bf16),
+            like((count, 128), f32),
+        ),
+        in_specs=[some] * 6,
+        out_specs=(far,) * 4 + (here,) * 10,
+        scratch_shapes=[
+            pltpu.VMEM((count, model), bf16),
+            pltpu.VMEM((count, model), bf16),
+            pltpu.VMEM((groups * ways * cols.shape[1], cols.shape[2]), bf16),
+            pltpu.VMEM((groups, ways) + meta.shape, f32),
+            pltpu.VMEM((packed, 128), f32),
+            pltpu.VMEM((packed, 128), f32),
+        ] + [pltpu.VMEM((packed // 2, 128), f32)] * 6
+        + [dma(8), dma(7), dma(7), dma(3), dma(3), dma(8), dma(8), dma(8), dma(8), dma(8), dma(8), dma(7), dma(7), dma(19), dma(19), dma(8), dma(8), dma(4), dma(4)]
+        + [dma(PIECES) for _ in range(8)],
+        compiler_params=pltpu.CompilerParams(collective_id=0, has_side_effects=True, vmem_limit_bytes=56 * 1024 * 1024),
+    )(tokens, upstream, cols, w_out, small, meta)
+
+
+GROUP = 4
+
+
+def k2_kernel(states, dl_ref, kq_ref, wdt_ref, vecs_ref, keep_ref, live_ref, v_ref, g_ref, ups_ref, wout_ref,
+              m_ref, dg_ref, dpre_ref, dv_ref, part_ref, stat_ref,
+              s_ref, h_ref, rate_ref, w_ref, y_ref, dm_ref, kb_ref, hot_ref, drr_ref):
+    tiles, count = v_ref.shape[:2]
+    steps = count // 8
+    wide = states * 128
+    chunk = 256
+    first = pl.program_id(0) == 0
+    half = pl.program_id(0)
+    both = range(tiles)
+    rank = wdt_ref.shape[1]
+
+    @pl.when(first)
+    def _():
+        row = lax.broadcasted_iota(jnp.int32, (128, 512), 0)
+        col = lax.broadcasted_iota(jnp.int32, (128, 512), 1) // 128
+        for part in range(0, 2 * wide, 512):
+            hot_ref[:, part:part + 512] = jnp.where((row % 32 == col + part // 128) & (row < 96), 1.0, 0.0).astype(bf16)
+
+    lane = lax.broadcasted_iota(jnp.int32, (chunk, 128), 1)
+
+    def spread(i, carry):
+        r = pl.ds(pl.multiple_of(i * chunk, chunk), chunk)
+        value = jnp.where(lane < 2 * states, kq_ref[r, :], 0.0)
+        hi = value.astype(bf16).astype(f32)
+        mid = (value - hi).astype(bf16).astype(f32)
+        low = value - hi - mid
+        left = (hi + pltpu.roll(mid, 32, 1) + pltpu.roll(low, 64, 1)).astype(bf16)
+        for part in range(0, 2 * wide, 512):
+            kb_ref[r, part:part + 512] = jnp.dot(left, hot_ref[:, part:part + 512], preferred_element_type=f32)
+        return carry
+
+    lax.fori_loop(0, count // chunk, spread, 0)
+    cols = (((1,), (1,)), ((), ()))
+    length = count // 8
+
+    def gate_step(i, carry):
+        r = pl.ds(pl.multiple_of(i * chunk, chunk), chunk)
+        product = lax.dot_general(ups_ref[r, :], wout_ref[...], cols, preferred_element_type=f32)
+        for j in range(chunk // length):
+            for n in both:
+                dm_ref[n, pl.ds(i * (chunk // length) + j, length, stride=8), :] = product[j * length:(j + 1) * length, n * 128:(n + 1) * 128]
+        return carry
+
+    lax.fori_loop(0, count // chunk, gate_step, 0)
+    bias = vecs_ref[5:6, :]
+    skip = vecs_ref[6:7, :]
+    tile_of = lambda x, n: x[:, n * 128:(n + 1) * 128]
+    ks = lax.broadcasted_iota(jnp.int32, (128, 128), 1)
+
+    def before(i, carry):
+        seen = list(carry)
+        r = pl.ds(pl.multiple_of(i * 128, 128), 128)
+        live = live_ref[0, r, :]
+        k = jnp.where(ks < states, kq_ref[r, :], 0.0)
+        sk = jnp.sum(k * k, axis=1, keepdims=True)
+        pre = lax.dot_general(dl_ref[r, :], wdt_ref[...], cols, preferred_element_type=f32) + bias
+        for n in both:
+            beta = jax.nn.sigmoid(tile_of(pre, n))
+            part = 1.0 / (1.0 + beta * sk)
+            rate_ref[n, r, :] = beta * part
+            w_ref[n, r, :] = part * part * beta * (1.0 - beta)
+            g = g_ref[n, r, :]
+            sg = jax.nn.sigmoid(g)
+            dm = dm_ref[n, r, :] * live
+            dv_ref[n, r, :] = dm * (g * sg)
+            dm_ref[n, r, :] = dm * (sg * (1.0 + g * (1.0 - sg)))
+            shown = (beta * live).reshape(16, 8, 128)
+            seen[n] = seen[n] + jnp.sum(shown, axis=0)
+            seen[tiles + n] = jnp.maximum(seen[tiles + n], jnp.max(shown, axis=0))
+        return tuple(seen)
+
+    blank = jnp.zeros((8, 128), f32)
+    seen = lax.fori_loop(0, count // 128, before, (blank,) * (2 * tiles))
+    s_ref[0, 0] = jnp.zeros(s_ref.shape[2:], f32)
+    span = GROUP * 8
+    at = [slice(j * 8, j * 8 + 8) for j in range(GROUP)]
+
+    def view(ref, i):
+        r = pl.ds(pl.multiple_of(i * span, span), span)
+        return ref.at[:, r] if len(ref.shape) == 3 else ref.at[r]
+
+    def pair(ref, r):
+        return jnp.concatenate([ref[n, r, :] for n in both], axis=1)
+
+    def keep_pair(ref, r, value):
+        for n in both:
+            ref[n, r, :] = tile_of(value, n)
+
+    tile = lambda x: jnp.concatenate([x] * tiles, axis=1)
+
+    def fold(x):
+        total = tile_of(x, 0)
+        for n in range(1, tiles):
+            total = total + tile_of(x, n)
+        return total
+
+    def forward(i, carry):
+        keeps, rates, vs, kbs, ys = [view(x, i) for x in (keep_ref, rate_ref, v_ref, kb_ref, y_ref)]
+        keep = [keeps[0, r, :] for r in at]
+        rate = [pair(rates, r) for r in at]
+        value = [pair(vs, r) for r in at]
+        rv = [a * b for a, b in zip(rate, value)]
+        y = [skip * b for b in value]
+        for n in range(states):
+            state = s_ref[i, 0, n]
+            for j, r in enumerate(at):
+                kb = kbs[r, n * 128:(n + 1) * 128]
+                qb = kbs[r, wide + n * 128:wide + (n + 1) * 128]
+                state = (tile(keep[j]) - rate[j] * tile(kb * kb * keep[j])) * state + rv[j] * tile(kb)
+                if j < GROUP - 1:
+                    s_ref[i, j + 1, n] = state
+                else:
+                    s_ref[i + 1, 0, n] = state
+                y[j] = y[j] + state * tile(qb)
+        for j, r in enumerate(at):
+            keep_pair(ys, r, y[j])
+        return carry
+
+    lax.fori_loop(0, steps // GROUP, forward, 0)
+    h_ref[...] = jnp.zeros_like(h_ref)
+
+    def backward(step, carry):
+        i = steps // GROUP - 1 - step
+        keeps, rates, vs, kbs, dvs, ws, drrs = [view(x, i) for x in (keep_ref, rate_ref, v_ref, kb_ref, dv_ref, w_ref, drr_ref)]
+        keep = [keeps[0, r, :] for r in at]
+        rate = [pair(rates, r) for r in at]
+        value = [pair(vs, r) for r in at]
+        rv = [a * b for a, b in zip(rate, value)]
+        dy = [pair(dvs, r) for r in at]
+        hk = [jnp.zeros((8, tiles * 128), f32) for r in at]
+        hs2 = [jnp.zeros((8, tiles * 128), f32) for r in at]
+        for n in range(states):
+            ah = h_ref[n]
+            later = s_ref[i + 1, 0, n]
+            for j in range(GROUP - 1, -1, -1):
+                r = at[j]
+                kb = kbs[r, n * 128:(n + 1) * 128]
+                qb = kbs[r, wide + n * 128:wide + (n + 1) * 128]
+                kk = kb * keep[j]
+                held = tile(kb * kk)
+                h = dy[j] * tile(qb) + ah
+                prior = s_ref[i, j, n]
+                hs = h * prior
+                hk[j] = hk[j] + h * tile(kb)
+                hs2[j] = hs2[j] + hs * held
+                kbs[r, n * 128:(n + 1) * 128] = fold(h * rv[j]) - 2.0 * kk * fold(hs * rate[j])
+                kbs[r, wide + n * 128:wide + (n + 1) * 128] = fold(dy[j] * later)
+                later = prior
+                ah = (tile(keep[j]) - rate[j] * held) * h
+            h_ref[n] = ah
+        dskip = carry
+        for j, r in enumerate(at):
+            drate = value[j] * hk[j] - hs2[j]
+            drrs[r, :] = fold(drate * rate[j] * rate[j]) * (-2.0)
+            keep_pair(ws, r, drate * pair(ws, r))
+            keep_pair(dvs, r, rate[j] * hk[j] + skip * dy[j])
+            dskip = dskip + dy[j] * value[j]
+        return dskip
+
+    dskip = lax.fori_loop(0, steps // GROUP, backward, jnp.zeros((8, tiles * 128), f32))
+
+    quarter = count // 4
+    packed = jnp.zeros((quarter, 128), f32)
+    for b in range(4):
+        r = slice(b * quarter, (b + 1) * quarter)
+        total = jnp.zeros((quarter, 128), f32)
+        for part in range(0, 2 * wide, 512):
+            total = total + lax.dot_general(kb_ref[r, part:part + 512].astype(bf16), hot_ref[:, part:part + 512], cols, preferred_element_type=f32)
+        drr = jnp.sum(drr_ref[r, :], axis=1, keepdims=True)
+        k = kq_ref[r, :]
+        low = lax.broadcasted_iota(jnp.int32, (quarter, 128), 1)
+        total = jnp.where(low < 2 * states, total, 0.0) + jnp.where(low < states, k * drr, 0.0)
+        packed = packed + (pltpu.roll(total, 32 * b, 1) if b else total)
+
+    tail = pl.ds(count, quarter)
+    part_ref[tail, :] = jnp.where(first, packed, part_ref[tail, :] + packed)
+
+    def after(i, carry):
+        r = pl.ds(pl.multiple_of(i * 128, 128), 128)
+        live = live_ref[0, r, :]
+        sums = list(carry)
+        for n in both:
+            y = y_ref[n, r, :]
+            g = g_ref[n, r, :]
+            y_ref[n, r, :] = y * (g * jax.nn.sigmoid(g)) * live
+            dm_ref[n, r, :] = y * dm_ref[n, r, :]
+            low = w_ref[n, r, :].astype(bf16)
+            dpre_ref[r, n * 128:(n + 1) * 128] = low
+            sums[n] = sums[n] + jnp.sum(low.astype(f32).reshape(16, 8, 128), axis=0)
+        ddl = jnp.dot(dpre_ref[r, :], wdt_ref[...], preferred_element_type=f32)
+        part_ref[r, :] = jnp.where(first, ddl, part_ref[r, :] + ddl)
+        return tuple(sums)
+
+    sums = lax.fori_loop(0, count // 128, after, (blank,) * tiles)
+
+    def by_row(j, carry):
+        r = pl.ds(pl.multiple_of(j * length, length), length)
+        for n in both:
+            m_ref[r, n * 128:(n + 1) * 128] = y_ref[n, pl.ds(j, length, stride=8), :].astype(bf16)
+            dg_ref[r, n * 128:(n + 1) * 128] = dm_ref[n, pl.ds(j, length, stride=8), :].astype(bf16)
+        return carry
+
+    lax.fori_loop(0, 8, by_row, 0)
+    stat_ref[...] = jnp.zeros_like(stat_ref)
+    for n in both:
+        lanes = slice(n * 128, (n + 1) * 128)
+        stat_ref[0:1, lanes] = jnp.sum(seen[n], axis=0, keepdims=True)
+        stat_ref[1:2, lanes] = jnp.max(seen[tiles + n], axis=0, keepdims=True)
+        stat_ref[5:6, lanes] = jnp.sum(sums[n], axis=0, keepdims=True)
+        stat_ref[6:7, lanes] = jnp.sum(tile_of(dskip, n), axis=0, keepdims=True)
+
+
+def k2(dl, kq, smalls, vecs, masks, v, g, ups, wout, states):
+    count, rank = dl.shape
+    channels, model = wout.shape
+    tiles = 2
+    width = tiles * 128
+    like = jax.ShapeDtypeStruct
+    once = pl.Buffered(buffer_count=1)
+    whole = lambda a: pl.BlockSpec(a.shape, lambda h: (0,) * a.ndim, pipeline_mode=once)
+    deep = pl.BlockSpec((tiles, count, 128), lambda h: (h, 0, 0))
+    flat = pl.BlockSpec((count, width), lambda h: (0, h))
+    return pl.pallas_call(
+        functools.partial(k2_kernel, states),
+        grid=(channels // width,),
+        out_shape=(
+            like((count, channels), bf16),
+            like((count, channels), bf16),
+            like((count, channels), bf16),
+            like(v.shape, f32),
+            like((count + count // 4, 128), f32),
+            like((8, channels), f32),
+        ),
+        in_specs=[
+            whole(dl), whole(kq),
+            pl.BlockSpec((width, 128), lambda h: (h, 2)),
+            pl.BlockSpec((8, width), lambda h: (0, h)),
+            pl.BlockSpec((1, count, 128), lambda h: (0, 0, 0), pipeline_mode=once),
+            pl.BlockSpec((1, count, 128), lambda h: (3, 0, 0), pipeline_mode=once),
+            deep, deep, whole(ups),
+            pl.BlockSpec((width, model), lambda h: (h, 0)),
+        ],
+        out_specs=(flat, flat, flat, deep, pl.BlockSpec((count + count // 4, 128), lambda h: (0, 0)), pl.BlockSpec((8, width), lambda h: (0, h))),
+        scratch_shapes=[
+            pltpu.VMEM((count // 8 // GROUP + 1, GROUP, states, 8, width), f32),
+            pltpu.VMEM((states, 8, width), f32),
+        ] + [pltpu.VMEM((tiles, count, 128), f32)] * 4
+        + [pltpu.VMEM((count, 2 * states * 128), f32), pltpu.VMEM((128, 2 * states * 128), bf16), pltpu.VMEM((count, 128), f32)],
+        compiler_params=pltpu.CompilerParams(vmem_limit_bytes=60 * 1024 * 1024),
+    )(dl, kq, smalls, vecs, masks, masks, v, g, ups, wout)
 
 
 def add_rows(dst, sources):
@@ -755,7 +1266,6 @@
         compiler_params=pltpu.CompilerParams(collective_id=4, has_side_effects=True),
     )(part)
 
-
 def masks(lengths, count):
     ends = jnp.cumsum(lengths, axis=1)
     places = jnp.arange(count, dtype=jnp.int32)
@@ -770,15 +1280,6 @@
 def columns(weights, ways):
     rows, total = weights.shape
     return weights.reshape(rows, 2, total // (2 * ways * 128), ways, 128)
-
-
-def group_sum(part, rank, direct, which):
-    if not direct:
-        return lax.psum(part, TP)
-    count, rest = part.shape[0], part.shape[1] - rank
-    packed = jnp.concatenate([part[:, :rank], part[:, rank:].T.reshape(-1, rank)], axis=0)
-    packed = group_total(packed, which)
-    return jnp.concatenate([packed[:count], packed[count:].reshape(rest, count).T], axis=1)
 
 
 def on_device(tokens, lengths, gain, w_in, conv_w, conv_b, w_x, w_dt, dt_bias, skip, w_out, grad_out):
@@ -792,38 +1293,25 @@
     rank = w_dt.shape[1]
     states = (w_x.shape[1] - rank) // 2
     cols = w_in.reshape(own_d, 2, groups, ways, own_e).transpose(3, 0, 1, 2, 4).reshape(ways, own_d, 2 * channels)
+    cols = lax.all_to_all(cols, TP, split_axis=0, concat_axis=0, tiled=True)
+    win = lax.all_gather(cols, "dp", axis=0, tiled=True).reshape(model, 2 * channels)
     small = jnp.concatenate([w_x, w_dt, conv_w, conv_b[:, None], dt_bias[:, None], skip[:, None]], axis=1)
     small_width = small.shape[1]
-    direct = groups == 4 and lax.axis_size("z") == 4
+    small = lax.all_gather(small, "dp", axis=0, tiled=True)
+    wx = small[:, :rank + 2 * states]
+    wdt = small[:, rank + 2 * states:2 * rank + 2 * states]
+    rest = small[:, 2 * rank + 2 * states:].astype(f32)
+    taps, bias, dtb, skips = rest[:, :4], rest[:, 4], rest[:, 5], rest[:, 6]
+    wout = lax.all_gather(w_out, "dp", axis=0, tiled=True)
+    gains = lax.all_gather(gain, ALL, axis=0, tiled=True).astype(f32)
     x = tokens[0].astype(f32)
     scale = lax.rsqrt(jnp.mean(x * x, axis=1, keepdims=True) + EPS)
-    if direct:
-        padded = -small_width % 128
-        meta = jnp.zeros((16, 128), bf16).at[0, :own_d].set(gain).at[1, :5].set(lengths[0].astype(bf16))
-        xs, ups, win, wout, small, metas = front(tokens, grad_out, cols, w_out, jnp.pad(small, ((0, 0), (0, padded))), meta)
-        gains = metas[:, :, 0, :own_d].reshape(model).astype(f32)
-        lens = lax.dynamic_index_in_dim(metas, lax.axis_index("dp"), keepdims=False)[:, 1, :5].astype(jnp.int32)
-    else:
-        cols = lax.all_to_all(cols, TP, split_axis=0, concat_axis=0, tiled=True)
-        win = lax.all_gather(cols, "dp", axis=0, tiled=True)
-        small = lax.all_gather(small, "dp", axis=0, tiled=True)
-        wout = lax.all_gather(w_out, "dp", axis=0, tiled=True)
-        gains = lax.all_gather(gain, ALL, axis=0, tiled=True).astype(f32)
-        xs = lax.all_gather(tokens, TP, axis=0, tiled=True)
-        ups = lax.all_gather(grad_out, TP, axis=0, tiled=True)
-        lens = lax.all_gather(lengths, TP, axis=0, tiled=True)
+    xn = (x * scale * gains).astype(bf16)
+    xns = lax.all_gather(xn, TP, axis=0, tiled=True)
+    ups = lax.all_gather(grad_out[0], TP, axis=0, tiled=True)
+    lens = lax.all_gather(lengths, TP, axis=0, tiled=True)
     rows = lens.shape[0]
     tall = rows * length
-    win = win.reshape(model, 2 * channels)
-    wout = wout.reshape(channels, model)
-    small = small.reshape(channels, -1)
-    ups = ups.reshape(tall, model)
-    wide_x = xs.reshape(tall, model).astype(f32)
-    xns = (wide_x * lax.rsqrt(jnp.mean(wide_x * wide_x, axis=1, keepdims=True) + EPS) * gains).astype(bf16)
-    wx = small[:, :rank + 2 * states]
-    wdt = small[:, rank + 2 * states:2 * rank + 2 * states]
-    rest = small[:, 2 * rank + 2 * states:small_width].astype(f32)
-    taps, bias, dtb, skips = rest[:, :4], rest[:, 4], rest[:, 5], rest[:, 6]
 
     def time_major(a):
         return a.reshape(rows, length, -1).transpose(1, 0, 2).reshape(tall, -1)
@@ -844,8 +1332,7 @@
     sig = jax.nn.sigmoid(c)
     v16 = (c * sig).astype(bf16).reshape(tall, channels)
     v = v16.astype(f32)
-    whole = group_sum(jnp.dot(v16, wx, preferred_element_type=f32), rank, direct, 1)
-    p = whole
+    p = lax.psum(jnp.dot(v16, wx, preferred_element_type=f32), TP)
     dl = p[:, :rank].astype(bf16)
     kq = p[:, rank:]
     dims_cols = (((1,), (1,)), ((), ()))
@@ -862,15 +1349,21 @@
     m, dg, dpre, dv, dkq, stats = mixer(flags, kq3, sk, pre, v, g, dm, skips[None], states=states, width=256, unroll=4)
     stats = stats.transpose(1, 2, 0, 3).reshape(3, 8, channels)
     dskip = jnp.sum(stats[0], axis=0)
+    total = lax.psum(jnp.sum(stats[1]), ALL)
+    peak = lax.pmax(jnp.max(stats[2]), ALL)
+    beta_mean = total / float(groups * ways * length * inner)
     m16 = row_major(m).astype(bf16)
     out = jnp.dot(m16, wout, preferred_element_type=f32).astype(bf16)
+    out = lax.psum_scatter(out, TP, scatter_dimension=0, tiled=True)
+    block_out = (x + out.astype(f32)).astype(bf16)
     grad_wout = lax.dot_general(m16, ups, dims_rows, preferred_element_type=f32).astype(bf16)
+    grad_wout = lax.psum_scatter(grad_wout, "dp", scatter_dimension=0, tiled=True)
     dpre16 = dpre.astype(bf16)
     grad_dtb = jnp.sum(dpre16.astype(f32), axis=0)
     grad_wdt = lax.dot_general(dpre16, dl, dims_rows, preferred_element_type=f32)
     ddl = jnp.dot(dpre16, wdt, preferred_element_type=f32)
     dkq = dkq[:, :2 * states] + dkq[:, 2 * states:2 * states + 1] * jnp.pad(keys, ((0, 0), (0, states)))
-    dp16 = group_sum(jnp.concatenate([ddl, dkq], axis=1), rank, direct, 2).astype(bf16)
+    dp16 = lax.psum(jnp.concatenate([ddl, dkq], axis=1), TP).astype(bf16)
     grad_wx = lax.dot_general(v16, dp16, dims_rows, preferred_element_type=f32)
     dvt = dv + lax.dot_general(dp16, wx, dims_cols, preferred_element_type=f32)
     dc = (dvt * (sig.reshape(tall, channels) * (1.0 + c.reshape(tall, channels) * (1.0 - sig.reshape(tall, channels))))).reshape(length, rows, channels)
@@ -882,37 +1375,117 @@
     grad_conv = jnp.stack(grad_taps[::-1] + [jnp.sum(dc, axis=(0, 1)), grad_dtb, dskip], axis=1)
     dz = row_major(jnp.concatenate([du.reshape(tall, channels), dg], axis=1)).astype(bf16)
     gwin = lax.dot_general(xns, dz, dims_rows, preferred_element_type=f32).astype(bf16)
+    gwin = lax.psum_scatter(gwin, "dp", scatter_dimension=0, tiled=True)
+    gwin = lax.all_to_all(gwin.reshape(ways, own_d, 2 * channels), TP, split_axis=0, concat_axis=0, tiled=True)
+    grad_win = gwin.reshape(ways, own_d, 2, groups, own_e).transpose(1, 2, 3, 0, 4).reshape(own_d, 2 * inner).astype(f32)
+    dxn = lax.dot_general(dz, win, dims_cols, preferred_element_type=f32).astype(bf16)
+    dxn = lax.psum_scatter(dxn, TP, scatter_dimension=0, tiled=True).astype(f32)
+    small_grad = lax.psum_scatter(jnp.concatenate([grad_wx, grad_wdt, grad_conv], axis=1), "dp", scatter_dimension=0, tiled=True)
+    inner_grad = dxn * gains
+    dxx = scale * inner_grad - x * (scale * scale * scale) * (jnp.sum(inner_grad * x, axis=1, keepdims=True) / model)
+    grad_tokens = (grad_out[0].astype(f32) + dxx).astype(bf16)
+    grad_gain = lax.psum_scatter(jnp.sum(dxn * x * scale, axis=0), ALL, scatter_dimension=0, tiled=True)
+    at = rank + 2 * states
+    return (
+        block_out[None],
+        grad_tokens[None],
+        grad_gain,
+        grad_win,
+        small_grad[:, at + rank:at + rank + 4],
+        small_grad[:, at + rank + 4],
+        small_grad[:, :at],
+        small_grad[:, at:at + rank],
+        small_grad[:, at + rank + 5],
+        small_grad[:, at + rank + 6],
+        grad_wout.astype(f32),
+        beta_mean,
+        peak,
+    )
+
+
+def prepare(gain, lengths, w_in, conv_w, conv_b, w_x, w_dt, dt_bias, skip, ways, groups):
+    own_d, own_e = w_in.shape[0], conv_w.shape[0]
+    channels = own_e * groups
+    cols = w_in.reshape(own_d, 2, groups, ways, own_e).transpose(3, 0, 1, 2, 4).reshape(ways, own_d, 2 * channels)
+    small = jnp.concatenate([jnp.pad(w_x, ((0, 0), (0, 256 - w_x.shape[1]))), w_dt], axis=1)
+    top = jnp.concatenate([jnp.tile(gain.astype(f32), 2)[None], jnp.pad(lengths.astype(f32), ((0, 0), (0, 123))), jnp.zeros((6, 128), f32)])
+    low = jnp.concatenate([conv_w.astype(f32).T, conv_b.astype(f32)[None], dt_bias.astype(f32)[None], skip.astype(f32)[None], jnp.zeros((1, own_e), f32)])
+    return cols, small, jnp.concatenate([top, low])
+
+
+def on_device_direct(tokens, lengths, gain, w_in, conv_w, conv_b, w_x, w_dt, dt_bias, skip, w_out, grad_out):
+    groups, ways = 4, 8
+    length, model = tokens.shape[1:]
+    own_d = w_in.shape[0]
+    own_e = conv_w.shape[0]
+    inner = w_in.shape[1] // 2
+    channels = inner // ways
+    rank = w_dt.shape[1]
+    states = (w_x.shape[1] - rank) // 2
+    rows = ways
+    tall = rows * length
+    cols, small, meta = prepare(gain, lengths, w_in, conv_w, conv_b, w_x, w_dt, dt_bias, skip, ways, groups)
+    xns, ups, win, wout, smalls, vecs, gains, masks, u_pad, g, v, slope, dl, kq_wide = k1(tokens, grad_out, cols, w_out, small, meta)
+    wx = smalls[:, :rank + 2 * states]
+    taps = vecs[:4].T
+    x = tokens[0].astype(f32)
+    scale = lax.rsqrt(jnp.mean(x * x, axis=1, keepdims=True) + EPS)
+
+    def time_major(a):
+        return a.reshape(rows, length, -1).transpose(1, 0, 2).reshape(tall, -1)
+
+    def row_major(a):
+        return a.reshape(length, rows, -1).transpose(1, 0, 2).reshape(tall, -1)
+
+    v4, g4 = v, g
+    u_pad, v, slope = [a.transpose(1, 0, 2).reshape(-1, channels) for a in (u_pad, v, slope)]
+    u = u_pad[24:].reshape(length, rows, channels)
+    same = [masks[o, :, 0].reshape(length, rows) for o in range(3)]
+    shifted = []
+    for offset in range(1, 4):
+        shifted.append(jnp.pad(u, ((offset, 0), (0, 0), (0, 0)))[:length] * same[offset - 1][:, :, None])
+    v16 = v.astype(bf16)
+    dims_cols = (((1,), (1,)), ((), ()))
+    dims_rows = (((0,), (0,)), ((), ()))
+    m16, dg16, dpre16, dv, part, stat = k2(dl, kq_wide, smalls, vecs, masks, v4, g4, ups, wout, states)
+    dv = dv.transpose(1, 0, 2).reshape(tall, channels)
+    dskip, grad_dtb = stat[6], stat[5]
+    out = jnp.dot(m16, wout, preferred_element_type=f32).astype(bf16)
+    grad_wout = lax.dot_general(m16, ups, dims_rows, preferred_element_type=f32).astype(bf16)
+    grad_wdt = lax.dot_general(dpre16, dl, dims_rows, preferred_element_type=f32)
+    part = group_total(part, 2)
+    dp16 = jnp.concatenate([part[:tall], part[tall:].reshape(tall // 4, 4, 32).transpose(1, 0, 2).reshape(tall, 32)], axis=1).astype(bf16)
+    grad_wx = lax.dot_general(v16, dp16, dims_rows, preferred_element_type=f32)
+    dvt = dv + lax.dot_general(dp16, wx, dims_cols, preferred_element_type=f32)
+    dc = (dvt * slope).reshape(length, rows, channels)
+    du = taps[:, 3] * dc
+    grad_taps = [jnp.sum(dc * u, axis=(0, 1))]
+    for offset in range(1, 4):
+        grad_taps.append(jnp.sum(dc * shifted[offset - 1], axis=(0, 1)))
+        du = du + taps[:, 3 - offset] * jnp.pad((dc * same[offset - 1][:, :, None])[offset:], ((0, offset), (0, 0), (0, 0)))
+    grad_conv = jnp.stack(grad_taps[::-1] + [jnp.sum(dc, axis=(0, 1)), grad_dtb, dskip], axis=1)
+    dz = jnp.concatenate([row_major(du.reshape(tall, channels)).astype(bf16), dg16], axis=1)
+    gwin = lax.dot_general(xns, dz, dims_rows, preferred_element_type=f32).astype(bf16)
     dxn = lax.dot_general(dz, win, dims_cols, preferred_element_type=f32).astype(bf16)
     small_grad = jnp.concatenate([grad_wx, grad_wdt, grad_conv], axis=1)
-    if direct:
-        small_grad = jnp.pad(small_grad, ((0, 0), (0, padded)))
-        dxn, out, gwin, grad_wout, small_grad = back(
-            dxn.reshape(2, 4, length, model), out.reshape(2, 4, length, model), gwin.reshape(groups, ways * own_d, 2 * channels),
-            grad_wout.reshape(groups, own_e, model), small_grad.reshape(groups, own_e, -1))
-    else:
-        out = lax.psum_scatter(out, TP, scatter_dimension=0, tiled=True).astype(f32)
-        grad_wout = lax.psum_scatter(grad_wout, "dp", scatter_dimension=0, tiled=True).astype(f32)
-        gwin = lax.psum_scatter(gwin, "dp", scatter_dimension=0, tiled=True)
-        gwin = lax.all_to_all(gwin.reshape(ways, own_d, 2 * channels), TP, split_axis=0, concat_axis=0, tiled=True)
-        dxn = lax.psum_scatter(dxn, TP, scatter_dimension=0, tiled=True).astype(f32)
-        small_grad = lax.psum_scatter(small_grad, "dp", scatter_dimension=0, tiled=True)
+    small_grad = jnp.pad(small_grad, ((0, 0), (0, -small_grad.shape[1] % 128)))
+    dxn, out, gwin, grad_wout, small_grad = back(
+        dxn.reshape(2, 4, length, model), out.reshape(2, 4, length, model), gwin.reshape(groups, ways * own_d, 2 * channels),
+        grad_wout.reshape(groups, own_e, model), small_grad.reshape(groups, own_e, -1))
     block_out = (x + out).astype(bf16)
     grad_win = gwin.reshape(ways, own_d, 2, groups, own_e).transpose(1, 2, 3, 0, 4).reshape(own_d, 2 * inner).astype(f32)
+    gains = gains[0]
     inner_grad = dxn * gains
     dxx = scale * inner_grad - x * (scale * scale * scale) * (jnp.sum(inner_grad * x, axis=1, keepdims=True) / model)
     grad_tokens = (grad_out[0].astype(f32) + dxx).astype(bf16)
     grad_gain = jnp.sum(dxn * x * scale, axis=0)
-    seen, peak = jnp.sum(stats[1]), jnp.max(stats[2])
-    if direct:
-        part = grad_gain.reshape(groups, ways, own_d).transpose(1, 0, 2)
-        part = jnp.pad(part, ((0, 0), (0, 8 - groups), (0, 128 - own_d)))
-        part = part.at[:, 4, 0].set(seen).at[:, 4, 1].set(peak)
-        part = tiny(part)
-        grad_gain = lax.dynamic_index_in_dim(part, lax.axis_index("dp"), keepdims=False)[:own_d]
-        seen, peak = part[4, 0], part[4, 1]
-    else:
-        grad_gain = lax.psum_scatter(grad_gain, ALL, scatter_dimension=0, tiled=True)
-        seen, peak = lax.psum(seen, ALL), lax.pmax(peak, ALL)
+    seen, peak = jnp.sum(stat[0]), jnp.max(stat[1])
+    part = grad_gain.reshape(groups, ways, own_d).transpose(1, 0, 2)
+    part = jnp.pad(part, ((0, 0), (0, 8 - groups), (0, 128 - own_d)))
+    part = part.at[:, 4, 0].set(seen).at[:, 4, 1].set(peak)
+    part = tiny(part)
+    grad_gain = lax.dynamic_index_in_dim(part, lax.axis_index("dp"), keepdims=False)[:own_d]
+    seen, peak = part[4, 0], part[4, 1]
     beta_mean = seen / float(groups * ways * length * inner)
     at = rank + 2 * states
     return (
@@ -932,10 +1505,16 @@
     )
 
 
+def on_device_any(*args):
+    if lax.axis_size("dp") == 4 and lax.axis_size("z") == 4:
+        return on_device_direct(*args)
+    return on_device(*args)
+
+
 def solution(mesh):
     wide, narrow = mesh.devices.shape
     fine = Mesh(mesh.devices.reshape(wide // 2, 2, narrow), ALL)
     cut = (P(ALL, None), P(ALL))
     in_specs = (P(ALL, None, None), cut[0], cut[1], cut[0], cut[0], cut[1], cut[0], cut[0], cut[1], cut[1], cut[0], P(ALL, None, None))
     out_specs = (P(ALL, None, None), P(ALL, None, None), cut[1], cut[0], cut[0], cut[1], cut[0], cut[0], cut[1], cut[1], cut[0], P(), P())
-    return jax.shard_map(on_device, mesh=fine, in_specs=in_specs, out_specs=out_specs, check_vma=False)
+    return jax.shard_map(on_device_any, mesh=fine, in_specs=in_specs, out_specs=out_specs, check_vma=False)

time: 474 us -> 429 us (0.905)
  matrix products: 47.6 us -> 28.8 us
  other arithmetic: 32.5 us -> 16 us
  local copies, waits for them, and re-layouts: 60.2 us -> 49.1 us
  Pallas kernels: 323 us -> 329 us
    pallas_call x2, Pallas kernels: 155 us -> 182 us  [the longest x1 124 us: k1(): pl.pallas_call(k1_kernel, out_shape=(like((count, model), bf16), like((co...]
    pallas_call x2 -> x1, Pallas kernels: 45.2 us -> 24.7 us  [group_total(): pl.pallas_call(total_kernel, out_shape=jax.ShapeDtypeStruct(part.shape, f...]
    dot_general x12 -> x7, matrix products: 47.6 us -> 28.8 us  [the longest x1 8.57 us: on_device_direct(): lax.dot_general(xns, dz, dims_rows, preferred_element_type=f32).astype(bf16)]
    unnamed x117 -> x65, local copies, waits for them, and re-layouts: 25 us -> 10.7 us
    reduce_sum x7 -> x3, other arithmetic: 15.3 us -> 5.86 us  [the longest x1 5.39 us: on_device_direct(): grad_taps.append(jnp.sum(dc * shifted[offset - 1], axis=(0, 1)))]
    div x2 -> x1, other arithmetic: 6.97 us -> 0.01 us  [on_device_direct(): jnp.sum(inner_grad * x, axis=1, keepdims=True) / model]
    reshape x12 -> x8, local copies, waits for them, and re-layouts: 10.5 us -> 11.8 us  [the longest x2 6.02 us: on_device_direct(): u = u_pad[24:].reshape(length, rows, channels)]
where the time goes in v3:
time: 429 us; the launch traced here: 426 us
  Pallas kernels  329 us (77%)
  local copies, waits for them, and re-layouts  49.1 us (11%)
  matrix products  28.8 us (7%)
  other arithmetic  16 us (4%)
    pallas_call x1, Pallas kernels, k1(): pl.pallas_call(k1_kernel, out_shape=(like((count, model), bf16), like((co...  124 us
    pallas_call x1, Pallas kernels, back(): pl.pallas_call(back_kernel, out_shape=(like((rows, columns), f32), like((...  112 us
    pallas_call x1, Pallas kernels, k2(): pl.pallas_call(functools.partial(k2_kernel, states), grid=(channels // wi...  58.1 us
    pallas_call x1, Pallas kernels, group_total(): pl.pallas_call(total_kernel, out_shape=jax.ShapeDtypeStruct(part.shape, f...  24.7 us
    pallas_call x1, Pallas kernels, tiny(): pl.pallas_call(tiny_kernel, out_shape=jax.ShapeDtypeStruct((8, 128), f32)...  11 us
    unnamed x65, local copies, waits for them, and re-layouts  10.7 us

profile of v3, /device:TPU:8, one launch (start us, length us, event | category | flops | bytes accessed | tf_op | source)
XLA Modules:
  0.0 425.9 jit_solution(13201276152317095410)
XLA Ops:
  7.2 1.5 reshape.176.cols_ref
  9.6 123.6 %shard_map.219 = (bf16[1024,2048]{1,0:T(8,128)(2,1)}, bf16[1024,2048]{1,0:T(8,128)(2,1)}, bf16[2048,1024]{1,0:T(8,128)(2,1)}, bf16[512,2048]{1,0:T(8,128)(2,1)},...) custom-call(bf16[1,128,2048]{2,1,0:T(8,128)(2,1)} %tok_ref.1, ...), custom_call_target="tpu_custom_call" | custom-call | tf_op jit(solution)/shard_map/pallas_call | solution.py:732
  133.2 58.1 %shard_map.220 = (bf16[1024,512]{1,0:T(8,128)(2,1)}, bf16[1024,512]{1,0:T(8,128)(2,1)}, bf16[1024,512]{1,0:T(8,128)(2,1)}, f32[4,1024,128]{2,1,0:T(8,128)}, f32[1280,128]{1,0:T(8,128)}, /*index=5*/f32[8,512]{1,0:T(8,128)}) custom-call(bf16[1024,128]{1,0:T(8,128)(2,1)} %get-tuple-element.63.dl_ref, f32[1024,128]{1,0:T(8,128)} %get-tuple-element.64.kq_ref, ...), custom_call_target="tpu_custom_call" | custom-call | tf_op jit(solution)/shard_map/pallas_call | solution.py:992
  192.4 24.7 %shard_map.221 = f32[1280,128]{1,0:T(8,128)S(1)} custom-call(f32[1280,128]{1,0:T(8,128)S(1)} %copy-done), custom_call_target="tpu_custom_call" | custom-call | tf_op jit(solution)/shard_map/pallas_call | solution.py:328
  220.5 1.9 copy.44
  222.4 1.9 copy.47
  224.3 1.7 slice.187
  226.1 2.0 copy.53
  228.1 2.9 copy.54
  231.0 1.9 copy.48
  233.0 1.8 copy.49
  234.8 4.2 fusion.29
  245.3 2.7 copy.52
  247.9 3.1 reshape.186
  251.0 5.4 %fusion.2 = (f32[512]{0:T(512)S(1)}, f32[512]{0:T(512)S(1)}, f32[512]{0:T(512)S(1)}, bf16[8,128,512]{2,0,1:T(8,128)(2,1)S(1)}) fusion(f32[128,8,512]{2,1,0:T(8,128)} %reshape.186, f32[128,8]{1,0:T(8,128)S(1)} %mul.175, f32[1024,512]{1,0:T(8,128)S(1)} %get-tuple-element.141, f32[128,8]{1,0:T(8,128)} %copy-done.18, f32[128,8]{1,0:T(8,128)} %copy-done.19, ...), kind=kLoop, calls=%fused_computation.9 | loop fusion | flops 8911360 | bytes 11462656 | tf_op jit(solution)/shard_map/reduce_sum | solution.py:1464
  260.0 8.6 %convolution_convert_fusion.1 = bf16[2048,1024]{1,0:T(8,128)(2,1)} fusion(bf16[1024,2048]{1,0:T(8,128)(2,1)} %get-tuple-element.77, bf16[1024,512]{1,0:T(8,128)(2,1)S(1)} %copy-done.28, bf16[1024,512]{1,0:T(8,128)(2,1)S(1)} %bitcast.118), kind=kOutput, calls=%fused_computation.1 | convolution fusion | flops 4301258752 | bytes 10485760 | tf_op jit(solution)/shard_map/dot_general | solution.py:1468
  268.6 6.4 %convolution_convert_fusion.2 = bf16[1024,2048]{1,0:T(8,128)(2,1)} fusion(bf16[2048,1024]{1,0:T(8,128)(2,1)S(1)} %copy-done.26, bf16[1024,512]{1,0:T(8,128)(2,1)S(1)} %copy-done.28, bf16[1024,512]{1,0:T(8,128)(2,1)S(1)} %bitcast.119), kind=kOutput, calls=%fused_computation.2 | convolution fusion | flops 4301258752 | bytes 10485760 | tf_op jit(solution)/shard_map/dot_general | solution.py:1469
  275.0 4.4 %convolution_convert_fusion = bf16[1024,2048]{1,0:T(8,128)(2,1)} fusion(bf16[1024,512]{1,0:T(8,128)(2,1)S(1)} %copy-done.27, bf16[512,2048]{1,0:T(8,128)(2,1)S(1)} %copy-done.10), kind=kOutput, calls=%fused_computation | convolution fusion | flops 2149580800 | bytes 7340032 | tf_op jit(solution)/shard_map/dot_general | solution.py:1453
  279.4 3.7 convolution_convert_fusion.3
  283.1 111.6 %shard_map.222 = (f32[128,2048]{1,0:T(8,128)}, f32[128,2048]{1,0:T(8,128)}, bf16[8,64,1024]{2,1,0:T(8,128)(2,1)}, f32[128,2048]{1,0:T(8,128)}, f32[128,384]{1,0:T(8,128)}) custom-call(bf16[2,4,128,2048]{3,2,1,0:T(8,128)(2,1)} %bitcast.107, bf16[2,4,128,2048]{3,2,1,0:T(8,128)(2,1)} %bitcast.108, bf16[4,512,1024]{2,1,0:T(8,128)(2,1)} %bitcast.106, ...), custom_call_target="tpu_custom_call" | custom-call | tf_op jit(solution)/shard_map/pallas_call | solution.py:1206
  394.7 2.0 reshape.196
  398.0 2.5 copy.66
  403.8 11.0 %shard_map.223 = f32[8,128]{1,0:T(8,128)} custom-call(f32[8,8,128]{2,1,0:T(8,128)} %copy-done.20), custom_call_target="tpu_custom_call" | custom-call | tf_op jit(solution)/shard_map/pallas_call | solution.py:1260
  422.4 2.3 copy.72
  (120 shorter events, 32.9 us)
Async XLA Ops:
  6.8 2.0 copy-start.21
  6.8 2.1 copy-start.24
  192.4 25.8 %copy-start.4 = (f32[4,1024,128]{2,1,0:T(8,128)S(1)}, f32[4,1024,128]{2,1,0:T(8,128)}, u32[]{:S(2)}) copy-start(f32[4,1024,128]{2,1,0:T(8,128)} %get-tuple-element.67.v_ref) | copy-start | bytes 6291460
  226.1 2.0 copy-start.1
  232.9 1.9 copy-start.9
  232.9 1.9 copy-start.13
  234.8 4.2 copy-start.3
  241.2 1.6 copy-start.18
  242.9 1.6 copy-start.19
  242.9 1.5 copy-start.22
  242.9 2.4 copy-start.2
  251.0 5.4 %copy-start.15 = (bf16[1024,128]{1,0:T(8,128)(2,1)S(1)}, bf16[1024,128]{1,0:T(8,128)(2,1)}, u32[]{:S(2)}) copy-start(bf16[1024,128]{1,0:T(8,128)(2,1)} %get-tuple-element.63.dl_ref) | copy-start | bytes 786436
  251.0 5.4 %copy-start.17 = (bf16[1024,512]{1,0:T(8,128)(2,1)S(1)}, bf16[1024,512]{1,0:T(8,128)(2,1)}, u32[]{:S(2)}) copy-start(bf16[1024,512]{1,0:T(8,128)(2,1)} %get-tuple-element.78) | copy-start | bytes 3145732
  251.0 5.8 %copy-start.25 = (f32[8,512]{1,0:T(8,128)S(1)}, f32[8,512]{1,0:T(8,128)}, u32[]{:S(2)}) copy-start(f32[8,512]{1,0:T(8,128)} %get-tuple-element.80) | copy-start | bytes 49156
  251.0 6.4 %copy-start.12 = (f32[512,160]{0,1:T(8,128)S(1)}, f32[512,160]{0,1:T(8,128)}, u32[]{:S(2)}) copy-start(f32[512,160]{0,1:T(8,128)} %fusion.21) | copy-start | bytes 983044
  260.0 8.6 %copy-start.26 = (bf16[2048,1024]{1,0:T(8,128)(2,1)S(1)}, bf16[2048,1024]{1,0:T(8,128)(2,1)}, u32[]{:S(2)}) copy-start(bf16[2048,1024]{1,0:T(8,128)(2,1)} %get-tuple-element.75) | copy-start | bytes 12582916
  268.6 6.4 %copy-start.10 = (bf16[512,2048]{1,0:T(8,128)(2,1)S(1)}, bf16[512,2048]{1,0:T(8,128)(2,1)}, u32[]{:S(2)}) copy-start(bf16[512,2048]{1,0:T(8,128)(2,1)} %get-tuple-element.70.wout_ref) | copy-start | bytes 6291460
  268.6 6.4 %copy-start.27 = (bf16[1024,512]{1,0:T(8,128)(2,1)S(1)}, bf16[1024,512]{1,0:T(8,128)(2,1)}, u32[]{:S(2)}) copy-start(bf16[1024,512]{1,0:T(8,128)(2,1)} %get-tuple-element.76) | copy-start | bytes 3145732
  275.0 4.4 %copy-start.6 = (bf16[1024,2048]{1,0:T(8,128)(2,1)S(1)}, bf16[1024,2048]{1,0:T(8,128)(2,1)}, u32[]{:S(2)}) copy-start(bf16[1024,2048]{1,0:T(8,128)(2,1)} %get-tuple-element.69.ups_ref) | copy-start | bytes 12582916
  398.0 2.6 copy-start.5
  398.0 2.7 copy-start.7
  398.0 2.7 copy-start.23
  400.5 17.5 %copy-start.11 = (bf16[1,128,2048]{2,1,0:T(8,128)(2,1)S(1)}, bf16[1,128,2048]{2,1,0:T(8,128)(2,1)}, u32[]{:S(2)}) copy-start(bf16[1,128,2048]{2,1,0:T(8,128)(2,1)} %up_ref.1) | copy-start | bytes 1572868
  400.5 17.5 %copy-start.16 = (f32[128,2048]{1,0:T(8,128)S(1)}, f32[128,2048]{1,0:T(8,128)}, u32[]{:S(2)}) copy-start(f32[128,2048]{1,0:T(8,128)} %get-tuple-element.81) | copy-start | bytes 3145732
  (5 other events, 5.6 us)

commit v4 on v3

--- a/solution.py
+++ b/solution.py
@@ -226,119 +226,10 @@
 PIECES = 4
 
 
-def total_kernel(part_ref, out_ref, sib_ref, base_ref, left_ref, right_ref, tor_ref, tol_ref, ss, sr, ls, lr, rs, rr, os_, or_):
-    d, c, z = place()
-    sib = (d, flip(c, 1), z)
-    left = (d, c, lax.rem(z + 3, 4))
-    right = (d, c, lax.rem(z + 1, 4))
-    rows = part_ref.shape[0] // 2
-    piece = rows // PIECES
-    mine, theirs = c * rows, flip(c, 1) * rows
-    barrier = pltpu.get_barrier_semaphore()
-    pl.semaphore_signal(barrier, inc=1, device_id=sib, device_id_type=MESH)
-    pl.semaphore_signal(barrier, inc=1, device_id=left, device_id_type=MESH)
-    pl.semaphore_signal(barrier, inc=1, device_id=right, device_id_type=MESH)
-    pl.semaphore_wait(barrier, 3)
-
-    def cut(p):
-        return pl.ds(p * piece, piece)
-
-    def far(base, p):
-        return pl.ds(pl.multiple_of(base + p * piece, 8), piece)
-
-    for p in range(PIECES):
-        put(part_ref.at[far(theirs, p)], sib_ref.at[cut(p)], ss.at[p], sr.at[p], sib)
-    for p in range(PIECES):
-        landed(sib_ref.at[cut(p)], sr.at[p], sib)
-        base_ref[cut(p), :] = part_ref[far(mine, p), :] + sib_ref[cut(p), :]
-
-        @pl.when(z == 0)
-        def _():
-            put(base_ref.at[cut(p)], left_ref.at[cut(p)], rs.at[p], lr.at[p], right)
-
-        @pl.when(z == 3)
-        def _():
-            put(base_ref.at[cut(p)], right_ref.at[cut(p)], ls.at[p], rr.at[p], left)
-
-    def from_left(p):
-        landed(left_ref.at[cut(p)], lr.at[p], left)
-
-        @pl.when(z < 3)
-        def _():
-            tor_ref[cut(p), :] = base_ref[cut(p), :] + left_ref[cut(p), :]
-            put(tor_ref.at[cut(p)], left_ref.at[cut(p)], rs.at[p], lr.at[p], right)
-
-    def from_right(p):
-        landed(right_ref.at[cut(p)], rr.at[p], right)
-
-        @pl.when(z > 0)
-        def _():
-            tol_ref[cut(p), :] = base_ref[cut(p), :] + right_ref[cut(p), :]
-            put(tol_ref.at[cut(p)], right_ref.at[cut(p)], ls.at[p], rr.at[p], left)
-
-    def finish(p):
-        value = base_ref[cut(p), :]
-        out_ref[far(mine, p), :] = value
-
-        @pl.when(z > 0)
-        def _():
-            out_ref[far(mine, p), :] += left_ref[cut(p), :]
-
-        @pl.when(z < 3)
-        def _():
-            out_ref[far(mine, p), :] += right_ref[cut(p), :]
-
-        put(out_ref.at[far(mine, p)], out_ref.at[far(mine, p)], os_.at[p], or_.at[p], sib)
-
-    @pl.when(z == 1)
-    def _():
-        for p in range(PIECES):
-            from_left(p)
-
-    @pl.when(z < 3)
-    def _():
-        for p in range(PIECES):
-            from_right(p)
-
-    @pl.when(z >= 2)
-    def _():
-        for p in range(PIECES):
-            from_left(p)
-
-    for p in range(PIECES):
-        finish(p)
-    for p in range(PIECES):
-        landed(out_ref.at[far(theirs, p)], or_.at[p], sib)
-        sent(out_ref.at[far(mine, p)], os_.at[p], sib)
-        sent(part_ref.at[far(theirs, p)], ss.at[p], sib)
-
-        @pl.when(z < 3)
-        def _():
-            sent(base_ref.at[cut(p)], rs.at[p], right)
-
-        @pl.when(z > 0)
-        def _():
-            sent(base_ref.at[cut(p)], ls.at[p], left)
-
-
-def group_total(part, which):
-    rows = part.shape[0] // 2
-    dma = lambda: pltpu.SemaphoreType.DMA((PIECES,))
-    here = pl.BlockSpec(memory_space=pltpu.VMEM)
-    return pl.pallas_call(
-        total_kernel,
-        out_shape=jax.ShapeDtypeStruct(part.shape, f32),
-        in_specs=[here],
-        out_specs=here,
-        scratch_shapes=[pltpu.VMEM((rows, 128), f32)] * 6 + [dma() for _ in range(8)],
-        compiler_params=pltpu.CompilerParams(collective_id=which, has_side_effects=True, vmem_limit_bytes=16 * 1024 * 1024),
-    )(part)
-
-
 def k1_kernel(tok_ref, up_ref, cols_ref, wout_ref, small_ref, meta_ref,
-              xn_out, ups_ref, win_out, wouts_ref, smalls_ref, vecs_ref, gains_ref, masks_ref,
-              u_ref, g_ref, v_ref, slope_ref, dl_ref, kq_ref,
-              xs_ref, xn_ref, win_ref, metas_ref, part_ref, out_ref, sib_ref, base_ref, left_ref, right_ref, tor_ref, tol_ref,
+              xnt_out, ups_ref, win_out, wouts_ref, smalls_ref, vecs_ref, gains_ref, masks_ref, live_ref,
+              u_ref, g_ref, v_ref, vt_ref, slope_ref, dl_ref, kq_ref,
+              xs_ref, xn_ref, xnt_ref, win_ref, metas_ref, part_ref, out_ref, sib_ref, base_ref, left_ref, right_ref, tor_ref, tol_ref,
               own_sem, ms, mr, qs, qr, xls, xlr, xrs, xrr, xcs, xcr, as_, ar, ps, pr, rs, rr, ws, wr, ts, tr, tls, tlr, trs, trr, tos, tor):
     d, c, z = place()
     j = c * 4 + z
@@ -496,10 +387,11 @@
         for o in range(1, 4):
             same = jnp.where(segment(here - o) == now, 1.0, 0.0)
             masks_ref[o - 1, r, :] = jnp.where(here >= o, same, 0.0)
-        masks_ref[3, r, :] = jnp.where(now < DOCS, 1.0, 0.0)
+        live_ref[0, r, :] = jnp.where(now < DOCS, 1.0, 0.0)
         return carry
 
     lax.fori_loop(0, length, mask_step, 0)
+    masks_ref[:, count:, :] = jnp.zeros((3, masks_ref.shape[1] - count, 128), f32)
     lane = lax.broadcasted_iota(jnp.int32, (1, 128), 1)
     for group in range(4):
         for pair in range(4):
@@ -516,6 +408,13 @@
             return carry
 
         lax.fori_loop(0, length // 16, body, 0)
+
+        def turn(i, carry):
+            part = pl.ds(pl.multiple_of(i * 256, 256), 256)
+            xnt_ref[part, rows(rank)] = xn_ref[rows(rank), part].T
+            return carry
+
+        lax.fori_loop(0, model // 256, turn, 0)
 
     for i in range(1, 7):
         pass_on(i)
@@ -542,7 +441,7 @@
             landed(slot, rr.at[k // 2], yn)
         else:
             landed(slot, rr.at[4 + k // 2], xn)
-    own += [pltpu.make_async_copy(xn_ref, xn_out, own_sem.at[6]), pltpu.make_async_copy(win_ref, win_out, own_sem.at[7])]
+    own += [pltpu.make_async_copy(xnt_ref, xnt_out, own_sem.at[6]), pltpu.make_async_copy(win_ref, win_out, own_sem.at[7])]
     own[6].start()
     own[7].start()
     row_hop(ups_ref, 4, 0)
@@ -605,6 +504,14 @@
         spread(g_ref, 0, width)
         row_hop(ups_ref, 4, 1)
 
+        def turn(i, carry):
+            r = pl.ds(pl.multiple_of(i * 128, 128), 128)
+            for n in range(tiles):
+                vt_ref[n * 128:(n + 1) * 128, r] = v_ref[n, r, :].T.astype(bf16)
+            return carry
+
+        lax.fori_loop(0, count // 128, turn, 0)
+
     line_total(part_ref, out_ref, sib_ref, base_ref, left_ref, right_ref, tor_ref, tol_ref, ts, tr, tls, tlr, trs, trr, tos, tor, between)
     dl_ref[...] = out_ref[0:count, :].astype(bf16)
     for b in range(4):
@@ -624,7 +531,7 @@
         copy.wait_send()
 
 
-def line_total(part_ref, out_ref, sib_ref, base_ref, left_ref, right_ref, tor_ref, tol_ref, ss, sr, ls, lr, rs, rr, os_, or_, between):
+def line_total(part_ref, out_ref, sib_ref, base_ref, left_ref, right_ref, tor_ref, tol_ref, ss, sr, ls, lr, rs, rr, os_, or_, between, early=None):
     d, c, z = place()
     sib = (d, flip(c, 1), z)
     left = (d, c, lax.rem(z + 3, 4))
@@ -652,6 +559,9 @@
         @pl.when(z == 3)
         def _():
             put(base_ref.at[cut(p)], right_ref.at[cut(p)], ls.at[p], rr.at[p], left)
+
+    if early is not None:
+        early()
 
     def from_left(p):
         landed(left_ref.at[cut(p)], lr.at[p], left)
@@ -732,26 +642,29 @@
     return pl.pallas_call(
         k1_kernel,
         out_shape=(
-            like((count, model), bf16),
+            like((model, count), bf16),
             like((count, model), bf16),
             like((groups * ways * cols.shape[1], cols.shape[2]), bf16),
             like((channels, model), bf16),
             like((channels, small.shape[1]), bf16),
             like((8, channels), f32),
             like((1, model), f32),
-            like((4, count, 128), f32),
+            like((3, count + 32, 128), f32),
+            like((1, count, 128), f32),
             like((channels // 128, count + 24, 128), f32),
             like((channels // 128, count, 128), f32),
             like((channels // 128, count, 128), f32),
+            like((channels, count), bf16),
             like((channels // 128, count, 128), f32),
             like((count, 128), bf16),
             like((count, 128), f32),
         ),
         in_specs=[some] * 6,
-        out_specs=(far,) * 4 + (here,) * 10,
+        out_specs=(far,) * 4 + (here,) * 12,
         scratch_shapes=[
             pltpu.VMEM((count, model), bf16),
             pltpu.VMEM((count, model), bf16),
+            pltpu.VMEM((model, count), bf16),
             pltpu.VMEM((groups * ways * cols.shape[1], cols.shape[2]), bf16),
             pltpu.VMEM((groups, ways) + meta.shape, f32),
             pltpu.VMEM((packed, 128), f32),
@@ -767,8 +680,8 @@
 
 
 def k2_kernel(states, dl_ref, kq_ref, wdt_ref, vecs_ref, keep_ref, live_ref, v_ref, g_ref, ups_ref, wout_ref,
-              m_ref, dg_ref, dpre_ref, dv_ref, part_ref, stat_ref,
-              s_ref, h_ref, rate_ref, w_ref, y_ref, dm_ref, kb_ref, hot_ref, drr_ref):
+              m_ref, mt_ref, dg_ref, gwdt_ref, dv_ref, part_ref, stat_ref,
+              dpre_ref, s_ref, h_ref, rate_ref, w_ref, y_ref, dm_ref, kb_ref, hot_ref, drr_ref):
     tiles, count = v_ref.shape[:2]
     steps = count // 8
     wide = states * 128
@@ -965,11 +878,14 @@
     def by_row(j, carry):
         r = pl.ds(pl.multiple_of(j * length, length), length)
         for n in both:
-            m_ref[r, n * 128:(n + 1) * 128] = y_ref[n, pl.ds(j, length, stride=8), :].astype(bf16)
+            value = y_ref[n, pl.ds(j, length, stride=8), :]
+            m_ref[r, n * 128:(n + 1) * 128] = value.astype(bf16)
+            mt_ref[n * 128:(n + 1) * 128, r] = value.T.astype(bf16)
             dg_ref[r, n * 128:(n + 1) * 128] = dm_ref[n, pl.ds(j, length, stride=8), :].astype(bf16)
         return carry
 
     lax.fori_loop(0, 8, by_row, 0)
+    gwdt_ref[...] = lax.dot_general(dpre_ref[...], dl_ref[...], (((0,), (0,)), ((), ())), preferred_element_type=f32)
     stat_ref[...] = jnp.zeros_like(stat_ref)
     for n in both:
         lanes = slice(n * 128, (n + 1) * 128)
@@ -979,7 +895,7 @@
         stat_ref[6:7, lanes] = jnp.sum(tile_of(dskip, n), axis=0, keepdims=True)
 
 
-def k2(dl, kq, smalls, vecs, masks, v, g, ups, wout, states):
+def k2(dl, kq, smalls, vecs, masks, live, v, g, ups, wout, states):
     count, rank = dl.shape
     channels, model = wout.shape
     tiles = 2
@@ -994,8 +910,9 @@
         grid=(channels // width,),
         out_shape=(
             like((count, channels), bf16),
+            like((channels, count), bf16),
             like((count, channels), bf16),
-            like((count, channels), bf16),
+            like((channels, rank), f32),
             like(v.shape, f32),
             like((count + count // 4, 128), f32),
             like((8, channels), f32),
@@ -1005,38 +922,24 @@
             pl.BlockSpec((width, 128), lambda h: (h, 2)),
             pl.BlockSpec((8, width), lambda h: (0, h)),
             pl.BlockSpec((1, count, 128), lambda h: (0, 0, 0), pipeline_mode=once),
-            pl.BlockSpec((1, count, 128), lambda h: (3, 0, 0), pipeline_mode=once),
+            pl.BlockSpec((1, count, 128), lambda h: (0, 0, 0), pipeline_mode=once),
             deep, deep, whole(ups),
             pl.BlockSpec((width, model), lambda h: (h, 0)),
         ],
-        out_specs=(flat, flat, flat, deep, pl.BlockSpec((count + count // 4, 128), lambda h: (0, 0)), pl.BlockSpec((8, width), lambda h: (0, h))),
+        out_specs=(flat, pl.BlockSpec((width, count), lambda h: (h, 0)), flat, pl.BlockSpec((width, rank), lambda h: (h, 0)), deep, pl.BlockSpec((count + count // 4, 128), lambda h: (0, 0)), pl.BlockSpec((8, width), lambda h: (0, h))),
         scratch_shapes=[
+            pltpu.VMEM((count, width), bf16),
             pltpu.VMEM((count // 8 // GROUP + 1, GROUP, states, 8, width), f32),
             pltpu.VMEM((states, 8, width), f32),
         ] + [pltpu.VMEM((tiles, count, 128), f32)] * 4
         + [pltpu.VMEM((count, 2 * states * 128), f32), pltpu.VMEM((128, 2 * states * 128), bf16), pltpu.VMEM((count, 128), f32)],
         compiler_params=pltpu.CompilerParams(vmem_limit_bytes=60 * 1024 * 1024),
-    )(dl, kq, smalls, vecs, masks, masks, v, g, ups, wout)
-
-
-def add_rows(dst, sources):
-    rows = dst.shape[0]
-    step = 16
-
-    def body(i, carry):
-        r = pl.ds(pl.multiple_of(i * step, step), step)
-        value = sources[0][r, :].astype(f32)
-        for more in sources[1:]:
-            value = value + more[r, :].astype(f32)
-        dst[r, :] = value.astype(dst.dtype)
-        return carry
-
-    lax.fori_loop(0, rows // step, body, 0)
-
-
-class Line:
-    def __init__(self, part, out, sib, send, left, right, sems):
-        self.part, self.out, self.sib, self.send, self.left, self.right = part, out, sib, send, left, right
+    )(dl, kq, smalls, vecs, masks, live, v, g, ups, wout)
+
+
+class Row:
+    def __init__(self, part, sib, recv, sems):
+        self.part, self.sib, self.recv = part, sib, recv
         self.ss, self.sr, self.gs, self.lr, self.rr = sems
         d, c, z = place()
         self.c = c
@@ -1048,223 +951,430 @@
         for zp in (3, 0, 2, 1):
             put(self.part.at[flip(self.c, 1), zp], self.sib.at[zp], self.ss.at[zp], self.sr.at[zp], self.other)
 
+    def terms(self, zs, zp):
+        landed(self.sib.at[zp], self.sr.at[zp], self.other)
+        found = [self.sib.at[zp], self.part.at[self.c, zp]]
+        if zp >= zs and zs > 0:
+            landed(self.recv.at[zp], self.lr.at[zp], self.to_left)
+            found.append(self.recv.at[zp])
+        if zp <= zs and zs < 3:
+            slot = self.recv.at[4 if zp == zs else zp]
+            landed(slot, self.rr.at[zp], self.to_right)
+            found.append(slot)
+        return found
+
     def step(self, zs, k):
         for zp in range(4):
             if zp > zs and k == 3 - zp + zs:
-                landed(self.sib.at[zp], self.sr.at[zp], self.other)
-                terms = [self.part.at[self.c, zp], self.sib.at[zp]]
-                if zs > 0:
-                    landed(self.left.at[zp], self.lr.at[zp], self.to_left)
-                    terms.append(self.left.at[zp])
-                add_rows(self.send.at[zp], terms)
-                put(self.send.at[zp], self.left.at[zp], self.gs.at[zp], self.lr.at[zp], self.to_right)
+                add_rows(self.sib.at[zp], self.terms(zs, zp))
+                put(self.sib.at[zp], self.recv.at[zp], self.gs.at[zp], self.lr.at[zp], self.to_right)
             if zp < zs and k == zp + 3 - zs:
-                landed(self.sib.at[zp], self.sr.at[zp], self.other)
-                terms = [self.part.at[self.c, zp], self.sib.at[zp]]
-                if zs < 3:
-                    landed(self.right.at[zp], self.rr.at[zp], self.to_right)
-                    terms.append(self.right.at[zp])
-                add_rows(self.send.at[zp], terms)
-                put(self.send.at[zp], self.right.at[zp], self.gs.at[zp], self.rr.at[zp], self.to_left)
+                add_rows(self.sib.at[zp], self.terms(zs, zp))
+                put(self.sib.at[zp], self.recv.at[4 if zp == zs - 1 else zp], self.gs.at[zp], self.rr.at[zp], self.to_left)
 
     def finish(self, zs):
-        landed(self.sib.at[zs], self.sr.at[zs], self.other)
-        terms = [self.part.at[self.c, zs], self.sib.at[zs]]
-        if zs > 0:
-            landed(self.left.at[zs], self.lr.at[zs], self.to_left)
-            terms.append(self.left.at[zs])
-        if zs < 3:
-            landed(self.right.at[zs], self.rr.at[zs], self.to_right)
-            terms.append(self.right.at[zs])
-        add_rows(self.out, terms)
+        add_rows(self.sib.at[zs], self.terms(zs, zs), self.total)
 
     def close(self, zs):
         for zp in range(4):
             sent(self.sib.at[zp], self.ss.at[zp], self.other)
             if zp != zs:
-                sent(self.send.at[zp], self.gs.at[zp], self.other)
-
-
-class Plane:
-    def __init__(self, part, out, xa, yb, sx, sy, rx, ry, sems):
-        self.part, self.out, self.xa, self.yb, self.sx, self.sy, self.rx, self.ry = part, out, xa, yb, sx, sy, rx, ry
-        self.ss, self.rs = sems
+                sent(self.sib.at[zp], self.gs.at[zp], self.other)
+
+    def along(self, k, total=None):
+        self.total = total
+        d, c, z = place()
+        for zs in range(4):
+            @pl.when(z == zs)
+            def _():
+                if k < 3:
+                    self.step(zs, k)
+                else:
+                    self.finish(zs)
+                    self.close(zs)
+
+
+def row_scratch(rows, columns):
+    return [pltpu.VMEM((4, rows, columns), bf16), pltpu.VMEM((5, rows, columns), bf16)] + [pltpu.SemaphoreType.DMA((4,))] * 5
+
+
+def add_rows(dst, sources, total=None):
+    rows = (total if total is not None else dst).shape[0]
+    step = 16
+
+    def body(i, carry):
+        r = pl.ds(pl.multiple_of(i * step, step), step)
+        value = sources[0][r, :].astype(f32)
+        for more in sources[1:]:
+            value = value + more[r, :].astype(f32)
+        if total is not None:
+            total[r, :] = value
+        else:
+            dst[r, :] = value.astype(dst.dtype)
+        return carry
+
+    lax.fori_loop(0, rows // step, body, 0)
+
+
+class Flat:
+    def __init__(self, part, xa, yb, rx, ry, ss, rs):
+        self.part, self.xa, self.yb, self.rx, self.ry, self.ss, self.rs = part, xa, yb, rx, ry, ss, rs
         d, c, z = place()
         self.d, self.dx, self.dy, self.dd = d, flip(d, 1), flip(d, 2), flip(flip(d, 1), 2)
         self.xn, self.yn = (self.dx, c, z), (self.dy, c, z)
         half = part.shape[1] // 2
         self.a, self.b = pl.ds(0, half), pl.ds(half, half)
-
-    def start(self):
+        self.sends = []
+
+    def start_far(self):
         p = self.part
-        self.sends = [
-            put(p.at[self.dd, self.a], self.xa, self.ss.at[0], self.rs.at[0], self.xn),
-            put(p.at[self.dd, self.b], self.yb, self.ss.at[1], self.rs.at[1], self.yn),
-            put(p.at[self.dx, self.a], self.rx.at[self.a], self.ss.at[2], self.rs.at[2], self.xn),
-            put(p.at[self.dy, self.b], self.ry.at[self.b], self.ss.at[3], self.rs.at[3], self.yn),
-        ]
+        self.sends.append(put(p.at[self.dd, self.a], self.xa, self.ss.at[0], self.rs.at[0], self.xn))
+        self.sends.append(put(p.at[self.dd, self.b], self.yb, self.ss.at[1], self.rs.at[1], self.yn))
+
+    def start_near(self):
+        p = self.part
+        self.sends.append(put(p.at[self.dx, self.a], self.rx.at[self.a], self.ss.at[2], self.rs.at[2], self.xn))
+        self.sends.append(put(p.at[self.dy, self.b], self.ry.at[self.b], self.ss.at[3], self.rs.at[3], self.yn))
 
     def middle(self):
         p = self.part
         landed(self.xa, self.rs.at[0], self.xn)
-        add_rows(self.sy, [p.at[self.dy, self.a], self.xa])
-        self.sends.append(put(self.sy, self.ry.at[self.a], self.ss.at[4], self.rs.at[4], self.yn))
+        add_rows(self.xa, [self.xa, p.at[self.dy, self.a]])
+        self.sends.append(put(self.xa, self.ry.at[self.a], self.ss.at[4], self.rs.at[4], self.yn))
         landed(self.yb, self.rs.at[1], self.yn)
-        add_rows(self.sx, [p.at[self.dx, self.b], self.yb])
-        self.sends.append(put(self.sx, self.rx.at[self.b], self.ss.at[5], self.rs.at[5], self.xn))
-
-    def finish(self):
+        add_rows(self.yb, [self.yb, p.at[self.dx, self.b]])
+        self.sends.append(put(self.yb, self.rx.at[self.b], self.ss.at[5], self.rs.at[5], self.xn))
+
+    def finish(self, out):
         landed(self.rx.at[self.a], self.rs.at[2], self.xn)
         landed(self.ry.at[self.b], self.rs.at[3], self.yn)
         landed(self.ry.at[self.a], self.rs.at[4], self.yn)
         landed(self.rx.at[self.b], self.rs.at[5], self.xn)
-        add_rows(self.out, [self.part.at[self.d], self.rx, self.ry])
+        add_rows(out, [self.part.at[self.d], self.rx, self.ry])
 
     def close(self):
         for copy in self.sends:
             copy.wait_send()
 
 
-def plane_scratch(rows, columns, dtype):
+def flat_scratch(rows, columns, dtype):
     half = pltpu.VMEM((rows // 2, columns), dtype)
     full = pltpu.VMEM((rows, columns), dtype)
-    return [half, half, half, half, full, full, pltpu.SemaphoreType.DMA((6,)), pltpu.SemaphoreType.DMA((6,))]
-
-
-def line_scratch(rows, columns, dtype):
-    four = pltpu.VMEM((4, rows, columns), dtype)
-    return [four] * 4 + [pltpu.SemaphoreType.DMA((4,))] * 5
-
-
-def back_kernel(dxn_ref, outp_ref, gwin_ref, gwout_ref, small_ref,
-                dxns_ref, outs_ref, gwins_ref, gwouts_ref, smalls_ref, *scratch):
-    lines = [Line(dxn_ref, dxns_ref, *scratch[0:4], scratch[4:9]), Line(outp_ref, outs_ref, *scratch[9:13], scratch[13:18])]
-    scratch = scratch[18:]
-    fin, own, as_, ar = scratch[:4]
-    scratch = scratch[4:]
-    planes = []
-    for part, out in ((gwin_ref, fin), (gwout_ref, gwouts_ref), (small_ref, smalls_ref)):
-        planes.append(Plane(part, out, *scratch[:6], scratch[6:8]))
-        scratch = scratch[8:]
+    return [half, half, full, full, pltpu.SemaphoreType.DMA((6,)), pltpu.SemaphoreType.DMA((6,))]
+
+
+def k3_kernel(part_ref, stat_ref, smalls_ref, vecs_ref, gains_ref, gwdt_ref, masks_ref, tok_ref, up_ref,
+              m_any, mt_any, dg_any, dv_any, slope_any, u_any, vt_any, xnt_any, win_any, wout_any, ups_any,
+              block_ref, gtok_ref, gwin_ref, gwout_ref, small_ref, tiny_ref, *scratch):
+    scratch = list(scratch)
+
+    def take(n):
+        found = scratch[:n]
+        del scratch[:n]
+        return found
+
+    outp, dxnp, gwinp, gwoutp, smallp = take(5)
+    m_ref, mt_ref, dz_ref, dc_ref, slope_ref, u_ref, xnt_ref, dp_ref, slots_ref, row_ref = take(10)
+    near_ref, pairs_ref, sum_ref, far_ref = take(4)
+    loads, as_, ar, ns, nr, fs, fr = take(7)
+    totals = take(7)
+    total_sems = take(8)
+    out_row = Row(outp, *take(2), take(5))
+    dxn_row = Row(dxnp, *take(2), take(5))
+    gwin_flat = Flat(gwinp, *take(6))
+    gwout_flat = Flat(gwoutp, *take(6))
+    small_flat = Flat(smallp, *take(6))
     d, c, z = place()
     j = c * 4 + z
+    other = flip(c, 1)
     steps = mates()
-    greet([mate(s) for s in steps] + [planes[0].xn, planes[0].yn])
-    lines[0].start()
-    planes[0].start()
-    lines[1].start()
-
-    def along(line, k):
-        for zs in range(4):
-            @pl.when(z == zs)
-            def _():
-                if k < 3:
-                    line.step(zs, k)
-                else:
-                    line.finish(zs)
-                    line.close(zs)
-
-    along(lines[0], 0)
-    along(lines[1], 0)
-    planes[1].start()
-    planes[2].start()
-    along(lines[0], 1)
-    planes[0].middle()
-    along(lines[0], 2)
-    planes[0].finish()
-    block = fin.shape[0] // 8
+    planes = [(flip(d, 1), c, z), (flip(d, 2), c, z), (flip(flip(d, 1), 2), c, z)]
+    length, model = tok_ref.shape[1:]
+    tiles, padded, _ = dc_ref.shape
+    count = dz_ref.shape[0]
+    width = tiles * 128
+    rows_any = [(m_any, m_ref), (wout_any, gwoutp), (ups_any, dxnp), (mt_any, mt_ref), (dv_any, dc_ref.at[:, pl.ds(0, count)]),
+                (slope_any, slope_ref), (u_any, u_ref), (dg_any, dz_ref.at[:, pl.ds(width, width)]), (xnt_any, xnt_ref), (win_any, gwinp)]
+    copies = [pltpu.make_async_copy(a, b, loads.at[i]) for i, (a, b) in enumerate(rows_any)]
+    for copy in copies:
+        copy.start()
+    greet([mate(s) for s in steps] + planes)
+    tile = 256
+    nn = (((1,), (0,)), ((), ()))
+    nt = (((1,), (1,)), ((), ()))
+
+    def rows_product(half, target, left, right, dims, right_rows):
+        def body(i, carry):
+            if right_rows:
+                group = i // (512 // tile)
+                value = right[group, pl.ds(pl.multiple_of((i % (512 // tile)) * tile, tile), tile), :]
+            else:
+                value = jnp.concatenate([right[g, :, pl.ds(pl.multiple_of(i * tile, tile), tile)] for g in range(4)], axis=0)
+            product = lax.dot_general(left[pl.ds(pl.multiple_of(half * 512, 512), 512), :], value, dims, preferred_element_type=f32)
+            for zp in range(4):
+                target[half, zp, :, pl.ds(pl.multiple_of(i * tile, tile), tile)] = product[zp * length:(zp + 1) * length].astype(bf16)
+            return carry
+
+        lax.fori_loop(0, model // tile, body, 0)
+
+    def early():
+        copies[0].wait()
+        copies[1].wait()
+        rows_product(other, outp, m_ref, gwoutp, nn, False)
+        out_row.start()
+        rows_product(c, outp, m_ref, gwoutp, nn, False)
+
+    def between():
+        out_row.along(0)
+        copies[2].wait()
+        copies[3].wait()
+
+        def body(i, carry):
+            lanes = pl.ds(pl.multiple_of(i * tile, tile), tile)
+            value = dxnp[:, :, :, lanes].reshape(count, tile)
+            product = jnp.dot(mt_ref[...], value, preferred_element_type=f32)
+            for g in range(4):
+                gwoutp[g, :, lanes] = product[g * 128:(g + 1) * 128].astype(bf16)
+            return carry
+
+        lax.fori_loop(0, model // tile, body, 0)
+        gwout_flat.start_far()
+        gwout_flat.start_near()
+
+    total_ref = totals[0]
+    line_total(part_ref, *totals, *total_sems, between, early)
+    vt_copy = pltpu.make_async_copy(vt_any, mt_ref, loads.at[10])
+    vt_copy.start()
+    quarter = count // 4
+    lane = lax.broadcasted_iota(jnp.int32, (quarter, 128), 1)
+    dp_ref[:, 0:128] = total_ref[0:count, :].astype(bf16)
+    for b in range(4):
+        packed = total_ref[count:count + quarter, :]
+        packed = pltpu.roll(packed, 128 - 32 * b, 1) if b else packed
+        dp_ref[b * quarter:(b + 1) * quarter, 128:256] = jnp.where(lane < 32, packed, 0.0).astype(bf16)
+    copies[4].wait()
+    copies[5].wait()
+    dc_ref[:, count:, :] = jnp.zeros((tiles, padded - count, 128), f32)
+
+    def slope_step(i, carry):
+        r = pl.ds(pl.multiple_of(i * 256, 256), 256)
+        product = lax.dot_general(dp_ref[r, :], smalls_ref[:, 0:256], nt, preferred_element_type=f32)
+        for n in range(tiles):
+            dc_ref[n, r, :] = (dc_ref[n, r, :] + product[:, n * 128:(n + 1) * 128]) * slope_ref[n, r, :]
+        return carry
+
+    lax.fori_loop(0, count // 256, slope_step, 0)
+    copies[6].wait()
+    taps = [vecs_ref[o:o + 1, :] for o in range(4)]
+    lead = u_ref.shape[1] - count
+
+    for n in range(tiles):
+        lanes = slice(n * 128, (n + 1) * 128)
+        tap = [t[:, lanes] for t in taps]
+
+        def conv_step(i, carry):
+            r = pl.ds(pl.multiple_of(i * 32, 32), 32)
+            sums = list(carry)
+            dc = dc_ref[n, r, :]
+            du = tap[3] * dc
+            fold8 = lambda x: x[0:8] + x[8:16] + x[16:24] + x[24:32]
+            sums[4] = sums[4] + fold8(dc)
+            sums[3] = sums[3] + fold8(dc * u_ref[n, pl.ds(pl.multiple_of(lead + i * 32, 8), 32), :])
+            for o in range(1, 4):
+                sums[3 - o] = sums[3 - o] + fold8(dc * (u_ref[n, pl.ds(pl.multiple_of(lead + i * 32 - 8 * o, 8), 32), :] * masks_ref[o - 1, pl.ds(pl.multiple_of(i * 32, 8), 32), :]))
+                du = du + tap[3 - o] * (dc_ref[n, pl.ds(pl.multiple_of(i * 32 + 8 * o, 8), 32), :] * masks_ref[o - 1, pl.ds(pl.multiple_of(i * 32 + 8 * o, 8), 32), :])
+            dc_ref[n, r, :] = du
+            return tuple(sums)
+
+        sums = lax.fori_loop(0, count // 32, conv_step, (jnp.zeros((8, 128), f32),) * 5)
+        smallp[n, 128:160, :] = jnp.zeros((32, 384), f32)
+        for k in range(5):
+            smallp[n, 128 + k:129 + k, 0:128] = jnp.sum(sums[k], axis=0, keepdims=True)
+        smallp[n, 133:134, 0:128] = stat_ref[5:6, lanes]
+        smallp[n, 134:135, 0:128] = stat_ref[6:7, lanes]
+        smallp[n, 0:128, 256:384] = gwdt_ref[n * 128:(n + 1) * 128, :]
+
+    copies[7].wait()
+
+    def by_row(i, carry):
+        r = pl.ds(pl.multiple_of(i * length, length), length)
+        for n in range(tiles):
+            dz_ref[r, n * 128:(n + 1) * 128] = dc_ref[n, pl.ds(i, length, stride=8), :].astype(bf16)
+        return carry
+
+    lax.fori_loop(0, 8, by_row, 0)
+    copies[9].wait()
+    rows_product(other, dxnp, dz_ref, gwinp, nt, True)
+    dxn_row.start()
+    rows_product(c, dxnp, dz_ref, gwinp, nt, True)
+    out_row.along(1)
+    copies[8].wait()
+
+    def weight_rows(group):
+        def body(i, carry):
+            lanes = pl.ds(pl.multiple_of(i * tile, tile), tile)
+            left = xnt_ref[pl.ds(pl.multiple_of(group * 512, 512), 512), :]
+            gwinp[group, :, lanes] = jnp.dot(left, dz_ref[:, lanes], preferred_element_type=f32).astype(bf16)
+            return carry
+
+        lax.fori_loop(0, 2 * width // tile, body, 0)
+
+    weight_rows(gwin_flat.dd)
+    gwin_flat.start_far()
+    weight_rows(gwin_flat.dx)
+    weight_rows(gwin_flat.dy)
+    gwin_flat.start_near()
+    out_row.along(2)
+    dxn_row.along(0)
+    weight_rows(d)
+    gwout_flat.middle()
+    vt_copy.wait()
+    for n in range(tiles):
+        smallp[n, 0:128, 0:256] = jnp.dot(mt_ref[n * 128:(n + 1) * 128, :], dp_ref[...], preferred_element_type=f32)
+    small_flat.start_far()
+    small_flat.start_near()
+    out_row.along(3, row_ref)
+
+    def block_step(i, carry):
+        r = pl.ds(pl.multiple_of(i * 16, 16), 16)
+        block_ref[r, :] = (tok_ref[0, r, :].astype(f32) + row_ref[r, :]).astype(bf16)
+        return carry
+
+    lax.fori_loop(0, length // 16, block_step, 0)
+    gwin_flat.middle()
+    dxn_row.along(1)
+    gwout_flat.finish(gwout_ref)
+    dxn_row.along(2)
+    small_flat.middle()
+    block = gwin_ref.shape[0]
+    fin = gwinp.at[d]
+    gwin_flat.finish(fin)
+
     def rows_of(rank):
-        return fin.at[pl.ds(pl.multiple_of(rank * block, 16), block)]
-    keep = pltpu.make_async_copy(rows_of(j), gwins_ref.at[j], own)
-    keep.start()
+        return gwinp.at[d, pl.ds(pl.multiple_of(rank * block, block), block)]
+
     pending = []
     for i, s in enumerate(steps):
         to = mate(s)
-        pending.append(put(rows_of(rank_of(to)), gwins_ref.at[j], as_.at[i], ar.at[i], to))
-    along(lines[0], 3)
-    planes[1].middle()
-    planes[2].middle()
-    along(lines[1], 1)
-    planes[1].finish()
-    planes[2].finish()
-    along(lines[1], 2)
-    for i, s in enumerate(steps):
-        src = mate(s, -1)
-        landed(gwins_ref.at[rank_of(src)], ar.at[i], src)
-    along(lines[1], 3)
-    keep.wait()
-    for copy in pending:
-        copy.wait_send()
-    for plane in planes:
-        plane.close()
-
-
-def back(dxn, outp, gwin, gwout, small):
-    like = jax.ShapeDtypeStruct
-    here = pl.BlockSpec(memory_space=pltpu.VMEM)
-    rows, columns = dxn.shape[2:]
-    return pl.pallas_call(
-        back_kernel,
-        out_shape=(
-            like((rows, columns), f32),
-            like((rows, columns), f32),
-            like((8, gwin.shape[1] // 8, gwin.shape[2]), bf16),
-            like(gwout.shape[1:], f32),
-            like(small.shape[1:], f32),
-        ),
-        in_specs=[here] * 5,
-        out_specs=(here,) * 5,
-        scratch_shapes=line_scratch(rows, columns, bf16) + line_scratch(rows, columns, bf16)
-        + [pltpu.VMEM(gwin.shape[1:], bf16), pltpu.SemaphoreType.DMA(()), pltpu.SemaphoreType.DMA((7,)), pltpu.SemaphoreType.DMA((7,))]
-        + plane_scratch(*gwin.shape[1:], bf16) + plane_scratch(*gwout.shape[1:], bf16) + plane_scratch(*small.shape[1:], f32),
-        compiler_params=pltpu.CompilerParams(collective_id=3, has_side_effects=True, vmem_limit_bytes=60 * 1024 * 1024),
-    )(dxn, outp, gwin, gwout, small)
-
-
-def tiny_kernel(part_ref, out_ref, near_ref, sum_ref, far_ref, ns, nr, fs, fr):
-    d, c, z = place()
-    j = c * 4 + z
-    steps = mates()
-    planes = [(flip(d, 1), c, z), (flip(d, 2), c, z), (flip(flip(d, 1), 2), c, z)]
-    greet([mate(s) for s in steps] + planes)
+        pending.append(put(rows_of(rank_of(to)), slots_ref.at[i], as_.at[i], ar.at[i], to))
+    dxn_row.along(3, row_ref)
+
+    def norm_step(i, carry):
+        r = pl.ds(pl.multiple_of(i * 16, 16), 16)
+        x = tok_ref[0, r, :].astype(f32)
+        scale = lax.rsqrt(jnp.sum(x * x, axis=1, keepdims=True) * (1.0 / model) + EPS)
+        dxn = row_ref[r, :]
+        inner = dxn * gains_ref[...]
+        dot = jnp.sum(inner * x, axis=1, keepdims=True) * (1.0 / model)
+        dxx = scale * inner - x * (scale * scale * scale * dot)
+        gtok_ref[r, :] = (up_ref[0, r, :].astype(f32) + dxx).astype(bf16)
+        gain = dxn * (x * scale)
+        return carry + gain[0:8] + gain[8:16]
+
+    dgain = lax.fori_loop(0, length // 16, norm_step, jnp.zeros((8, model), f32))
+    dgain = jnp.sum(dgain, axis=0, keepdims=True)
+    seen = jnp.sum(stat_ref[0:1, :], axis=1, keepdims=True)
+    peak = jnp.max(stat_ref[1:2, :], axis=1, keepdims=True)
+    lane1 = lax.broadcasted_iota(jnp.int32, (1, 128), 1)
+    for q in range(4):
+        pairs_ref[q] = jnp.zeros((8, 128), f32)
+        for g in range(4):
+            at = g * 512 + q * 128
+            pairs_ref[q, g:g + 1, :] = dgain[:, at:at + 128]
+        pairs_ref[q, 4:5, :] = jnp.where(lane1 == 0, seen, jnp.where(lane1 == 1, peak, 0.0))
     for i, s in enumerate(steps):
         to = mate(s)
-        put(part_ref.at[rank_of(to)], near_ref.at[i], ns.at[i], nr.at[i], to)
-    row = lax.broadcasted_iota(jnp.int32, (8, 128), 0)
-    lane = lax.broadcasted_iota(jnp.int32, (8, 128), 1)
-    peak = (row == 4) & (lane == 1)
+        put(pairs_ref.at[rank_of(to) // 2], near_ref.at[i], ns.at[i], nr.at[i], to)
+    row8 = lax.broadcasted_iota(jnp.int32, (8, 128), 0)
+    lane8 = lax.broadcasted_iota(jnp.int32, (8, 128), 1)
+    top = (row8 == 4) & (lane8 == 1)
 
     def join(a, b):
-        return jnp.where(peak, jnp.maximum(a, b), a + b)
-
-    value = part_ref[j]
+        return jnp.where(top, jnp.maximum(a, b), a + b)
+
+    small_flat.finish(small_ref)
+    value = pairs_ref[j // 2]
     for i, s in enumerate(steps):
         landed(near_ref.at[i], nr.at[i], mate(s, -1))
         value = join(value, near_ref[i])
     sum_ref[...] = value
     for i, to in enumerate(planes):
         put(sum_ref, far_ref.at[i], fs.at[i], fr.at[i], to)
+
+    def settle(rank, source):
+        for s in range(2):
+            for g in range(4):
+                at = s * width * 8 + g * 1024
+                gwin_ref[:, pl.ds(pl.multiple_of(at + rank * 128, 128), 128)] = source[:, s * width + g * 128:s * width + (g + 1) * 128]
+
+    settle(j, rows_of(j))
+    for i, s in enumerate(steps):
+        src = mate(s, -1)
+        landed(slots_ref.at[i], ar.at[i], src)
+        settle(rank_of(src), slots_ref.at[i])
     for i, to in enumerate(planes):
         landed(far_ref.at[i], fr.at[i], to)
         value = join(value, far_ref[i])
-    out_ref[...] = value
+    tiny_ref[...] = value
     for i, to in enumerate(planes):
         sent(sum_ref, fs.at[i], to)
     for i, s in enumerate(steps):
         sent(near_ref.at[i], ns.at[i], mate(s))
-
-
-def tiny(part):
+    for copy in pending:
+        copy.wait_send()
+    for flat in (gwin_flat, gwout_flat, small_flat):
+        flat.close()
+
+
+def k3(part, stat, smalls, vecs, gains, gwdt, masks, tokens, upstream, m, mt, dg, dv, slope, u, vt, xnt, win, wout, ups):
+    like = jax.ShapeDtypeStruct
+    length, model = tokens.shape[1:]
+    count, channels = m.shape
+    tiles = channels // 128
     here = pl.BlockSpec(memory_space=pltpu.VMEM)
+    far = pl.BlockSpec(memory_space=pl.ANY)
     dma = lambda n: pltpu.SemaphoreType.DMA((n,))
+    own_d = model // 32
+    packed = part.shape[0]
     return pl.pallas_call(
-        tiny_kernel,
-        out_shape=jax.ShapeDtypeStruct((8, 128), f32),
-        in_specs=[here],
-        out_specs=here,
-        scratch_shapes=[pltpu.VMEM((7, 8, 128), f32), pltpu.VMEM((8, 128), f32), pltpu.VMEM((3, 8, 128), f32), dma(7), dma(7), dma(3), dma(3)],
-        compiler_params=pltpu.CompilerParams(collective_id=4, has_side_effects=True),
-    )(part)
+        k3_kernel,
+        out_shape=(
+            like((length, model), bf16),
+            like((length, model), bf16),
+            like((own_d, 16 * channels), bf16),
+            like((128, model), f32),
+            like((160, 384), f32),
+            like((8, 128), f32),
+        ),
+        in_specs=[here] * 9 + [far] * 11,
+        out_specs=(here,) * 6,
+        scratch_shapes=[
+            pltpu.VMEM((2, 4, length, model), bf16),
+            pltpu.VMEM((2, 4, length, model), bf16),
+            pltpu.VMEM((4, 512, 2 * channels), bf16),
+            pltpu.VMEM((4, 128, model), bf16),
+            pltpu.VMEM((4, 160, 384), f32),
+            pltpu.VMEM((count, channels), bf16),
+            pltpu.VMEM((channels, count), bf16),
+            pltpu.VMEM((count, 2 * channels), bf16),
+            pltpu.VMEM((tiles, count + 32, 128), f32),
+            pltpu.VMEM((tiles, count, 128), f32),
+            pltpu.VMEM(u.shape, f32),
+            pltpu.VMEM((model, count), bf16),
+            pltpu.VMEM((count, 256), bf16),
+            pltpu.VMEM((7, own_d, 2 * channels), bf16),
+            pltpu.VMEM((length, model), f32),
+            pltpu.VMEM((7, 8, 128), f32),
+            pltpu.VMEM((4, 8, 128), f32),
+            pltpu.VMEM((8, 128), f32),
+            pltpu.VMEM((3, 8, 128), f32),
+            dma(11), dma(7), dma(7), dma(7), dma(7), dma(3), dma(3),
+            pltpu.VMEM((packed, 128), f32),
+        ] + [pltpu.VMEM((packed // 2, 128), f32)] * 6 + [dma(PIECES) for _ in range(8)]
+        + row_scratch(length, model) * 2
+        + flat_scratch(512, 2 * channels, bf16) + flat_scratch(128, model, bf16) + flat_scratch(160, 384, f32),
+        compiler_params=pltpu.CompilerParams(collective_id=1, has_side_effects=True, vmem_limit_bytes=63400000),
+    )(part, stat, smalls, vecs, gains, gwdt, masks, tokens, upstream, m, mt, dg, dv, slope, u, vt, xnt, win, wout, ups)
 
 def masks(lengths, count):
     ends = jnp.cumsum(lengths, axis=1)
@@ -1422,86 +1532,29 @@
     channels = inner // ways
     rank = w_dt.shape[1]
     states = (w_x.shape[1] - rank) // 2
-    rows = ways
-    tall = rows * length
     cols, small, meta = prepare(gain, lengths, w_in, conv_w, conv_b, w_x, w_dt, dt_bias, skip, ways, groups)
-    xns, ups, win, wout, smalls, vecs, gains, masks, u_pad, g, v, slope, dl, kq_wide = k1(tokens, grad_out, cols, w_out, small, meta)
-    wx = smalls[:, :rank + 2 * states]
-    taps = vecs[:4].T
-    x = tokens[0].astype(f32)
-    scale = lax.rsqrt(jnp.mean(x * x, axis=1, keepdims=True) + EPS)
-
-    def time_major(a):
-        return a.reshape(rows, length, -1).transpose(1, 0, 2).reshape(tall, -1)
-
-    def row_major(a):
-        return a.reshape(length, rows, -1).transpose(1, 0, 2).reshape(tall, -1)
-
-    v4, g4 = v, g
-    u_pad, v, slope = [a.transpose(1, 0, 2).reshape(-1, channels) for a in (u_pad, v, slope)]
-    u = u_pad[24:].reshape(length, rows, channels)
-    same = [masks[o, :, 0].reshape(length, rows) for o in range(3)]
-    shifted = []
-    for offset in range(1, 4):
-        shifted.append(jnp.pad(u, ((offset, 0), (0, 0), (0, 0)))[:length] * same[offset - 1][:, :, None])
-    v16 = v.astype(bf16)
-    dims_cols = (((1,), (1,)), ((), ()))
-    dims_rows = (((0,), (0,)), ((), ()))
-    m16, dg16, dpre16, dv, part, stat = k2(dl, kq_wide, smalls, vecs, masks, v4, g4, ups, wout, states)
-    dv = dv.transpose(1, 0, 2).reshape(tall, channels)
-    dskip, grad_dtb = stat[6], stat[5]
-    out = jnp.dot(m16, wout, preferred_element_type=f32).astype(bf16)
-    grad_wout = lax.dot_general(m16, ups, dims_rows, preferred_element_type=f32).astype(bf16)
-    grad_wdt = lax.dot_general(dpre16, dl, dims_rows, preferred_element_type=f32)
-    part = group_total(part, 2)
-    dp16 = jnp.concatenate([part[:tall], part[tall:].reshape(tall // 4, 4, 32).transpose(1, 0, 2).reshape(tall, 32)], axis=1).astype(bf16)
-    grad_wx = lax.dot_general(v16, dp16, dims_rows, preferred_element_type=f32)
-    dvt = dv + lax.dot_general(dp16, wx, dims_cols, preferred_element_type=f32)
-    dc = (dvt * slope).reshape(length, rows, channels)
-    du = taps[:, 3] * dc
-    grad_taps = [jnp.sum(dc * u, axis=(0, 1))]
-    for offset in range(1, 4):
-        grad_taps.append(jnp.sum(dc * shifted[offset - 1], axis=(0, 1)))
-        du = du + taps[:, 3 - offset] * jnp.pad((dc * same[offset - 1][:, :, None])[offset:], ((0, offset), (0, 0), (0, 0)))
-    grad_conv = jnp.stack(grad_taps[::-1] + [jnp.sum(dc, axis=(0, 1)), grad_dtb, dskip], axis=1)
-    dz = jnp.concatenate([row_major(du.reshape(tall, channels)).astype(bf16), dg16], axis=1)
-    gwin = lax.dot_general(xns, dz, dims_rows, preferred_element_type=f32).astype(bf16)
-    dxn = lax.dot_general(dz, win, dims_cols, preferred_element_type=f32).astype(bf16)
-    small_grad = jnp.concatenate([grad_wx, grad_wdt, grad_conv], axis=1)
-    small_grad = jnp.pad(small_grad, ((0, 0), (0, -small_grad.shape[1] % 128)))
-    dxn, out, gwin, grad_wout, small_grad = back(
-        dxn.reshape(2, 4, length, model), out.reshape(2, 4, length, model), gwin.reshape(groups, ways * own_d, 2 * channels),
-        grad_wout.reshape(groups, own_e, model), small_grad.reshape(groups, own_e, -1))
-    block_out = (x + out).astype(bf16)
-    grad_win = gwin.reshape(ways, own_d, 2, groups, own_e).transpose(1, 2, 3, 0, 4).reshape(own_d, 2 * inner).astype(f32)
-    gains = gains[0]
-    inner_grad = dxn * gains
-    dxx = scale * inner_grad - x * (scale * scale * scale) * (jnp.sum(inner_grad * x, axis=1, keepdims=True) / model)
-    grad_tokens = (grad_out[0].astype(f32) + dxx).astype(bf16)
-    grad_gain = jnp.sum(dxn * x * scale, axis=0)
-    seen, peak = jnp.sum(stat[0]), jnp.max(stat[1])
-    part = grad_gain.reshape(groups, ways, own_d).transpose(1, 0, 2)
-    part = jnp.pad(part, ((0, 0), (0, 8 - groups), (0, 128 - own_d)))
-    part = part.at[:, 4, 0].set(seen).at[:, 4, 1].set(peak)
-    part = tiny(part)
-    grad_gain = lax.dynamic_index_in_dim(part, lax.axis_index("dp"), keepdims=False)[:own_d]
-    seen, peak = part[4, 0], part[4, 1]
-    beta_mean = seen / float(groups * ways * length * inner)
-    at = rank + 2 * states
+    xnt, ups, win, wout, smalls, vecs, gains, masks, live, u, g, v, vt, slope, dl, kq = k1(tokens, grad_out, cols, w_out, small, meta)
+    m, mt, dg, gwdt, dv, part, stat = k2(dl, kq, smalls, vecs, masks, live, v, g, ups, wout, states)
+    block_out, grad_tokens, grad_win, grad_wout, small_grad, tiny = k3(
+        part, stat, smalls, vecs, gains, gwdt, masks, tokens, grad_out, m, mt, dg, dv, slope, u, vt, xnt,
+        win.reshape(groups, ways * own_d, 2 * channels), wout.reshape(groups, own_e, model), ups.reshape(2, 4, length, model))
+    d, c, z = place()
+    grad_gain = lax.dynamic_slice(tiny, (d, lax.rem(z, 2) * own_d), (1, own_d))[0]
+    vectors = small_grad[own_e:own_e + 8, :own_e]
     return (
         block_out[None],
         grad_tokens[None],
         grad_gain,
-        grad_win,
-        small_grad[:, at + rank:at + rank + 4],
-        small_grad[:, at + rank + 4],
-        small_grad[:, :at],
-        small_grad[:, at:at + rank],
-        small_grad[:, at + rank + 5],
-        small_grad[:, at + rank + 6],
+        grad_win.astype(f32),
+        vectors[:4].T,
+        vectors[4],
+        small_grad[:own_e, :rank + 2 * states],
+        small_grad[:own_e, 256:],
+        vectors[5],
+        vectors[6],
         grad_wout,
-        beta_mean,
-        peak,
+        tiny[4, 0] / float(groups * ways * length * inner),
+        tiny[4, 1],
     )
 
 

time: 429 us -> 346 us (0.81)
  local copies, waits for them, and re-layouts: 49.1 us -> 13.2 us
  matrix products: 28.8 us -> 0 us
  other arithmetic: 16 us -> 6.11 us
  Pallas kernels: 329 us -> 322 us
    dot_general x7 -> x0, matrix products: 28.8 us -> none  [the longest x1 8.57 us: on_device_direct(): lax.dot_general(xns, dz, dims_rows, preferred_element_type=f32).astype(bf16)]
    reshape x6 -> x0, local copies, waits for them, and re-layouts: 9.83 us -> none  [the longest x2 6.02 us: on_device_direct(): u = u_pad[24:].reshape(length, rows, channels)]
    slice x17 -> x3, local copies, waits for them, and re-layouts: 11.8 us -> 1.97 us  [the longest x1 1.33 us: on_device_direct(): tiny[4, 1]]
    pallas_call x4 -> x2, Pallas kernels: 271 us -> 262 us  [the longest x1 135 us: k3(): pl.pallas_call(k3_kernel, out_shape=(like((length, model), bf16), like((l...]
    reduce_sum x3 -> x0, other arithmetic: 5.86 us -> none  [the longest x1 5.39 us: on_device_direct(): grad_taps.append(jnp.sum(dc * shifted[offset - 1], axis=(0, 1)))]
    unnamed x65 -> x18, local copies, waits for them, and re-layouts: 10.7 us -> 4.92 us
    mul x4 -> x0, other arithmetic: 4.59 us -> none  [the longest x3 4.58 us: on_device_direct(): dc * same[offset - 1][:, :, None]]
where the time goes in v4:
time: 346 us; the launch traced here: 343 us
  Pallas kernels  322 us (93%)
  local copies, waits for them, and re-layouts  13.2 us (4%)
  other arithmetic  6.11 us (2%)
    pallas_call x1, Pallas kernels, k3(): pl.pallas_call(k3_kernel, out_shape=(like((length, model), bf16), like((l...  135 us
    pallas_call x1, Pallas kernels, k1(): pl.pallas_call(k1_kernel, out_shape=(like((model, count), bf16), like((co...  127 us
    pallas_call x1, Pallas kernels, k2(): pl.pallas_call(functools.partial(k2_kernel, states), grid=(channels // wi...  59.6 us

profile of v4, /device:TPU:8, one launch (start us, length us, event | category | flops | bytes accessed | tf_op | source)
XLA Modules:
  0.0 343.5 jit_solution(9395116574517309907)
XLA Ops:
  0.6 0.7 bitcast_convert_fusion
  1.3 0.7 convert_bitcast_fusion
  2.0 0.7 tile.2
  2.7 0.7 convert_element_type.18
  3.4 0.7 bitcast_convert_fusion.2
  4.1 1.2 concatenate.7.meta_ref
  5.3 1.5 copy.28
  6.8 0.4 copy.30
  7.2 1.5 reshape.45.cols_ref
  8.8 0.1 copy.26
  8.9 0.7 fusion.1.small_ref
  9.6 126.9 %shard_map.219 = (bf16[2048,1024]{1,0:T(8,128)(2,1)}, bf16[1024,2048]{1,0:T(8,128)(2,1)}, bf16[2048,1024]{1,0:T(8,128)(2,1)}, bf16[512,2048]{1,0:T(8,128)(2,1)},...) custom-call(bf16[1,128,2048]{2,1,0:T(8,128)(2,1)} %tok_ref.3, ...), custom_call_target="tpu_custom_call" | custom-call | tf_op jit(solution)/shard_map/pallas_call | solution.py:642
  136.4 59.6 %shard_map.220 = (bf16[1024,512]{1,0:T(8,128)(2,1)}, bf16[512,1024]{1,0:T(8,128)(2,1)}, bf16[1024,512]{1,0:T(8,128)(2,1)}, f32[512,128]{1,0:T(8,128)}, f32[4,102...) custom-call(bf16[1024,128]{1,0:T(8,128)(2,1)} %get-tuple-element.42.dl_ref, ...), custom_call_target="tpu_custom_call" | custom-call | tf_op jit(solution)/shard_map/pallas_call | solution.py:908
  196.1 135.1 %shard_map.221 = (bf16[128,2048]{1,0:T(8,128)(2,1)}, bf16[128,2048]{1,0:T(8,128)(2,1)}, bf16[64,8192]{1,0:T(8,128)(2,1)}, f32[128,2048]{1,0:T(8,128)}, f32[160,384]{1,0:T(8,128)}, /*index=5*/f32[8,128]{1,0:T(8,128)}) custom-call(f32[1280,128]{1,0:T(8,128)} %get-tuple-element.52.part_ref, f32[8,512]{1,0:T(8,128)} %get-tuple-element.53.stat_ref, ...), custom_call_target="tpu_custom_call" | custom-call | tf_op jit(solution)/shard_map/pallas_call | solution.py:1339
  331.2 2.8 convert_element_type.19
  334.0 0.7 copy.27
  334.8 0.6 slice.32
  335.4 1.3 dynamic-slice_bitcast_fusion
  336.7 0.6 slice_bitcast_fusion
  337.3 1.3 fusion.2
  339.2 0.5 slice_bitcast_fusion.1
  339.8 0.8 copy.34
  340.6 0.8 copy.35
  341.4 1.0 copy.36
  (17 shorter events, 0.1 us)
Async XLA Ops:
  6.8 2.0 copy-start.4
  6.8 2.1 copy-start.5
  331.2 2.8 copy-start.3
  331.2 8.5 %copy-start.2 = (bf16[128,2048]{1,0:T(8,128)(2,1)S(1)}, bf16[128,2048]{1,0:T(8,128)(2,1)}, u32[]{:S(2)}) copy-start(bf16[128,2048]{1,0:T(8,128)(2,1)} %get-tuple-element.65) | copy-start | bytes 1572868
  331.2 9.3 %copy-start.1 = (bf16[128,2048]{1,0:T(8,128)(2,1)S(1)}, bf16[128,2048]{1,0:T(8,128)(2,1)}, u32[]{:S(2)}) copy-start(bf16[128,2048]{1,0:T(8,128)(2,1)} %get-tuple-element.66) | copy-start | bytes 1572868
  334.0 7.3 %copy-start = (f32[128,2048]{1,0:T(8,128)S(1)}, f32[128,2048]{1,0:T(8,128)}, u32[]{:S(2)}) copy-start(f32[128,2048]{1,0:T(8,128)} %get-tuple-element.114) | copy-start | bytes 3145732

commit v5 on v4

--- a/solution.py
+++ b/solution.py
@@ -226,9 +226,10 @@
 PIECES = 4
 
 
-def k1_kernel(tok_ref, up_ref, cols_ref, wout_ref, small_ref, meta_ref,
-              xnt_out, ups_ref, win_out, wouts_ref, smalls_ref, vecs_ref, gains_ref, masks_ref, live_ref,
-              u_ref, g_ref, v_ref, vt_ref, slope_ref, dl_ref, kq_ref,
+def k1_kernel(tok_ref, up_ref, w_ref, wout_ref, small_ref, gain_ref, lens_ref, convw_ref, vec_ref,
+              xnt_out, ups_ref, win_out, wouts_ref, smalls_ref, vecs_ref, gains_ref, masks_out, live_out,
+              u_out, g_out, v_out, vt_out, slope_out, dl_ref, kq_ref,
+              masks_ref, live_ref, u_ref, g_ref, v_ref, vt_ref, slope_ref, save_sem, cols_ref, meta_ref,
               xs_ref, xn_ref, xnt_ref, win_ref, metas_ref, part_ref, out_ref, sib_ref, base_ref, left_ref, right_ref, tor_ref, tol_ref,
               own_sem, ms, mr, qs, qr, xls, xlr, xrs, xrr, xcs, xcr, as_, ar, ps, pr, rs, rr, ws, wr, ts, tr, tls, tlr, trs, trr, tos, tor):
     d, c, z = place()
@@ -239,10 +240,19 @@
     left = (d, c, lax.rem(z + 3, 4))
     right = (d, c, lax.rem(z + 1, 4))
     steps = mates()
-    greet([mate(s) for s in steps] + [xn, yn, dn])
     length = tok_ref.shape[1]
     model = tok_ref.shape[2]
     depth = cols_ref.shape[1]
+    for rank in range(8):
+        for n in range(8):
+            cols_ref[rank, :, n * 128:(n + 1) * 128] = w_ref[:, (n * 8 + rank) * 128:(n * 8 + rank + 1) * 128]
+    meta_ref[...] = jnp.zeros_like(meta_ref)
+    meta_ref[0:1, 0:depth] = gain_ref[...].astype(f32)
+    meta_ref[0:1, depth:2 * depth] = gain_ref[...].astype(f32)
+    meta_ref[1:2, 0:5] = lens_ref[...].astype(f32)
+    meta_ref[8:12, :] = convw_ref[...].astype(f32)
+    meta_ref[12:15, :] = vec_ref[...].astype(f32)
+    greet([mate(s) for s in steps] + [xn, yn, dn])
     tiles = u_ref.shape[0]
     width = tiles * 128
     count = g_ref.shape[1]
@@ -277,6 +287,9 @@
         pending.append(put(cols_ref.at[rank_of(to)], win_ref.at[block(d, j)], as_.at[i], ar.at[i], to))
     for i, to in enumerate((xn, yn, dn)):
         pending.append(put(small_ref, smalls_ref.at[part_e(d)], ps.at[16 + i], pr.at[16 + i], to))
+    halves = own_e // 2
+    pending.append(put(wout_ref, wouts_ref.at[part_e(d)], ws.at[0], wr.at[0], xn))
+    pending.append(put(wout_ref, wouts_ref.at[part_e(d)], ws.at[1], wr.at[1], yn))
     own[2].wait()
     slot = win_ref.at[block(d, j)]
     pending.append(put(slot, slot, ps.at[7], pr.at[7], xn))
@@ -334,7 +347,6 @@
             def _():
                 sent(out.at[rows(j)], xcs.at[base + at], sib)
 
-    row_start(tok_ref, xs_ref, 0)
     own[5].wait()
     for i, s in enumerate(steps):
         landed(metas_ref.at[d, rank_of(mate(s, -1))], mr.at[i], xn)
@@ -407,30 +419,32 @@
             xn_ref[r, :] = (x * scale * gains_ref[...]).astype(bf16)
             return carry
 
-        lax.fori_loop(0, length // 16, body, 0)
-
-        def turn(i, carry):
-            part = pl.ds(pl.multiple_of(i * 256, 256), 256)
-            xnt_ref[part, rows(rank)] = xn_ref[rows(rank), part].T
-            return carry
-
-        lax.fori_loop(0, model // 256, turn, 0)
-
-    for i in range(1, 7):
+        lax.fori_loop(0, length // 16, body, 0, unroll=4)
+
+    for i in range(1, 4):
+        pass_on(i)
+    slot = wouts_ref.at[part_e(dx)]
+    landed(slot, wr.at[0], xn)
+    slot = wouts_ref.at[part_e(dx, 0, halves)]
+    pending.append(put(slot, slot, ws.at[2], wr.at[2], yn))
+    slot = wouts_ref.at[part_e(dy)]
+    landed(slot, wr.at[1], yn)
+    slot = wouts_ref.at[part_e(dy, halves, halves)]
+    pending.append(put(slot, slot, ws.at[3], wr.at[3], xn))
+
+    row_start(tok_ref, xs_ref, 0)
+    for i in range(4, 7):
         pass_on(i)
     own[0].wait()
     normalize(j)
     row_hop(xs_ref, 0, 0, normalize)
-    row_start(up_ref, ups_ref, 4)
-    halves = own_e // 2
-    pending.append(put(wout_ref, wouts_ref.at[part_e(d)], ws.at[0], wr.at[0], xn))
-    pending.append(put(wout_ref, wouts_ref.at[part_e(d)], ws.at[1], wr.at[1], yn))
     for k in range(4):
         relay(k)
     row_hop(xs_ref, 0, 1, normalize)
     for k in range(4, 8):
         relay(k)
     row_hop(xs_ref, 0, 2, normalize)
+    row_start(up_ref, ups_ref, 4)
     for at in range(4):
         rank = flip(c, 1) * 4 + at
         landed(xs_ref.at[rows(rank)], xcr.at[at], sib)
@@ -442,9 +456,7 @@
         else:
             landed(slot, rr.at[4 + k // 2], xn)
     own += [pltpu.make_async_copy(xnt_ref, xnt_out, own_sem.at[6]), pltpu.make_async_copy(win_ref, win_out, own_sem.at[7])]
-    own[6].start()
     own[7].start()
-    row_hop(ups_ref, 4, 0)
     lead = u_ref.shape[1] - count
     u_ref[:, 0:lead, :] = jnp.zeros((tiles, lead, 128), f32)
 
@@ -476,7 +488,7 @@
             slope_ref[n, r, :] = sig * (1.0 + total * (1.0 - sig))
         return carry
 
-    lax.fori_loop(0, count // 32, conv_step, 0)
+    lax.fori_loop(0, count // 32, conv_step, 0, unroll=2)
     for copy in own[3:5]:
         copy.wait()
     for i, (to, at) in enumerate(((xn, dx), (yn, dy), (dn, dd))):
@@ -491,28 +503,40 @@
         turned = pltpu.roll(narrow, 32 * b, 1) if b else narrow
         packed = packed + jnp.dot(values, turned.astype(bf16), preferred_element_type=f32)
     part_ref[count:count + quarter, :] = packed
-    slot = wouts_ref.at[part_e(dx)]
-    landed(slot, wr.at[0], xn)
-    slot = wouts_ref.at[part_e(dx, 0, halves)]
-    pending.append(put(slot, slot, ws.at[2], wr.at[2], yn))
-    slot = wouts_ref.at[part_e(dy)]
-    landed(slot, wr.at[1], yn)
-    slot = wouts_ref.at[part_e(dy, halves, halves)]
-    pending.append(put(slot, slot, ws.at[3], wr.at[3], xn))
+    saves = [(u_ref, u_out), (v_ref, v_out), (slope_ref, slope_out), (masks_ref, masks_out), (live_ref, live_out), (g_ref, g_out), (vt_ref, vt_out)]
+    saves = [pltpu.make_async_copy(a, b, save_sem.at[i]) for i, (a, b) in enumerate(saves)]
+    for copy in saves[:5]:
+        copy.start()
+
+    def early():
+        row_hop(ups_ref, 4, 0)
 
     def between():
         spread(g_ref, 0, width)
+        saves[5].start()
+
+    def late():
+        def turn_x(i, carry):
+            part = pl.ds(pl.multiple_of(i * 128, 128), 128)
+            for rank in range(8):
+                r = slice(rank * length, (rank + 1) * length)
+                xnt_ref[part, r] = xn_ref[r, part].T
+            return carry
+
+        lax.fori_loop(0, model // 128, turn_x, 0)
+        own[6].start()
         row_hop(ups_ref, 4, 1)
 
-        def turn(i, carry):
+        def turn_v(i, carry):
             r = pl.ds(pl.multiple_of(i * 128, 128), 128)
             for n in range(tiles):
                 vt_ref[n * 128:(n + 1) * 128, r] = v_ref[n, r, :].T.astype(bf16)
             return carry
 
-        lax.fori_loop(0, count // 128, turn, 0)
-
-    line_total(part_ref, out_ref, sib_ref, base_ref, left_ref, right_ref, tor_ref, tol_ref, ts, tr, tls, tlr, trs, trr, tos, tor, between)
+        lax.fori_loop(0, count // 128, turn_v, 0)
+        saves[6].start()
+
+    line_total(part_ref, out_ref, sib_ref, base_ref, left_ref, right_ref, tor_ref, tol_ref, ts, tr, tls, tlr, trs, trr, tos, tor, early, between, late)
     dl_ref[...] = out_ref[0:count, :].astype(bf16)
     for b in range(4):
         packed = out_ref[count:count + quarter, :]
@@ -525,13 +549,15 @@
     row_end(xs_ref, 0)
     row_end(ups_ref, 4)
     own[1].wait()
+    for copy in saves:
+        copy.wait()
     own[6].wait()
     own[7].wait()
     for copy in pending:
         copy.wait_send()
 
 
-def line_total(part_ref, out_ref, sib_ref, base_ref, left_ref, right_ref, tor_ref, tol_ref, ss, sr, ls, lr, rs, rr, os_, or_, between, early=None):
+def line_total(part_ref, out_ref, sib_ref, base_ref, left_ref, right_ref, tor_ref, tol_ref, ss, sr, ls, lr, rs, rr, os_, or_, early, between, late):
     d, c, z = place()
     sib = (d, flip(c, 1), z)
     left = (d, c, lax.rem(z + 3, 4))
@@ -560,8 +586,7 @@
         def _():
             put(base_ref.at[cut(p)], right_ref.at[cut(p)], ls.at[p], rr.at[p], left)
 
-    if early is not None:
-        early()
+    early()
 
     def from_left(p):
         landed(left_ref.at[cut(p)], lr.at[p], left)
@@ -589,8 +614,7 @@
         for p in range(PIECES):
             from_right(p)
 
-    if between is not None:
-        between()
+    between()
 
     @pl.when(z < 2)
     def _():
@@ -614,6 +638,7 @@
             out_ref[far(mine, p), :] += right_ref[cut(p), :]
 
         put(out_ref.at[far(mine, p)], out_ref.at[far(mine, p)], os_.at[p], or_.at[p], sib)
+    late()
     for p in range(PIECES):
         landed(out_ref.at[far(theirs, p)], or_.at[p], sib)
         sent(out_ref.at[far(mine, p)], os_.at[p], sib)
@@ -628,8 +653,10 @@
             sent(base_ref.at[cut(p)], ls.at[p], left)
 
 
-def k1(tokens, upstream, cols, w_out, small, meta):
-    groups, ways = 4, cols.shape[0]
+def k1(tokens, upstream, w_in, w_out, small, gain, lengths, conv_w, vec):
+    groups, ways = 4, 8
+    cols = jax.ShapeDtypeStruct((ways, w_in.shape[0], w_in.shape[1] // ways), bf16)
+    meta = jax.ShapeDtypeStruct((16, 128), f32)
     like = jax.ShapeDtypeStruct
     length, model = tokens.shape[1:]
     count = ways * length
@@ -659,9 +686,19 @@
             like((count, 128), bf16),
             like((count, 128), f32),
         ),
-        in_specs=[some] * 6,
-        out_specs=(far,) * 4 + (here,) * 12,
+        in_specs=[some] * 2 + [here, some, some] + [here] * 4,
+        out_specs=(far,) * 4 + (here,) * 3 + (far,) * 7 + (here,) * 2,
         scratch_shapes=[
+            pltpu.VMEM((3, count + 32, 128), f32),
+            pltpu.VMEM((1, count, 128), f32),
+            pltpu.VMEM((channels // 128, count + 24, 128), f32),
+            pltpu.VMEM((channels // 128, count, 128), f32),
+            pltpu.VMEM((channels // 128, count, 128), f32),
+            pltpu.VMEM((channels, count), bf16),
+            pltpu.VMEM((channels // 128, count, 128), f32),
+            dma(7),
+            pltpu.VMEM(cols.shape, bf16),
+            pltpu.VMEM(meta.shape, f32),
             pltpu.VMEM((count, model), bf16),
             pltpu.VMEM((count, model), bf16),
             pltpu.VMEM((model, count), bf16),
@@ -673,7 +710,7 @@
         + [dma(8), dma(7), dma(7), dma(3), dma(3), dma(8), dma(8), dma(8), dma(8), dma(8), dma(8), dma(7), dma(7), dma(19), dma(19), dma(8), dma(8), dma(4), dma(4)]
         + [dma(PIECES) for _ in range(8)],
         compiler_params=pltpu.CompilerParams(collective_id=0, has_side_effects=True, vmem_limit_bytes=56 * 1024 * 1024),
-    )(tokens, upstream, cols, w_out, small, meta)
+    )(tokens, upstream, w_in, w_out, small, gain, lengths, conv_w, vec)
 
 
 GROUP = 4
@@ -951,9 +988,17 @@
         for zp in (3, 0, 2, 1):
             put(self.part.at[flip(self.c, 1), zp], self.sib.at[zp], self.ss.at[zp], self.sr.at[zp], self.other)
 
+    def gather(self):
+        for zp in (3, 0, 2, 1):
+            landed(self.sib.at[zp], self.sr.at[zp], self.other)
+            add_rows(self.sib.at[zp], [self.sib.at[zp], self.part.at[self.c, zp]])
+
+    def release(self):
+        for zp in range(4):
+            sent(self.part.at[flip(self.c, 1), zp], self.ss.at[zp], self.other)
+
     def terms(self, zs, zp):
-        landed(self.sib.at[zp], self.sr.at[zp], self.other)
-        found = [self.sib.at[zp], self.part.at[self.c, zp]]
+        found = [self.sib.at[zp]]
         if zp >= zs and zs > 0:
             landed(self.recv.at[zp], self.lr.at[zp], self.to_left)
             found.append(self.recv.at[zp])
@@ -963,13 +1008,18 @@
             found.append(slot)
         return found
 
+    def join(self, zs, zp):
+        found = self.terms(zs, zp)
+        if len(found) > 1:
+            add_rows(self.sib.at[zp], found)
+
     def step(self, zs, k):
-        for zp in range(4):
-            if zp > zs and k == 3 - zp + zs:
-                add_rows(self.sib.at[zp], self.terms(zs, zp))
+        for zp in ((3, 2, 1, 0) if zs == 0 else (0, 1, 2, 3)):
+            if zp > zs and k == (0 if zs == 0 else 3 - zp + zs):
+                self.join(zs, zp)
                 put(self.sib.at[zp], self.recv.at[zp], self.gs.at[zp], self.lr.at[zp], self.to_right)
-            if zp < zs and k == zp + 3 - zs:
-                add_rows(self.sib.at[zp], self.terms(zs, zp))
+            if zp < zs and k == (0 if zs == 3 else zp + 3 - zs):
+                self.join(zs, zp)
                 put(self.sib.at[zp], self.recv.at[4 if zp == zs - 1 else zp], self.gs.at[zp], self.rr.at[zp], self.to_left)
 
     def finish(self, zs):
@@ -977,7 +1027,6 @@
 
     def close(self, zs):
         for zp in range(4):
-            sent(self.sib.at[zp], self.ss.at[zp], self.other)
             if zp != zs:
                 sent(self.sib.at[zp], self.gs.at[zp], self.other)
 
@@ -1065,7 +1114,7 @@
 
 def k3_kernel(part_ref, stat_ref, smalls_ref, vecs_ref, gains_ref, gwdt_ref, masks_ref, tok_ref, up_ref,
               m_any, mt_any, dg_any, dv_any, slope_any, u_any, vt_any, xnt_any, win_any, wout_any, ups_any,
-              block_ref, gtok_ref, gwin_ref, gwout_ref, small_ref, tiny_ref, *scratch):
+              block_out, gtok_out, gwin_out, gwout_out, small_out, tiny_out, *scratch):
     scratch = list(scratch)
 
     def take(n):
@@ -1073,15 +1122,16 @@
         del scratch[:n]
         return found
 
-    outp, dxnp, gwinp, gwoutp, smallp = take(5)
+    block_ref, gtok_ref, gwin_ref, gwout_ref, small_ref, tiny_ref, stores = take(7)
+    outp, win_ref, up, gp, gwoutp, smallp = take(6)
     m_ref, mt_ref, dz_ref, dc_ref, slope_ref, u_ref, xnt_ref, dp_ref, slots_ref, row_ref = take(10)
     near_ref, pairs_ref, sum_ref, far_ref = take(4)
     loads, as_, ar, ns, nr, fs, fr = take(7)
     totals = take(7)
     total_sems = take(8)
     out_row = Row(outp, *take(2), take(5))
-    dxn_row = Row(dxnp, *take(2), take(5))
-    gwin_flat = Flat(gwinp, *take(6))
+    dxn_row = Row(outp, *take(2), take(5))
+    flats = [Flat(up, *take(6)), Flat(gp, *take(6))]
     gwout_flat = Flat(gwoutp, *take(6))
     small_flat = Flat(smallp, *take(6))
     d, c, z = place()
@@ -1093,12 +1143,19 @@
     tiles, padded, _ = dc_ref.shape
     count = dz_ref.shape[0]
     width = tiles * 128
-    rows_any = [(m_any, m_ref), (wout_any, gwoutp), (ups_any, dxnp), (mt_any, mt_ref), (dv_any, dc_ref.at[:, pl.ds(0, count)]),
-                (slope_any, slope_ref), (u_any, u_ref), (dg_any, dz_ref.at[:, pl.ds(width, width)]), (xnt_any, xnt_ref), (win_any, gwinp)]
+    rows_any = [(m_any, m_ref), (wout_any, gwoutp), (mt_any, mt_ref)]
+    for at, holder in ((0, gp), (1024, up)):
+        for h in range(2):
+            for q in range(2):
+                rows_any.append((ups_any.at[pl.ds(q * 512, 512), pl.ds(at + h * 512, 512)], holder.at[2 * h + q]))
+    rows_any += [(dg_any, dz_ref.at[:, pl.ds(width, width)]), (xnt_any, xnt_ref), (dv_any, dc_ref.at[:, pl.ds(0, count)]),
+                 (slope_any, slope_ref), (u_any, u_ref), (win_any, win_ref)]
     copies = [pltpu.make_async_copy(a, b, loads.at[i]) for i, (a, b) in enumerate(rows_any)]
     for copy in copies:
         copy.start()
     greet([mate(s) for s in steps] + planes)
+    outs = [(block_ref, block_out), (gtok_ref, gtok_out), (gwin_ref, gwin_out), (gwout_ref, gwout_out), (small_ref, small_out), (tiny_ref, tiny_out)]
+    outs = [pltpu.make_async_copy(a, b, stores.at[i]) for i, (a, b) in enumerate(outs)]
     tile = 256
     nn = (((1,), (0,)), ((), ()))
     nt = (((1,), (1,)), ((), ()))
@@ -1117,6 +1174,26 @@
 
         lax.fori_loop(0, model // tile, body, 0)
 
+    def weight_rows(holder, first, group):
+        def body(i, carry):
+            lanes = pl.ds(pl.multiple_of(i * tile, tile), tile)
+            left = xnt_ref[pl.ds(pl.multiple_of(group * 512, 512), 512), :]
+            value = dz_ref[:, pl.ds(pl.multiple_of(first + i * tile, tile), tile)]
+            holder[group, :, lanes] = jnp.dot(left, value, preferred_element_type=f32).astype(bf16)
+            return carry
+
+        lax.fori_loop(0, width // tile, body, 0)
+
+    def weight_part(k):
+        flat = flats[k]
+        holder, first = (up, 0) if k == 0 else (gp, width)
+        weight_rows(holder, first, flat.dd)
+        flat.start_far()
+        weight_rows(holder, first, flat.dx)
+        weight_rows(holder, first, flat.dy)
+        flat.start_near()
+        weight_rows(holder, first, d)
+
     def early():
         copies[0].wait()
         copies[1].wait()
@@ -1125,26 +1202,50 @@
         rows_product(c, outp, m_ref, gwoutp, nn, False)
 
     def between():
+        out_row.gather()
         out_row.along(0)
-        copies[2].wait()
-        copies[3].wait()
-
-        def body(i, carry):
-            lanes = pl.ds(pl.multiple_of(i * tile, tile), tile)
-            value = dxnp[:, :, :, lanes].reshape(count, tile)
-            product = jnp.dot(mt_ref[...], value, preferred_element_type=f32)
-            for g in range(4):
-                gwoutp[g, :, lanes] = product[g * 128:(g + 1) * 128].astype(bf16)
-            return carry
-
-        lax.fori_loop(0, model // tile, body, 0)
-        gwout_flat.start_far()
-        gwout_flat.start_near()
+        for copy in copies[2:11]:
+            copy.wait()
+        for holder, at in ((gp, 0), (up, 1024)):
+            def body(i, carry):
+                h = i // 2
+                off = pl.ds(pl.multiple_of((i % 2) * tile, tile), tile)
+                value = jnp.concatenate([holder[2 * h, :, off], holder[2 * h + 1, :, off]], axis=0)
+                product = jnp.dot(mt_ref[...], value, preferred_element_type=f32)
+                for g in range(4):
+                    gwoutp[g, :, pl.ds(pl.multiple_of(at + i * tile, tile), tile)] = product[g * 128:(g + 1) * 128].astype(bf16)
+                return carry
+
+            lax.fori_loop(0, 4, body, 0)
+
+    def late():
+        for copy in copies[11:13]:
+            copy.wait()
+        weight_part(1)
+
+    seen = jnp.sum(stat_ref[0:1, :], axis=1, keepdims=True)
+    peak = jnp.max(stat_ref[1:2, :], axis=1, keepdims=True)
+    row8 = lax.broadcasted_iota(jnp.int32, (8, 128), 0)
+    lane8 = lax.broadcasted_iota(jnp.int32, (8, 128), 1)
+    pairs_ref[...] = jnp.where(lane8 == 0, seen, jnp.where(lane8 == 1, peak, 0.0))
+    for i, s in enumerate(steps):
+        put(pairs_ref, near_ref.at[i], ns.at[i], nr.at[i], mate(s))
+
+    def join(a, b):
+        return jnp.where(lane8 == 1, jnp.maximum(a, b), a + b)
 
     total_ref = totals[0]
-    line_total(part_ref, *totals, *total_sems, between, early)
-    vt_copy = pltpu.make_async_copy(vt_any, mt_ref, loads.at[10])
+    line_total(part_ref, *totals, *total_sems, early, between, late)
+    vt_copy = pltpu.make_async_copy(vt_any, mt_ref, loads.at[17])
     vt_copy.start()
+    out_row.along(1)
+    value = pairs_ref[...]
+    for i, s in enumerate(steps):
+        landed(near_ref.at[i], nr.at[i], mate(s, -1))
+        value = join(value, near_ref[i])
+    sum_ref[...] = value
+    for i, to in enumerate(planes):
+        put(sum_ref, far_ref.at[i], fs.at[i], fr.at[i], to)
     quarter = count // 4
     lane = lax.broadcasted_iota(jnp.int32, (quarter, 128), 1)
     dp_ref[:, 0:128] = total_ref[0:count, :].astype(bf16)
@@ -1152,8 +1253,8 @@
         packed = total_ref[count:count + quarter, :]
         packed = pltpu.roll(packed, 128 - 32 * b, 1) if b else packed
         dp_ref[b * quarter:(b + 1) * quarter, 128:256] = jnp.where(lane < 32, packed, 0.0).astype(bf16)
-    copies[4].wait()
-    copies[5].wait()
+    for copy in copies[13:16]:
+        copy.wait()
     dc_ref[:, count:, :] = jnp.zeros((tiles, padded - count, 128), f32)
 
     def slope_step(i, carry):
@@ -1164,7 +1265,7 @@
         return carry
 
     lax.fori_loop(0, count // 256, slope_step, 0)
-    copies[6].wait()
+    flats[1].middle()
     taps = [vecs_ref[o:o + 1, :] for o in range(4)]
     lead = u_ref.shape[1] - count
 
@@ -1194,8 +1295,6 @@
         smallp[n, 134:135, 0:128] = stat_ref[6:7, lanes]
         smallp[n, 0:128, 256:384] = gwdt_ref[n * 128:(n + 1) * 128, :]
 
-    copies[7].wait()
-
     def by_row(i, carry):
         r = pl.ds(pl.multiple_of(i * length, length), length)
         for n in range(tiles):
@@ -1203,36 +1302,36 @@
         return carry
 
     lax.fori_loop(0, 8, by_row, 0)
-    copies[9].wait()
-    rows_product(other, dxnp, dz_ref, gwinp, nt, True)
+    copies[16].wait()
+    out_row.release()
+    rows_product(other, outp, dz_ref, win_ref, nt, True)
     dxn_row.start()
-    rows_product(c, dxnp, dz_ref, gwinp, nt, True)
-    out_row.along(1)
-    copies[8].wait()
-
-    def weight_rows(group):
-        def body(i, carry):
-            lanes = pl.ds(pl.multiple_of(i * tile, tile), tile)
-            left = xnt_ref[pl.ds(pl.multiple_of(group * 512, 512), 512), :]
-            gwinp[group, :, lanes] = jnp.dot(left, dz_ref[:, lanes], preferred_element_type=f32).astype(bf16)
-            return carry
-
-        lax.fori_loop(0, 2 * width // tile, body, 0)
-
-    weight_rows(gwin_flat.dd)
-    gwin_flat.start_far()
-    weight_rows(gwin_flat.dx)
-    weight_rows(gwin_flat.dy)
-    gwin_flat.start_near()
+    rows_product(c, outp, dz_ref, win_ref, nt, True)
     out_row.along(2)
+    dxn_row.gather()
     dxn_row.along(0)
-    weight_rows(d)
-    gwout_flat.middle()
+    weight_part(0)
+    block = gwin_ref.shape[0]
+    pending = []
+
+    def rows_of(k, rank):
+        return flats[k].part.at[d, pl.ds(pl.multiple_of(rank * block, block), block)]
+
+    def give(k):
+        flats[k].finish(flats[k].part.at[d])
+        for i, s in enumerate(steps):
+            to = mate(s)
+            pending.append(put(rows_of(k, rank_of(to)), slots_ref.at[k, i], as_.at[7 * k + i], ar.at[7 * k + i], to))
+
+    give(1)
+    gwout_flat.start_far()
+    gwout_flat.start_near()
     vt_copy.wait()
     for n in range(tiles):
         smallp[n, 0:128, 0:256] = jnp.dot(mt_ref[n * 128:(n + 1) * 128, :], dp_ref[...], preferred_element_type=f32)
     small_flat.start_far()
     small_flat.start_near()
+    flats[0].middle()
     out_row.along(3, row_ref)
 
     def block_step(i, carry):
@@ -1241,24 +1340,16 @@
         return carry
 
     lax.fori_loop(0, length // 16, block_step, 0)
-    gwin_flat.middle()
+    outs[0].start()
     dxn_row.along(1)
+    give(0)
+    gwout_flat.middle()
+    small_flat.middle()
+    dxn_row.along(2)
     gwout_flat.finish(gwout_ref)
-    dxn_row.along(2)
-    small_flat.middle()
-    block = gwin_ref.shape[0]
-    fin = gwinp.at[d]
-    gwin_flat.finish(fin)
-
-    def rows_of(rank):
-        return gwinp.at[d, pl.ds(pl.multiple_of(rank * block, block), block)]
-
-    pending = []
-    for i, s in enumerate(steps):
-        to = mate(s)
-        pending.append(put(rows_of(rank_of(to)), slots_ref.at[i], as_.at[i], ar.at[i], to))
+    outs[3].start()
     dxn_row.along(3, row_ref)
-
+    dxn_row.release()
     def norm_step(i, carry):
         r = pl.ds(pl.multiple_of(i * 16, 16), 16)
         x = tok_ref[0, r, :].astype(f32)
@@ -1268,62 +1359,41 @@
         dot = jnp.sum(inner * x, axis=1, keepdims=True) * (1.0 / model)
         dxx = scale * inner - x * (scale * scale * scale * dot)
         gtok_ref[r, :] = (up_ref[0, r, :].astype(f32) + dxx).astype(bf16)
-        gain = dxn * (x * scale)
-        return carry + gain[0:8] + gain[8:16]
-
-    dgain = lax.fori_loop(0, length // 16, norm_step, jnp.zeros((8, model), f32))
-    dgain = jnp.sum(dgain, axis=0, keepdims=True)
-    seen = jnp.sum(stat_ref[0:1, :], axis=1, keepdims=True)
-    peak = jnp.max(stat_ref[1:2, :], axis=1, keepdims=True)
-    lane1 = lax.broadcasted_iota(jnp.int32, (1, 128), 1)
-    for q in range(4):
-        pairs_ref[q] = jnp.zeros((8, 128), f32)
+        return carry
+
+    lax.fori_loop(0, length // 16, norm_step, 0)
+    outs[1].start()
+    small_flat.finish(small_ref)
+    outs[4].start()
+
+    def settle(k, rank, source):
         for g in range(4):
-            at = g * 512 + q * 128
-            pairs_ref[q, g:g + 1, :] = dgain[:, at:at + 128]
-        pairs_ref[q, 4:5, :] = jnp.where(lane1 == 0, seen, jnp.where(lane1 == 1, peak, 0.0))
-    for i, s in enumerate(steps):
-        to = mate(s)
-        put(pairs_ref.at[rank_of(to) // 2], near_ref.at[i], ns.at[i], nr.at[i], to)
-    row8 = lax.broadcasted_iota(jnp.int32, (8, 128), 0)
-    lane8 = lax.broadcasted_iota(jnp.int32, (8, 128), 1)
-    top = (row8 == 4) & (lane8 == 1)
-
-    def join(a, b):
-        return jnp.where(top, jnp.maximum(a, b), a + b)
-
-    small_flat.finish(small_ref)
-    value = pairs_ref[j // 2]
-    for i, s in enumerate(steps):
-        landed(near_ref.at[i], nr.at[i], mate(s, -1))
-        value = join(value, near_ref[i])
-    sum_ref[...] = value
-    for i, to in enumerate(planes):
-        put(sum_ref, far_ref.at[i], fs.at[i], fr.at[i], to)
-
-    def settle(rank, source):
-        for s in range(2):
-            for g in range(4):
-                at = s * width * 8 + g * 1024
-                gwin_ref[:, pl.ds(pl.multiple_of(at + rank * 128, 128), 128)] = source[:, s * width + g * 128:s * width + (g + 1) * 128]
-
-    settle(j, rows_of(j))
-    for i, s in enumerate(steps):
-        src = mate(s, -1)
-        landed(slots_ref.at[i], ar.at[i], src)
-        settle(rank_of(src), slots_ref.at[i])
+            at = k * width * 8 + g * 1024
+            gwin_ref[:, pl.ds(pl.multiple_of(at + rank * 128, 128), 128)] = source[:, g * 128:(g + 1) * 128]
+
+    for k in (1, 0):
+        settle(k, j, rows_of(k, j))
+        for i, s in enumerate(steps):
+            src = mate(s, -1)
+            landed(slots_ref.at[k, i], ar.at[7 * k + i], src)
+            settle(k, rank_of(src), slots_ref.at[k, i])
+    outs[2].start()
+    value = sum_ref[...]
     for i, to in enumerate(planes):
         landed(far_ref.at[i], fr.at[i], to)
         value = join(value, far_ref[i])
     tiny_ref[...] = value
+    outs[5].start()
     for i, to in enumerate(planes):
         sent(sum_ref, fs.at[i], to)
     for i, s in enumerate(steps):
         sent(near_ref.at[i], ns.at[i], mate(s))
     for copy in pending:
         copy.wait_send()
-    for flat in (gwin_flat, gwout_flat, small_flat):
+    for flat in (*flats, gwout_flat, small_flat):
         flat.close()
+    for copy in outs:
+        copy.wait()
 
 
 def k3(part, stat, smalls, vecs, gains, gwdt, masks, tokens, upstream, m, mt, dg, dv, slope, u, vt, xnt, win, wout, ups):
@@ -1347,11 +1417,19 @@
             like((8, 128), f32),
         ),
         in_specs=[here] * 9 + [far] * 11,
-        out_specs=(here,) * 6,
+        out_specs=(pl.BlockSpec(memory_space=pltpu.HBM),) * 6,
         scratch_shapes=[
-            pltpu.VMEM((2, 4, length, model), bf16),
+            pltpu.VMEM((length, model), bf16),
+            pltpu.VMEM((length, model), bf16),
+            pltpu.VMEM((own_d, 16 * channels), bf16),
+            pltpu.VMEM((128, model), f32),
+            pltpu.VMEM((160, 384), f32),
+            pltpu.VMEM((8, 128), f32),
+            dma(6),
             pltpu.VMEM((2, 4, length, model), bf16),
             pltpu.VMEM((4, 512, 2 * channels), bf16),
+            pltpu.VMEM((4, 512, channels), bf16),
+            pltpu.VMEM((4, 512, channels), bf16),
             pltpu.VMEM((4, 128, model), bf16),
             pltpu.VMEM((4, 160, 384), f32),
             pltpu.VMEM((count, channels), bf16),
@@ -1362,19 +1440,59 @@
             pltpu.VMEM(u.shape, f32),
             pltpu.VMEM((model, count), bf16),
             pltpu.VMEM((count, 256), bf16),
-            pltpu.VMEM((7, own_d, 2 * channels), bf16),
+            pltpu.VMEM((2, 7, own_d, channels), bf16),
             pltpu.VMEM((length, model), f32),
             pltpu.VMEM((7, 8, 128), f32),
-            pltpu.VMEM((4, 8, 128), f32),
+            pltpu.VMEM((8, 128), f32),
             pltpu.VMEM((8, 128), f32),
             pltpu.VMEM((3, 8, 128), f32),
-            dma(11), dma(7), dma(7), dma(7), dma(7), dma(3), dma(3),
+            dma(18), dma(14), dma(14), dma(7), dma(7), dma(3), dma(3),
             pltpu.VMEM((packed, 128), f32),
         ] + [pltpu.VMEM((packed // 2, 128), f32)] * 6 + [dma(PIECES) for _ in range(8)]
         + row_scratch(length, model) * 2
-        + flat_scratch(512, 2 * channels, bf16) + flat_scratch(128, model, bf16) + flat_scratch(160, 384, f32),
+        + flat_scratch(512, channels, bf16) * 2 + flat_scratch(128, model, bf16) + flat_scratch(160, 384, f32),
         compiler_params=pltpu.CompilerParams(collective_id=1, has_side_effects=True, vmem_limit_bytes=63400000),
     )(part, stat, smalls, vecs, gains, gwdt, masks, tokens, upstream, m, mt, dg, dv, slope, u, vt, xnt, win, wout, ups)
+
+
+def k4_kernel(slots, block_in, gtok_in, gwin_in, gwout_in, small_in, tiny_in, win_ref, gain_ref,
+              block_ref, gtok_ref, gain_out, gwin_ref, convw_ref, convb_ref, gwx_ref, gwdt_ref, dtb_ref, skip_ref, gwout_ref, mean_ref, peak_ref):
+    block_ref[0] = block_in[...]
+    gtok_ref[0] = gtok_in[...]
+    gwout_ref[...] = gwout_in[...]
+    depth, total = gwin_in.shape
+    dot = jnp.zeros((depth, 128), f32)
+    for at in range(0, total, 128):
+        value = gwin_in[:, at:at + 128].astype(f32)
+        gwin_ref[:, at:at + 128] = value
+        dot = dot + value * win_ref[:, at:at + 128].astype(f32)
+    column = jnp.broadcast_to(jnp.sum(dot, axis=1, keepdims=True), (depth, 128))
+    gain_out[...] = column.T[0:1, :] / gain_ref[...].astype(f32)
+    gwx_ref[...] = small_in[0:128, 0:256].T[0:gwx_ref.shape[0], :]
+    gwdt_ref[...] = small_in[0:128, 256:384]
+    convw_ref[...] = small_in[128:132, 0:128]
+    convb_ref[...] = small_in[132:133, 0:128]
+    dtb_ref[...] = small_in[133:134, 0:128]
+    skip_ref[...] = small_in[134:135, 0:128]
+    mean_ref[...] = tiny_in[0:1, 0:1] * (1.0 / slots)
+    peak_ref[...] = tiny_in[0:1, 1:2]
+
+
+def k4(slots, block, gtok, gwin, gwout, small, tiny, w_in, gain, columns):
+    like = jax.ShapeDtypeStruct
+    here = pl.BlockSpec(memory_space=pltpu.VMEM)
+    row = like((1, 128), f32)
+    return pl.pallas_call(
+        functools.partial(k4_kernel, slots),
+        out_shape=(
+            like((1,) + block.shape, bf16), like((1,) + gtok.shape, bf16), like(gain.shape, f32), like(gwin.shape, f32),
+            like((4, 128), f32), row, like((columns, 128), f32), like((128, 128), f32), row, row, like(gwout.shape, f32),
+            like((1, 1), f32), like((1, 1), f32),
+        ),
+        in_specs=[here] * 8,
+        out_specs=(here,) * 13,
+        compiler_params=pltpu.CompilerParams(vmem_limit_bytes=63400000),
+    )(block, gtok, gwin, gwout, small, tiny, w_in, gain)
 
 def masks(lengths, count):
     ends = jnp.cumsum(lengths, axis=1)
@@ -1513,16 +1631,6 @@
     )
 
 
-def prepare(gain, lengths, w_in, conv_w, conv_b, w_x, w_dt, dt_bias, skip, ways, groups):
-    own_d, own_e = w_in.shape[0], conv_w.shape[0]
-    channels = own_e * groups
-    cols = w_in.reshape(own_d, 2, groups, ways, own_e).transpose(3, 0, 1, 2, 4).reshape(ways, own_d, 2 * channels)
-    small = jnp.concatenate([jnp.pad(w_x, ((0, 0), (0, 256 - w_x.shape[1]))), w_dt], axis=1)
-    top = jnp.concatenate([jnp.tile(gain.astype(f32), 2)[None], jnp.pad(lengths.astype(f32), ((0, 0), (0, 123))), jnp.zeros((6, 128), f32)])
-    low = jnp.concatenate([conv_w.astype(f32).T, conv_b.astype(f32)[None], dt_bias.astype(f32)[None], skip.astype(f32)[None], jnp.zeros((1, own_e), f32)])
-    return cols, small, jnp.concatenate([top, low])
-
-
 def on_device_direct(tokens, lengths, gain, w_in, conv_w, conv_b, w_x, w_dt, dt_bias, skip, w_out, grad_out):
     groups, ways = 4, 8
     length, model = tokens.shape[1:]
@@ -1532,29 +1640,18 @@
     channels = inner // ways
     rank = w_dt.shape[1]
     states = (w_x.shape[1] - rank) // 2
-    cols, small, meta = prepare(gain, lengths, w_in, conv_w, conv_b, w_x, w_dt, dt_bias, skip, ways, groups)
-    xnt, ups, win, wout, smalls, vecs, gains, masks, live, u, g, v, vt, slope, dl, kq = k1(tokens, grad_out, cols, w_out, small, meta)
+    small = jnp.concatenate([jnp.pad(w_x, ((0, 0), (0, 256 - w_x.shape[1]))), w_dt], axis=1)
+    vec = jnp.stack([conv_b, dt_bias, skip])
+    gain = gain[None]
+    xnt, ups, win, wout, smalls, vecs, gains, masks, live, u, g, v, vt, slope, dl, kq = k1(tokens, grad_out, w_in, w_out, small, gain, lengths, conv_w.T, vec)
     m, mt, dg, gwdt, dv, part, stat = k2(dl, kq, smalls, vecs, masks, live, v, g, ups, wout, states)
-    block_out, grad_tokens, grad_win, grad_wout, small_grad, tiny = k3(
+    sums = k3(
         part, stat, smalls, vecs, gains, gwdt, masks, tokens, grad_out, m, mt, dg, dv, slope, u, vt, xnt,
-        win.reshape(groups, ways * own_d, 2 * channels), wout.reshape(groups, own_e, model), ups.reshape(2, 4, length, model))
-    d, c, z = place()
-    grad_gain = lax.dynamic_slice(tiny, (d, lax.rem(z, 2) * own_d), (1, own_d))[0]
-    vectors = small_grad[own_e:own_e + 8, :own_e]
+        win.reshape(groups, ways * own_d, 2 * channels), wout.reshape(groups, own_e, model), ups)
+    block_out, grad_tokens, grad_gain, grad_win, convw, convb, gwx, gwdt, dtb, dskip, grad_wout, mean, peak = k4(
+        float(groups * ways * length * inner), *sums, w_in, gain, rank + 2 * states)
     return (
-        block_out[None],
-        grad_tokens[None],
-        grad_gain,
-        grad_win.astype(f32),
-        vectors[:4].T,
-        vectors[4],
-        small_grad[:own_e, :rank + 2 * states],
-        small_grad[:own_e, 256:],
-        vectors[5],
-        vectors[6],
-        grad_wout,
-        tiny[4, 0] / float(groups * ways * length * inner),
-        tiny[4, 1],
+        block_out, grad_tokens, grad_gain[0], grad_win, convw.T, convb[0], gwx.T, gwdt, dtb[0], dskip[0], grad_wout, mean[0, 0], peak[0, 0],
     )
 
 

time: 346 us -> 292 us (0.84)
  Pallas kernels: 322 us -> 288 us
  local copies, waits for them, and re-layouts: 13.2 us -> 0.87 us
    pallas_call x1, Pallas kernels: 135 us -> 113 us  [k3(): pl.pallas_call(k3_kernel, out_shape=(like((length, model), bf16), like((l...]
    pallas_call x1, Pallas kernels: 127 us -> 110 us  [k1(): pl.pallas_call(k1_kernel, out_shape=(like((model, count), bf16), like((co...]
    pallas_call x0 -> x1, Pallas kernels: none -> 4.61 us  [k4(): pl.pallas_call(functools.partial(k4_kernel, slots), out_shape=(like((1,)...]
    unnamed x18 -> x1, local copies, waits for them, and re-layouts: 4.92 us -> 0.87 us
where the time goes in v5:
time: 292 us
  Pallas kernels  288 us (99%)
    pallas_call x1, Pallas kernels, k3(): pl.pallas_call(k3_kernel, out_shape=(like((length, model), bf16), like((l...  113 us
    pallas_call x1, Pallas kernels, k1(): pl.pallas_call(k1_kernel, out_shape=(like((model, count), bf16), like((co...  110 us
    pallas_call x1, Pallas kernels, k2(): pl.pallas_call(functools.partial(k2_kernel, states), grid=(channels // wi...  59.6 us

profile of v5, /device:TPU:8, one launch (start us, length us, event | category | flops | bytes accessed | tf_op | source)
XLA Modules:
  0.0 292.0 jit_solution(8097601897595119368)
XLA Ops:
  0.6 1.3 pad_maximum_fusion.vec_ref
  1.9 0.9 copy.25
  2.8 1.4 fusion.1.small_ref
  4.2 110.4 %shard_map.219 = (bf16[2048,1024]{1,0:T(8,128)(2,1)}, bf16[1024,2048]{1,0:T(8,128)(2,1)}, bf16[2048,1024]{1,0:T(8,128)(2,1)}, bf16[512,2048]{1,0:T(8,128)(2,1)},...) custom-call(bf16[1,128,2048]{2,1,0:T(8,128)(2,1)} %tok_ref.3, ...), custom_call_target="tpu_custom_call" | custom-call | tf_op jit(solution)/shard_map/pallas_call | solution.py:669
  114.6 59.6 %shard_map.220 = (bf16[1024,512]{1,0:T(8,128)(2,1)}, bf16[512,1024]{1,0:T(8,128)(2,1)}, bf16[1024,512]{1,0:T(8,128)(2,1)}, f32[512,128]{1,0:T(8,128)}, f32[4,102...) custom-call(bf16[1024,128]{1,0:T(8,128)(2,1)} %get-tuple-element.55.dl_ref, ...), custom_call_target="tpu_custom_call" | custom-call | tf_op jit(solution)/shard_map/pallas_call | solution.py:945
  174.3 113.2 %shard_map.221 = (bf16[128,2048]{1,0:T(8,128)(2,1)}, bf16[128,2048]{1,0:T(8,128)(2,1)}, bf16[64,8192]{1,0:T(8,128)(2,1)}, f32[128,2048]{1,0:T(8,128)}, f32[160,384]{1,0:T(8,128)}, /*index=5*/f32[8,128]{1,0:T(8,128)}) custom-call(f32[1280,128]{1,0:T(8,128)} %get-tuple-element.65.part_ref, f32[8,512]{1,0:T(8,128)} %get-tuple-element.66.stat_ref, ...), custom_call_target="tpu_custom_call" | custom-call | tf_op jit(solution)/shard_map/pallas_call | solution.py:1409
  287.4 4.6 %shard_map.222 = (bf16[1,128,2048]{2,1,0:T(8,128)(2,1)}, bf16[1,128,2048]{2,1,0:T(8,128)(2,1)}, f32[1,64]{1,0:T(1,128)}, f32[64,8192]{1,0:T(8,128)}, f32[4,128]{...) custom-call(bf16[128,2048]{1,0:T(8,128)(2,1)} %get-tuple-element.78., ...), custom_call_target="tpu_custom_call" | custom-call | tf_op jit(solution)/shard_map/pallas_call | solution.py:1485

commit v6 on v5

--- a/solution.py
+++ b/solution.py
@@ -226,10 +226,13 @@
 PIECES = 4
 
 
-def k1_kernel(tok_ref, up_ref, w_ref, wout_ref, small_ref, gain_ref, lens_ref, convw_ref, vec_ref,
+UP_HOPS = 2
+
+
+def k1_kernel(tok_ref, up_ref, w_ref, wout_ref, wx_ref, wdt_ref, gain_ref, lens_ref, convw_ref, convb_ref, dtb_ref, skip_ref,
               xnt_out, ups_ref, win_out, wouts_ref, smalls_ref, vecs_ref, gains_ref, masks_out, live_out,
               u_out, g_out, v_out, vt_out, slope_out, dl_ref, kq_ref,
-              masks_ref, live_ref, u_ref, g_ref, v_ref, vt_ref, slope_ref, save_sem, cols_ref, meta_ref,
+              masks_ref, live_ref, u_ref, g_ref, v_ref, vt_ref, slope_ref, save_sem, cols_ref, meta_ref, small_ref,
               xs_ref, xn_ref, xnt_ref, win_ref, metas_ref, part_ref, out_ref, sib_ref, base_ref, left_ref, right_ref, tor_ref, tol_ref,
               own_sem, ms, mr, qs, qr, xls, xlr, xrs, xrr, xcs, xcr, as_, ar, ps, pr, rs, rr, ws, wr, ts, tr, tls, tlr, trs, trr, tos, tor):
     d, c, z = place()
@@ -251,7 +254,14 @@
     meta_ref[0:1, depth:2 * depth] = gain_ref[...].astype(f32)
     meta_ref[1:2, 0:5] = lens_ref[...].astype(f32)
     meta_ref[8:12, :] = convw_ref[...].astype(f32)
-    meta_ref[12:15, :] = vec_ref[...].astype(f32)
+    meta_ref[12:13, :] = convb_ref[...].astype(f32)
+    meta_ref[13:14, :] = dtb_ref[...].astype(f32)
+    meta_ref[14:15, :] = skip_ref[...].astype(f32)
+    narrow_rows = wx_ref.shape[0]
+    small_ref[:, 0:128] = wx_ref[0:128, :].astype(f32).T.astype(bf16)
+    tail = jnp.concatenate([wx_ref[128:narrow_rows, :].astype(f32), jnp.zeros((256 - narrow_rows, 128), f32)], axis=0)
+    small_ref[:, 128:256] = tail.T.astype(bf16)
+    small_ref[:, 256:384] = wdt_ref[...]
     greet([mate(s) for s in steps] + [xn, yn, dn])
     tiles = u_ref.shape[0]
     width = tiles * 128
@@ -306,13 +316,16 @@
         def _():
             put(ref.at[0], out.at[rows(j)], xrs.at[base], xrr.at[base], left)
 
-    def row_hop(out, base, i, then=None):
+    def row_hop(out, base, i, then=None, hops=3):
+        if i >= hops:
+            return
+
         @pl.when(z > i)
         def _():
             at = z - 1 - i
             slot = out.at[rows(c * 4 + at)]
             landed(slot, xlr.at[base + i], left)
-            if i < 2:
+            if i < hops - 1:
                 @pl.when(z < 3)
                 def _():
                     put(slot, slot, xls.at[base + i + 1], xlr.at[base + i + 1], right)
@@ -325,7 +338,7 @@
             at = z + 1 + i
             slot = out.at[rows(c * 4 + at)]
             landed(slot, xrr.at[base + i], right)
-            if i < 2:
+            if i < hops - 1:
                 @pl.when(z > 0)
                 def _():
                     put(slot, slot, xrs.at[base + i + 1], xrr.at[base + i + 1], left)
@@ -333,8 +346,8 @@
             if then is not None:
                 then(c * 4 + at)
 
-    def row_end(out, base):
-        for i in range(3):
+    def row_end(out, base, hops=3):
+        for i in range(hops):
             @pl.when((z < 3) & (z >= i))
             def _():
                 sent(out.at[rows(j)], xls.at[base + i], right)
@@ -343,7 +356,7 @@
             def _():
                 sent(out.at[rows(j)], xrs.at[base + i], left)
         for at in range(4):
-            @pl.when(z != at)
+            @pl.when((z != at) & (z <= at + hops) & (at <= z + hops))
             def _():
                 sent(out.at[rows(j)], xcs.at[base + at], sib)
 
@@ -509,7 +522,7 @@
         copy.start()
 
     def early():
-        row_hop(ups_ref, 4, 0)
+        row_hop(ups_ref, 4, 0, None, UP_HOPS)
 
     def between():
         spread(g_ref, 0, width)
@@ -525,7 +538,7 @@
 
         lax.fori_loop(0, model // 128, turn_x, 0)
         own[6].start()
-        row_hop(ups_ref, 4, 1)
+        row_hop(ups_ref, 4, 1, None, UP_HOPS)
 
         def turn_v(i, carry):
             r = pl.ds(pl.multiple_of(i * 128, 128), 128)
@@ -541,13 +554,16 @@
     for b in range(4):
         packed = out_ref[count:count + quarter, :]
         kq_ref[b * quarter:(b + 1) * quarter, :] = pltpu.roll(packed, 128 - 32 * b, 1) if b else packed
-    row_hop(ups_ref, 4, 2)
+    row_hop(ups_ref, 4, 2, None, UP_HOPS)
     for at in range(4):
-        landed(ups_ref.at[rows(flip(c, 1) * 4 + at)], xcr.at[4 + at], sib)
+        @pl.when((z <= at + UP_HOPS) & (at <= z + UP_HOPS))
+        def _():
+            landed(ups_ref.at[rows(flip(c, 1) * 4 + at)], xcr.at[4 + at], sib)
+
     landed(wouts_ref.at[part_e(dd, 0, halves)], wr.at[2], yn)
     landed(wouts_ref.at[part_e(dd, halves, halves)], wr.at[3], xn)
     row_end(xs_ref, 0)
-    row_end(ups_ref, 4)
+    row_end(ups_ref, 4, UP_HOPS)
     own[1].wait()
     for copy in saves:
         copy.wait()
@@ -653,8 +669,9 @@
             sent(base_ref.at[cut(p)], ls.at[p], left)
 
 
-def k1(tokens, upstream, w_in, w_out, small, gain, lengths, conv_w, vec):
+def k1(tokens, upstream, w_in, w_out, w_x, w_dt, gain, lengths, conv_w, conv_b, dt_bias, skip):
     groups, ways = 4, 8
+    small = jax.ShapeDtypeStruct((128, 384), bf16)
     cols = jax.ShapeDtypeStruct((ways, w_in.shape[0], w_in.shape[1] // ways), bf16)
     meta = jax.ShapeDtypeStruct((16, 128), f32)
     like = jax.ShapeDtypeStruct
@@ -686,7 +703,7 @@
             like((count, 128), bf16),
             like((count, 128), f32),
         ),
-        in_specs=[some] * 2 + [here, some, some] + [here] * 4,
+        in_specs=[some] * 2 + [here, some] + [here] * 8,
         out_specs=(far,) * 4 + (here,) * 3 + (far,) * 7 + (here,) * 2,
         scratch_shapes=[
             pltpu.VMEM((3, count + 32, 128), f32),
@@ -699,6 +716,7 @@
             dma(7),
             pltpu.VMEM(cols.shape, bf16),
             pltpu.VMEM(meta.shape, f32),
+            pltpu.VMEM(small.shape, bf16),
             pltpu.VMEM((count, model), bf16),
             pltpu.VMEM((count, model), bf16),
             pltpu.VMEM((model, count), bf16),
@@ -710,15 +728,15 @@
         + [dma(8), dma(7), dma(7), dma(3), dma(3), dma(8), dma(8), dma(8), dma(8), dma(8), dma(8), dma(7), dma(7), dma(19), dma(19), dma(8), dma(8), dma(4), dma(4)]
         + [dma(PIECES) for _ in range(8)],
         compiler_params=pltpu.CompilerParams(collective_id=0, has_side_effects=True, vmem_limit_bytes=56 * 1024 * 1024),
-    )(tokens, upstream, w_in, w_out, small, gain, lengths, conv_w, vec)
+    )(tokens, upstream, w_in, w_out, w_x, w_dt, gain, lengths, conv_w, conv_b, dt_bias, skip)
 
 
 GROUP = 4
 
 
-def k2_kernel(states, dl_ref, kq_ref, wdt_ref, vecs_ref, keep_ref, live_ref, v_ref, g_ref, ups_ref, wout_ref,
-              m_ref, mt_ref, dg_ref, gwdt_ref, dv_ref, part_ref, stat_ref,
-              dpre_ref, s_ref, h_ref, rate_ref, w_ref, y_ref, dm_ref, kb_ref, hot_ref, drr_ref):
+def k2_kernel(states, dl_ref, kq_ref, wdt_ref, vecs_ref, keep_ref, live_ref, v_ref, g_ref, ups_any, wout_ref,
+              m_ref, mt_ref, dg_ref, gwdt_ref, ups_out, dv_ref, part_ref, stat_ref,
+              ups_ref, loads, stores, zs, zr, cs, cr, dpre_ref, s_ref, h_ref, rate_ref, w_ref, y_ref, dm_ref, kb_ref, hot_ref, drr_ref):
     tiles, count = v_ref.shape[:2]
     steps = count // 8
     wide = states * 128
@@ -727,6 +745,61 @@
     half = pl.program_id(0)
     both = range(tiles)
     rank = wdt_ref.shape[1]
+
+    length = count // 8
+    d, c, z = place()
+    sib = (d, flip(c, 1), z)
+    left = (d, c, lax.rem(z + 3, 4))
+    right = (d, c, lax.rem(z + 1, 4))
+
+    def rows(rank):
+        return pl.ds(pl.multiple_of(rank * length, length), length)
+
+    keeps = [pltpu.make_async_copy(ups_ref.at[r // 4, r % 4], ups_out.at[rows(r)], stores.at[r]) for r in range(8)]
+
+    def arrive(act):
+        for rank in range(8):
+            at = rank % 4
+            here = jnp.logical_not(((z == 0) & (at == 3)) | ((z == 3) & (at == 0))) if at in (0, 3) else None
+            copy = pltpu.make_async_copy(ups_any.at[rows(rank)], ups_ref.at[rank // 4, at], loads.at[rank])
+            if here is None:
+                act(copy)
+            else:
+                @pl.when(here)
+                def _():
+                    act(copy)
+
+    @pl.when(first)
+    def _():
+        arrive(lambda copy: copy.start())
+        greet([sib, left, right])
+
+        @pl.when(z == 1)
+        def _():
+            put(ups_any.at[rows(c * 4 + 3)], ups_ref.at[c, 3], zs, zr, left)
+
+        @pl.when(z == 2)
+        def _():
+            put(ups_any.at[rows(c * 4)], ups_ref.at[c, 0], zs, zr, right)
+
+    def complete():
+        for end, source, at in ((0, right, 3), (3, left, 0)):
+            @pl.when(z == end)
+            def _():
+                slot = ups_ref.at[c, at]
+                landed(slot, zr, source)
+                put(slot, slot, cs, cr, sib)
+                landed(ups_ref.at[flip(c, 1), at], cr, sib)
+                sent(slot, cs, sib)
+
+        for end, target, at in ((1, left, 3), (2, right, 0)):
+            @pl.when(z == end)
+            def _():
+                sent(ups_any.at[rows(c * 4 + at)], zs, target)
+
+        arrive(lambda copy: copy.wait())
+        for copy in keeps:
+            copy.start()
 
     @pl.when(first)
     def _():
@@ -750,17 +823,15 @@
 
     lax.fori_loop(0, count // chunk, spread, 0)
     cols = (((1,), (1,)), ((), ()))
-    length = count // 8
 
     def gate_step(i, carry):
-        r = pl.ds(pl.multiple_of(i * chunk, chunk), chunk)
-        product = lax.dot_general(ups_ref[r, :], wout_ref[...], cols, preferred_element_type=f32)
+        value = ups_ref[i // 2, pl.ds((i % 2) * 2, 2)].reshape(chunk, wout_ref.shape[1])
+        product = lax.dot_general(value, wout_ref[...], cols, preferred_element_type=f32)
         for j in range(chunk // length):
             for n in both:
                 dm_ref[n, pl.ds(i * (chunk // length) + j, length, stride=8), :] = product[j * length:(j + 1) * length, n * 128:(n + 1) * 128]
         return carry
 
-    lax.fori_loop(0, count // chunk, gate_step, 0)
     bias = vecs_ref[5:6, :]
     skip = vecs_ref[6:7, :]
     tile_of = lambda x, n: x[:, n * 128:(n + 1) * 128]
@@ -778,11 +849,6 @@
             part = 1.0 / (1.0 + beta * sk)
             rate_ref[n, r, :] = beta * part
             w_ref[n, r, :] = part * part * beta * (1.0 - beta)
-            g = g_ref[n, r, :]
-            sg = jax.nn.sigmoid(g)
-            dm = dm_ref[n, r, :] * live
-            dv_ref[n, r, :] = dm * (g * sg)
-            dm_ref[n, r, :] = dm * (sg * (1.0 + g * (1.0 - sg)))
             shown = (beta * live).reshape(16, 8, 128)
             seen[n] = seen[n] + jnp.sum(shown, axis=0)
             seen[tiles + n] = jnp.maximum(seen[tiles + n], jnp.max(shown, axis=0))
@@ -837,6 +903,28 @@
 
     lax.fori_loop(0, steps // GROUP, forward, 0)
     h_ref[...] = jnp.zeros_like(h_ref)
+
+    @pl.when(first)
+    def _():
+        complete()
+
+    lax.fori_loop(0, count // chunk, gate_step, 0)
+
+    def gates(i, carry):
+        r = pl.ds(pl.multiple_of(i * 32, 32), 32)
+        live = live_ref[0, r, :]
+        for n in both:
+            g = g_ref[n, r, :]
+            sg = jax.nn.sigmoid(g)
+            silu = g * sg
+            y = y_ref[n, r, :]
+            dm = dm_ref[n, r, :] * live
+            dv_ref[n, r, :] = dm * silu
+            dm_ref[n, r, :] = dm * y * (sg * (1.0 + g * (1.0 - sg)))
+            y_ref[n, r, :] = y * silu * live
+        return carry
+
+    lax.fori_loop(0, count // 32, gates, 0, unroll=2)
 
     def backward(step, carry):
         i = steps // GROUP - 1 - step
@@ -896,13 +984,8 @@
 
     def after(i, carry):
         r = pl.ds(pl.multiple_of(i * 128, 128), 128)
-        live = live_ref[0, r, :]
         sums = list(carry)
         for n in both:
-            y = y_ref[n, r, :]
-            g = g_ref[n, r, :]
-            y_ref[n, r, :] = y * (g * jax.nn.sigmoid(g)) * live
-            dm_ref[n, r, :] = y * dm_ref[n, r, :]
             low = w_ref[n, r, :].astype(bf16)
             dpre_ref[r, n * 128:(n + 1) * 128] = low
             sums[n] = sums[n] + jnp.sum(low.astype(f32).reshape(16, 8, 128), axis=0)
@@ -923,6 +1006,11 @@
 
     lax.fori_loop(0, 8, by_row, 0)
     gwdt_ref[...] = lax.dot_general(dpre_ref[...], dl_ref[...], (((0,), (0,)), ((), ())), preferred_element_type=f32)
+    @pl.when(jnp.logical_not(first))
+    def _():
+        for copy in keeps:
+            copy.wait()
+
     stat_ref[...] = jnp.zeros_like(stat_ref)
     for n in both:
         lanes = slice(n * 128, (n + 1) * 128)
@@ -950,6 +1038,7 @@
             like((channels, count), bf16),
             like((count, channels), bf16),
             like((channels, rank), f32),
+            like(ups.shape, bf16),
             like(v.shape, f32),
             like((count + count // 4, 128), f32),
             like((8, channels), f32),
@@ -960,17 +1049,21 @@
             pl.BlockSpec((8, width), lambda h: (0, h)),
             pl.BlockSpec((1, count, 128), lambda h: (0, 0, 0), pipeline_mode=once),
             pl.BlockSpec((1, count, 128), lambda h: (0, 0, 0), pipeline_mode=once),
-            deep, deep, whole(ups),
+            deep, deep, pl.BlockSpec(memory_space=pl.ANY),
             pl.BlockSpec((width, model), lambda h: (h, 0)),
         ],
-        out_specs=(flat, pl.BlockSpec((width, count), lambda h: (h, 0)), flat, pl.BlockSpec((width, rank), lambda h: (h, 0)), deep, pl.BlockSpec((count + count // 4, 128), lambda h: (0, 0)), pl.BlockSpec((8, width), lambda h: (0, h))),
+        out_specs=(flat, pl.BlockSpec((width, count), lambda h: (h, 0)), flat, pl.BlockSpec((width, rank), lambda h: (h, 0)), pl.BlockSpec(memory_space=pltpu.HBM), deep, pl.BlockSpec((count + count // 4, 128), lambda h: (0, 0)), pl.BlockSpec((8, width), lambda h: (0, h))),
         scratch_shapes=[
+            pltpu.VMEM((2, 4, count // 8, model), bf16),
+            pltpu.SemaphoreType.DMA((8,)),
+            pltpu.SemaphoreType.DMA((8,)),
+        ] + [pltpu.SemaphoreType.DMA(())] * 4 + [
             pltpu.VMEM((count, width), bf16),
             pltpu.VMEM((count // 8 // GROUP + 1, GROUP, states, 8, width), f32),
             pltpu.VMEM((states, 8, width), f32),
         ] + [pltpu.VMEM((tiles, count, 128), f32)] * 4
         + [pltpu.VMEM((count, 2 * states * 128), f32), pltpu.VMEM((128, 2 * states * 128), bf16), pltpu.VMEM((count, 128), f32)],
-        compiler_params=pltpu.CompilerParams(vmem_limit_bytes=60 * 1024 * 1024),
+        compiler_params=pltpu.CompilerParams(collective_id=2, has_side_effects=True, vmem_limit_bytes=63400000),
     )(dl, kq, smalls, vecs, masks, live, v, g, ups, wout)
 
 
@@ -1640,11 +1733,10 @@
     channels = inner // ways
     rank = w_dt.shape[1]
     states = (w_x.shape[1] - rank) // 2
-    small = jnp.concatenate([jnp.pad(w_x, ((0, 0), (0, 256 - w_x.shape[1]))), w_dt], axis=1)
-    vec = jnp.stack([conv_b, dt_bias, skip])
     gain = gain[None]
-    xnt, ups, win, wout, smalls, vecs, gains, masks, live, u, g, v, vt, slope, dl, kq = k1(tokens, grad_out, w_in, w_out, small, gain, lengths, conv_w.T, vec)
-    m, mt, dg, gwdt, dv, part, stat = k2(dl, kq, smalls, vecs, masks, live, v, g, ups, wout, states)
+    xnt, ups, win, wout, smalls, vecs, gains, masks, live, u, g, v, vt, slope, dl, kq = k1(
+        tokens, grad_out, w_in, w_out, w_x.T, w_dt, gain, lengths, conv_w.T, conv_b[None], dt_bias[None], skip[None])
+    m, mt, dg, gwdt, ups, dv, part, stat = k2(dl, kq, smalls, vecs, masks, live, v, g, ups, wout, states)
     sums = k3(
         part, stat, smalls, vecs, gains, gwdt, masks, tokens, grad_out, m, mt, dg, dv, slope, u, vt, xnt,
         win.reshape(groups, ways * own_d, 2 * channels), wout.reshape(groups, own_e, model), ups)

time: 292 us -> 286 us (0.979)
    pallas_call x1, Pallas kernels: 110 us -> 102 us  [k1(): pl.pallas_call(k1_kernel, out_shape=(like((model, count), bf16), like((co...]
    pallas_call x1, Pallas kernels: 59.6 us -> 66.2 us  [k2(): pl.pallas_call(functools.partial(k2_kernel, states), grid=(channels // wi...]
where the time goes in v6:
time: 286 us
  Pallas kernels  286 us (100%)
    pallas_call x1, Pallas kernels, k3(): pl.pallas_call(k3_kernel, out_shape=(like((length, model), bf16), like((l...  113 us
    pallas_call x1, Pallas kernels, k1(): pl.pallas_call(k1_kernel, out_shape=(like((model, count), bf16), like((co...  102 us
    pallas_call x1, Pallas kernels, k2(): pl.pallas_call(functools.partial(k2_kernel, states), grid=(channels // wi...  66.2 us

profile of v6, /device:TPU:8, one launch (start us, length us, event | category | flops | bytes accessed | tf_op | source)
XLA Modules:
  0.0 286.3 jit_solution(2133022131973510487)
XLA Ops:
  0.6 101.5 %shard_map.219 = (bf16[2048,1024]{1,0:T(8,128)(2,1)}, bf16[1024,2048]{1,0:T(8,128)(2,1)}, bf16[2048,1024]{1,0:T(8,128)(2,1)}, bf16[512,2048]{1,0:T(8,128)(2,1)},...) custom-call(bf16[1,128,2048]{2,1,0:T(8,128)(2,1)} %tok_ref.3, ...), custom_call_target="tpu_custom_call" | custom-call | tf_op jit(solution)/shard_map/pallas_call | solution.py:686
  102.2 66.2 %shard_map.220 = (bf16[1024,512]{1,0:T(8,128)(2,1)}, bf16[512,1024]{1,0:T(8,128)(2,1)}, bf16[1024,512]{1,0:T(8,128)(2,1)}, f32[512,128]{1,0:T(8,128)}, bf16[1024...) custom-call(bf16[1024,128]{1,0:T(8,128)(2,1)} %get-tuple-element.56.dl_ref, ...), custom_call_target="tpu_custom_call" | custom-call | tf_op jit(solution)/shard_map/pallas_call | solution.py:1033
  168.4 113.3 %shard_map.221 = (bf16[128,2048]{1,0:T(8,128)(2,1)}, bf16[128,2048]{1,0:T(8,128)(2,1)}, bf16[64,8192]{1,0:T(8,128)(2,1)}, f32[128,2048]{1,0:T(8,128)}, f32[160,384]{1,0:T(8,128)}, /*index=5*/f32[8,128]{1,0:T(8,128)}) custom-call(f32[1280,128]{1,0:T(8,128)} %get-tuple-element.66.part_ref, f32[8,512]{1,0:T(8,128)} %get-tuple-element.67.stat_ref, ...), custom_call_target="tpu_custom_call" | custom-call | tf_op jit(solution)/shard_map/pallas_call | solution.py:1502
  281.7 4.6 %shard_map.222 = (bf16[1,128,2048]{2,1,0:T(8,128)(2,1)}, bf16[1,128,2048]{2,1,0:T(8,128)(2,1)}, f32[1,64]{1,0:T(1,128)}, f32[64,8192]{1,0:T(8,128)}, f32[4,128]{...) custom-call(bf16[128,2048]{1,0:T(8,128)(2,1)} %get-tuple-element.80., ...), custom_call_target="tpu_custom_call" | custom-call | tf_op jit(solution)/shard_map/pallas_call | solution.py:1578

commit v7 on v6

--- a/solution.py
+++ b/solution.py
@@ -734,9 +734,9 @@
 GROUP = 4
 
 
-def k2_kernel(states, dl_ref, kq_ref, wdt_ref, vecs_ref, keep_ref, live_ref, v_ref, g_ref, ups_any, wout_ref,
-              m_ref, mt_ref, dg_ref, gwdt_ref, ups_out, dv_ref, part_ref, stat_ref,
-              ups_ref, loads, stores, zs, zr, cs, cr, dpre_ref, s_ref, h_ref, rate_ref, w_ref, y_ref, dm_ref, kb_ref, hot_ref, drr_ref):
+def k2_kernel(states, dl_ref, kq_ref, wdt_ref, vecs_ref, keep_ref, live_ref, v_ref, g_ref, ups_any, wout_any,
+              acc_out, mt_ref, dg_ref, gwdt_ref, ups_out, dv_ref, part_ref, stat_ref,
+              ups_ref, loads, stores, zs, zr, cs, cr, ls, lr, ss, sr, m_ref, wout_ref, acc_ref, recv_ref, dpre_ref, s_ref, h_ref, rate_ref, w_ref, y_ref, dm_ref, kb_ref, hot_ref, drr_ref):
     tiles, count = v_ref.shape[:2]
     steps = count // 8
     wide = states * 128
@@ -744,6 +744,7 @@
     first = pl.program_id(0) == 0
     half = pl.program_id(0)
     both = range(tiles)
+    width = tiles * 128
     rank = wdt_ref.shape[1]
 
     length = count // 8
@@ -755,7 +756,7 @@
     def rows(rank):
         return pl.ds(pl.multiple_of(rank * length, length), length)
 
-    keeps = [pltpu.make_async_copy(ups_ref.at[r // 4, r % 4], ups_out.at[rows(r)], stores.at[r]) for r in range(8)]
+    keeps = [pltpu.make_async_copy(ups_ref.at[r // 4, r % 4], ups_out.at[r // 4, r % 4], stores.at[r]) for r in range(8)]
 
     def arrive(act):
         for rank in range(8):
@@ -772,6 +773,7 @@
     @pl.when(first)
     def _():
         arrive(lambda copy: copy.start())
+        pltpu.make_async_copy(wout_any, wout_ref, loads.at[8]).start()
         greet([sib, left, right])
 
         @pl.when(z == 1)
@@ -798,6 +800,7 @@
                 sent(ups_any.at[rows(c * 4 + at)], zs, target)
 
         arrive(lambda copy: copy.wait())
+        pltpu.make_async_copy(wout_any, wout_ref, loads.at[8]).wait()
         for copy in keeps:
             copy.start()
 
@@ -826,7 +829,7 @@
 
     def gate_step(i, carry):
         value = ups_ref[i // 2, pl.ds((i % 2) * 2, 2)].reshape(chunk, wout_ref.shape[1])
-        product = lax.dot_general(value, wout_ref[...], cols, preferred_element_type=f32)
+        product = lax.dot_general(value, wout_ref[pl.ds(pl.multiple_of(half * width, width), width), :], cols, preferred_element_type=f32)
         for j in range(chunk // length):
             for n in both:
                 dm_ref[n, pl.ds(i * (chunk // length) + j, length, stride=8), :] = product[j * length:(j + 1) * length, n * 128:(n + 1) * 128]
@@ -925,6 +928,51 @@
         return carry
 
     lax.fori_loop(0, count // 32, gates, 0, unroll=2)
+
+    def by_row(j, carry):
+        r = pl.ds(pl.multiple_of(j * length, length), length)
+        for n in both:
+            value = y_ref[n, pl.ds(j, length, stride=8), :]
+            m_ref[r, pl.ds(pl.multiple_of(half * width + n * 128, 128), 128)] = value.astype(bf16)
+            mt_ref[n * 128:(n + 1) * 128, r] = value.T.astype(bf16)
+            dg_ref[r, n * 128:(n + 1) * 128] = dm_ref[n, pl.ds(j, length, stride=8), :].astype(bf16)
+        return carry
+
+    lax.fori_loop(0, 8, by_row, 0)
+
+    def rows_product(core):
+        def body(i, carry):
+            lanes = pl.ds(pl.multiple_of(i * chunk, chunk), chunk)
+            product = jnp.dot(m_ref[pl.ds(pl.multiple_of(core * 4 * length, 4 * length), 4 * length), :], wout_ref[:, lanes], preferred_element_type=f32)
+            for at_z in range(4):
+                ups_ref[core, at_z, :, lanes] = product[at_z * length:(at_z + 1) * length].astype(bf16)
+            return carry
+
+        lax.fori_loop(0, wout_ref.shape[1] // chunk, body, 0)
+
+    def gather(at_z):
+        landed(acc_ref.at[at_z], sr.at[at_z], sib)
+        add_rows(acc_ref.at[at_z], [acc_ref.at[at_z], ups_ref.at[c, at_z]])
+
+    @pl.when(jnp.logical_not(first))
+    def _():
+        for copy in keeps:
+            copy.wait()
+        rows_product(flip(c, 1))
+        for at_z in (3, 0, 2, 1):
+            put(ups_ref.at[flip(c, 1), at_z], acc_ref.at[at_z], ss.at[at_z], sr.at[at_z], sib)
+        rows_product(c)
+        gather(3)
+        gather(0)
+
+        @pl.when(z == 0)
+        def _():
+            put(acc_ref.at[3], recv_ref, ls, lr, right)
+
+        @pl.when(z == 3)
+        def _():
+            put(acc_ref.at[0], recv_ref, ls, lr, left)
+
 
     def backward(step, carry):
         i = steps // GROUP - 1 - step
@@ -995,21 +1043,27 @@
 
     sums = lax.fori_loop(0, count // 128, after, (blank,) * tiles)
 
-    def by_row(j, carry):
-        r = pl.ds(pl.multiple_of(j * length, length), length)
-        for n in both:
-            value = y_ref[n, pl.ds(j, length, stride=8), :]
-            m_ref[r, n * 128:(n + 1) * 128] = value.astype(bf16)
-            mt_ref[n * 128:(n + 1) * 128, r] = value.T.astype(bf16)
-            dg_ref[r, n * 128:(n + 1) * 128] = dm_ref[n, pl.ds(j, length, stride=8), :].astype(bf16)
-        return carry
-
-    lax.fori_loop(0, 8, by_row, 0)
     gwdt_ref[...] = lax.dot_general(dpre_ref[...], dl_ref[...], (((0,), (0,)), ((), ())), preferred_element_type=f32)
+
     @pl.when(jnp.logical_not(first))
     def _():
-        for copy in keeps:
-            copy.wait()
+        gather(2)
+        gather(1)
+        for end, source, at_z in ((1, left, 3), (2, right, 0)):
+            @pl.when(z == end)
+            def _():
+                landed(recv_ref, lr, source)
+                add_rows(acc_ref.at[at_z], [acc_ref.at[at_z], recv_ref])
+
+        save = pltpu.make_async_copy(acc_ref, acc_out, loads.at[8])
+        save.start()
+        for at_z in range(4):
+            sent(ups_ref.at[flip(c, 1), at_z], ss.at[at_z], sib)
+        for end, target, at_z in ((0, right, 3), (3, left, 0)):
+            @pl.when(z == end)
+            def _():
+                sent(acc_ref.at[at_z], ls, target)
+        save.wait()
 
     stat_ref[...] = jnp.zeros_like(stat_ref)
     for n in both:
@@ -1034,11 +1088,11 @@
         functools.partial(k2_kernel, states),
         grid=(channels // width,),
         out_shape=(
-            like((count, channels), bf16),
+            like((4, count // 8, model), bf16),
             like((channels, count), bf16),
             like((count, channels), bf16),
             like((channels, rank), f32),
-            like(ups.shape, bf16),
+            like((2, 4, count // 8, model), bf16),
             like(v.shape, f32),
             like((count + count // 4, 128), f32),
             like((8, channels), f32),
@@ -1050,14 +1104,20 @@
             pl.BlockSpec((1, count, 128), lambda h: (0, 0, 0), pipeline_mode=once),
             pl.BlockSpec((1, count, 128), lambda h: (0, 0, 0), pipeline_mode=once),
             deep, deep, pl.BlockSpec(memory_space=pl.ANY),
-            pl.BlockSpec((width, model), lambda h: (h, 0)),
+            pl.BlockSpec(memory_space=pl.ANY),
         ],
-        out_specs=(flat, pl.BlockSpec((width, count), lambda h: (h, 0)), flat, pl.BlockSpec((width, rank), lambda h: (h, 0)), pl.BlockSpec(memory_space=pltpu.HBM), deep, pl.BlockSpec((count + count // 4, 128), lambda h: (0, 0)), pl.BlockSpec((8, width), lambda h: (0, h))),
+        out_specs=(pl.BlockSpec(memory_space=pltpu.HBM), pl.BlockSpec((width, count), lambda h: (h, 0)), flat, pl.BlockSpec((width, rank), lambda h: (h, 0)), pl.BlockSpec(memory_space=pltpu.HBM), deep, pl.BlockSpec((count + count // 4, 128), lambda h: (0, 0)), pl.BlockSpec((8, width), lambda h: (0, h))),
         scratch_shapes=[
             pltpu.VMEM((2, 4, count // 8, model), bf16),
+            pltpu.SemaphoreType.DMA((9,)),
             pltpu.SemaphoreType.DMA((8,)),
-            pltpu.SemaphoreType.DMA((8,)),
-        ] + [pltpu.SemaphoreType.DMA(())] * 4 + [
+        ] + [pltpu.SemaphoreType.DMA(())] * 6 + [
+            pltpu.SemaphoreType.DMA((4,)),
+            pltpu.SemaphoreType.DMA((4,)),
+            pltpu.VMEM((count, channels), bf16),
+            pltpu.VMEM((channels, model), bf16),
+            pltpu.VMEM((4, count // 8, model), bf16),
+            pltpu.VMEM((count // 8, model), bf16),
             pltpu.VMEM((count, width), bf16),
             pltpu.VMEM((count // 8 // GROUP + 1, GROUP, states, 8, width), f32),
             pltpu.VMEM((states, 8, width), f32),
@@ -1068,8 +1128,8 @@
 
 
 class Row:
-    def __init__(self, part, sib, recv, sems):
-        self.part, self.sib, self.recv = part, sib, recv
+    def __init__(self, part, sib, recv, sems, merged=False):
+        self.part, self.sib, self.recv, self.merged = part, sib, recv, merged
         self.ss, self.sr, self.gs, self.lr, self.rr = sems
         d, c, z = place()
         self.c = c
@@ -1092,10 +1152,10 @@
 
     def terms(self, zs, zp):
         found = [self.sib.at[zp]]
-        if zp >= zs and zs > 0:
+        if zp >= zs and zs > 0 and not (self.merged and (zs, zp) == (1, 3)):
             landed(self.recv.at[zp], self.lr.at[zp], self.to_left)
             found.append(self.recv.at[zp])
-        if zp <= zs and zs < 3:
+        if zp <= zs and zs < 3 and not (self.merged and (zs, zp) == (2, 0)):
             slot = self.recv.at[4 if zp == zs else zp]
             landed(slot, self.rr.at[zp], self.to_right)
             found.append(slot)
@@ -1106,12 +1166,17 @@
         if len(found) > 1:
             add_rows(self.sib.at[zp], found)
 
+    def skips(self, zs, zp):
+        return self.merged and (zs, zp) in ((0, 3), (3, 0))
+
     def step(self, zs, k):
+        k = k + 1 if self.merged else k
+        ends = 1 if self.merged else 0
         for zp in ((3, 2, 1, 0) if zs == 0 else (0, 1, 2, 3)):
-            if zp > zs and k == (0 if zs == 0 else 3 - zp + zs):
+            if zp > zs and not self.skips(zs, zp) and k == (ends if zs == 0 else 3 - zp + zs):
                 self.join(zs, zp)
                 put(self.sib.at[zp], self.recv.at[zp], self.gs.at[zp], self.lr.at[zp], self.to_right)
-            if zp < zs and k == (0 if zs == 3 else zp + 3 - zs):
+            if zp < zs and not self.skips(zs, zp) and k == (ends if zs == 3 else zp + 3 - zs):
                 self.join(zs, zp)
                 put(self.sib.at[zp], self.recv.at[4 if zp == zs - 1 else zp], self.gs.at[zp], self.rr.at[zp], self.to_left)
 
@@ -1120,7 +1185,7 @@
 
     def close(self, zs):
         for zp in range(4):
-            if zp != zs:
+            if zp != zs and not self.skips(zs, zp):
                 sent(self.sib.at[zp], self.gs.at[zp], self.other)
 
     def along(self, k, total=None):
@@ -1129,7 +1194,7 @@
         for zs in range(4):
             @pl.when(z == zs)
             def _():
-                if k < 3:
+                if k < (2 if self.merged else 3):
                     self.step(zs, k)
                 else:
                     self.finish(zs)
@@ -1206,7 +1271,7 @@
 
 
 def k3_kernel(part_ref, stat_ref, smalls_ref, vecs_ref, gains_ref, gwdt_ref, masks_ref, tok_ref, up_ref,
-              m_any, mt_any, dg_any, dv_any, slope_any, u_any, vt_any, xnt_any, win_any, wout_any, ups_any,
+              acc_any, mt_any, dg_any, dv_any, slope_any, u_any, vt_any, xnt_any, win_any, ups_any,
               block_out, gtok_out, gwin_out, gwout_out, small_out, tiny_out, *scratch):
     scratch = list(scratch)
 
@@ -1217,12 +1282,12 @@
 
     block_ref, gtok_ref, gwin_ref, gwout_ref, small_ref, tiny_ref, stores = take(7)
     outp, win_ref, up, gp, gwoutp, smallp = take(6)
-    m_ref, mt_ref, dz_ref, dc_ref, slope_ref, u_ref, xnt_ref, dp_ref, slots_ref, row_ref = take(10)
+    mt_ref, dz_ref, dc_ref, slope_ref, u_ref, xnt_ref, dp_ref, slots_ref, row_ref = take(9)
     near_ref, pairs_ref, sum_ref, far_ref = take(4)
     loads, as_, ar, ns, nr, fs, fr = take(7)
     totals = take(7)
     total_sems = take(8)
-    out_row = Row(outp, *take(2), take(5))
+    out_row = Row(None, *take(2), take(5), True)
     dxn_row = Row(outp, *take(2), take(5))
     flats = [Flat(up, *take(6)), Flat(gp, *take(6))]
     gwout_flat = Flat(gwoutp, *take(6))
@@ -1236,13 +1301,8 @@
     tiles, padded, _ = dc_ref.shape
     count = dz_ref.shape[0]
     width = tiles * 128
-    rows_any = [(m_any, m_ref), (wout_any, gwoutp), (mt_any, mt_ref)]
-    for at, holder in ((0, gp), (1024, up)):
-        for h in range(2):
-            for q in range(2):
-                rows_any.append((ups_any.at[pl.ds(q * 512, 512), pl.ds(at + h * 512, 512)], holder.at[2 * h + q]))
-    rows_any += [(dg_any, dz_ref.at[:, pl.ds(width, width)]), (xnt_any, xnt_ref), (dv_any, dc_ref.at[:, pl.ds(0, count)]),
-                 (slope_any, slope_ref), (u_any, u_ref), (win_any, win_ref)]
+    rows_any = [(dg_any, dz_ref.at[:, pl.ds(width, width)]), (xnt_any, xnt_ref), (acc_any, out_row.sib), (mt_any, mt_ref), (ups_any, outp),
+                (dv_any, dc_ref.at[:, pl.ds(0, count)]), (slope_any, slope_ref), (u_any, u_ref), (win_any, win_ref)]
     copies = [pltpu.make_async_copy(a, b, loads.at[i]) for i, (a, b) in enumerate(rows_any)]
     for copy in copies:
         copy.start()
@@ -1250,19 +1310,14 @@
     outs = [(block_ref, block_out), (gtok_ref, gtok_out), (gwin_ref, gwin_out), (gwout_ref, gwout_out), (small_ref, small_out), (tiny_ref, tiny_out)]
     outs = [pltpu.make_async_copy(a, b, stores.at[i]) for i, (a, b) in enumerate(outs)]
     tile = 256
-    nn = (((1,), (0,)), ((), ()))
     nt = (((1,), (1,)), ((), ()))
 
-    def rows_product(half, target, left, right, dims, right_rows):
+    def rows_product(half):
         def body(i, carry):
-            if right_rows:
-                group = i // (512 // tile)
-                value = right[group, pl.ds(pl.multiple_of((i % (512 // tile)) * tile, tile), tile), :]
-            else:
-                value = jnp.concatenate([right[g, :, pl.ds(pl.multiple_of(i * tile, tile), tile)] for g in range(4)], axis=0)
-            product = lax.dot_general(left[pl.ds(pl.multiple_of(half * 512, 512), 512), :], value, dims, preferred_element_type=f32)
+            value = win_ref[i // (512 // tile), pl.ds(pl.multiple_of((i % (512 // tile)) * tile, tile), tile), :]
+            product = lax.dot_general(dz_ref[pl.ds(pl.multiple_of(half * 512, 512), 512), :], value, nt, preferred_element_type=f32)
             for zp in range(4):
-                target[half, zp, :, pl.ds(pl.multiple_of(i * tile, tile), tile)] = product[zp * length:(zp + 1) * length].astype(bf16)
+                outp[half, zp, :, pl.ds(pl.multiple_of(i * tile, tile), tile)] = product[zp * length:(zp + 1) * length].astype(bf16)
             return carry
 
         lax.fori_loop(0, model // tile, body, 0)
@@ -1288,33 +1343,29 @@
         weight_rows(holder, first, d)
 
     def early():
-        copies[0].wait()
-        copies[1].wait()
-        rows_product(other, outp, m_ref, gwoutp, nn, False)
-        out_row.start()
-        rows_product(c, outp, m_ref, gwoutp, nn, False)
-
-    def between():
-        out_row.gather()
-        out_row.along(0)
-        for copy in copies[2:11]:
-            copy.wait()
-        for holder, at in ((gp, 0), (up, 1024)):
-            def body(i, carry):
-                h = i // 2
-                off = pl.ds(pl.multiple_of((i % 2) * tile, tile), tile)
-                value = jnp.concatenate([holder[2 * h, :, off], holder[2 * h + 1, :, off]], axis=0)
-                product = jnp.dot(mt_ref[...], value, preferred_element_type=f32)
-                for g in range(4):
-                    gwoutp[g, :, pl.ds(pl.multiple_of(at + i * tile, tile), tile)] = product[g * 128:(g + 1) * 128].astype(bf16)
-                return carry
-
-            lax.fori_loop(0, 4, body, 0)
-
-    def late():
-        for copy in copies[11:13]:
+        for copy in copies[0:2]:
             copy.wait()
         weight_part(1)
+
+    def between():
+        copies[2].wait()
+        out_row.along(0)
+        flats[1].middle()
+
+    def late():
+        for copy in copies[3:5]:
+            copy.wait()
+
+        def body(i, carry):
+            lanes = pl.ds(pl.multiple_of(i * tile, tile), tile)
+            product = jnp.dot(mt_ref[...], outp[:, :, :, lanes].reshape(count, tile), preferred_element_type=f32)
+            for g in range(4):
+                gwoutp[g, :, lanes] = product[g * 128:(g + 1) * 128].astype(bf16)
+            return carry
+
+        lax.fori_loop(0, model // tile, body, 0)
+        gwout_flat.start_far()
+        gwout_flat.start_near()
 
     seen = jnp.sum(stat_ref[0:1, :], axis=1, keepdims=True)
     peak = jnp.max(stat_ref[1:2, :], axis=1, keepdims=True)
@@ -1329,9 +1380,20 @@
 
     total_ref = totals[0]
     line_total(part_ref, *totals, *total_sems, early, between, late)
-    vt_copy = pltpu.make_async_copy(vt_any, mt_ref, loads.at[17])
+    vt_copy = pltpu.make_async_copy(vt_any, mt_ref, loads.at[9])
     vt_copy.start()
-    out_row.along(1)
+    block = gwin_ref.shape[0]
+    pending = []
+
+    def rows_of(k, rank):
+        return flats[k].part.at[d, pl.ds(pl.multiple_of(rank * block, block), block)]
+
+    def give(k):
+        flats[k].finish(flats[k].part.at[d])
+        for i, s in enumerate(steps):
+            to = mate(s)
+            pending.append(put(rows_of(k, rank_of(to)), slots_ref.at[k, i], as_.at[7 * k + i], ar.at[7 * k + i], to))
+
     value = pairs_ref[...]
     for i, s in enumerate(steps):
         landed(near_ref.at[i], nr.at[i], mate(s, -1))
@@ -1346,7 +1408,7 @@
         packed = total_ref[count:count + quarter, :]
         packed = pltpu.roll(packed, 128 - 32 * b, 1) if b else packed
         dp_ref[b * quarter:(b + 1) * quarter, 128:256] = jnp.where(lane < 32, packed, 0.0).astype(bf16)
-    for copy in copies[13:16]:
+    for copy in copies[5:8]:
         copy.wait()
     dc_ref[:, count:, :] = jnp.zeros((tiles, padded - count, 128), f32)
 
@@ -1358,7 +1420,8 @@
         return carry
 
     lax.fori_loop(0, count // 256, slope_step, 0)
-    flats[1].middle()
+    give(1)
+    out_row.along(1)
     taps = [vecs_ref[o:o + 1, :] for o in range(4)]
     lead = u_ref.shape[1] - count
 
@@ -1395,37 +1458,26 @@
         return carry
 
     lax.fori_loop(0, 8, by_row, 0)
-    copies[16].wait()
-    out_row.release()
-    rows_product(other, outp, dz_ref, win_ref, nt, True)
+    gwout_flat.middle()
+    copies[8].wait()
+    rows_product(other)
     dxn_row.start()
-    rows_product(c, outp, dz_ref, win_ref, nt, True)
-    out_row.along(2)
+    weight_rows(up, 0, flats[0].dd)
+    flats[0].start_far()
+    rows_product(c)
     dxn_row.gather()
     dxn_row.along(0)
-    weight_part(0)
-    block = gwin_ref.shape[0]
-    pending = []
-
-    def rows_of(k, rank):
-        return flats[k].part.at[d, pl.ds(pl.multiple_of(rank * block, block), block)]
-
-    def give(k):
-        flats[k].finish(flats[k].part.at[d])
-        for i, s in enumerate(steps):
-            to = mate(s)
-            pending.append(put(rows_of(k, rank_of(to)), slots_ref.at[k, i], as_.at[7 * k + i], ar.at[7 * k + i], to))
-
-    give(1)
-    gwout_flat.start_far()
-    gwout_flat.start_near()
+    weight_rows(up, 0, flats[0].dx)
+    weight_rows(up, 0, flats[0].dy)
+    flats[0].start_near()
+    weight_rows(up, 0, d)
     vt_copy.wait()
     for n in range(tiles):
         smallp[n, 0:128, 0:256] = jnp.dot(mt_ref[n * 128:(n + 1) * 128, :], dp_ref[...], preferred_element_type=f32)
     small_flat.start_far()
     small_flat.start_near()
     flats[0].middle()
-    out_row.along(3, row_ref)
+    out_row.along(2, row_ref)
 
     def block_step(i, carry):
         r = pl.ds(pl.multiple_of(i * 16, 16), 16)
@@ -1436,7 +1488,6 @@
     outs[0].start()
     dxn_row.along(1)
     give(0)
-    gwout_flat.middle()
     small_flat.middle()
     dxn_row.along(2)
     gwout_flat.finish(gwout_ref)
@@ -1489,10 +1540,10 @@
         copy.wait()
 
 
-def k3(part, stat, smalls, vecs, gains, gwdt, masks, tokens, upstream, m, mt, dg, dv, slope, u, vt, xnt, win, wout, ups):
+def k3(part, stat, smalls, vecs, gains, gwdt, masks, tokens, upstream, acc, mt, dg, dv, slope, u, vt, xnt, win, ups):
     like = jax.ShapeDtypeStruct
     length, model = tokens.shape[1:]
-    count, channels = m.shape
+    channels, count = mt.shape
     tiles = channels // 128
     here = pl.BlockSpec(memory_space=pltpu.VMEM)
     far = pl.BlockSpec(memory_space=pl.ANY)
@@ -1509,7 +1560,7 @@
             like((160, 384), f32),
             like((8, 128), f32),
         ),
-        in_specs=[here] * 9 + [far] * 11,
+        in_specs=[here] * 9 + [far] * 10,
         out_specs=(pl.BlockSpec(memory_space=pltpu.HBM),) * 6,
         scratch_shapes=[
             pltpu.VMEM((length, model), bf16),
@@ -1525,7 +1576,6 @@
             pltpu.VMEM((4, 512, channels), bf16),
             pltpu.VMEM((4, 128, model), bf16),
             pltpu.VMEM((4, 160, 384), f32),
-            pltpu.VMEM((count, channels), bf16),
             pltpu.VMEM((channels, count), bf16),
             pltpu.VMEM((count, 2 * channels), bf16),
             pltpu.VMEM((tiles, count + 32, 128), f32),
@@ -1539,13 +1589,13 @@
             pltpu.VMEM((8, 128), f32),
             pltpu.VMEM((8, 128), f32),
             pltpu.VMEM((3, 8, 128), f32),
-            dma(18), dma(14), dma(14), dma(7), dma(7), dma(3), dma(3),
+            dma(10), dma(14), dma(14), dma(7), dma(7), dma(3), dma(3),
             pltpu.VMEM((packed, 128), f32),
         ] + [pltpu.VMEM((packed // 2, 128), f32)] * 6 + [dma(PIECES) for _ in range(8)]
         + row_scratch(length, model) * 2
         + flat_scratch(512, channels, bf16) * 2 + flat_scratch(128, model, bf16) + flat_scratch(160, 384, f32),
         compiler_params=pltpu.CompilerParams(collective_id=1, has_side_effects=True, vmem_limit_bytes=63400000),
-    )(part, stat, smalls, vecs, gains, gwdt, masks, tokens, upstream, m, mt, dg, dv, slope, u, vt, xnt, win, wout, ups)
+    )(part, stat, smalls, vecs, gains, gwdt, masks, tokens, upstream, acc, mt, dg, dv, slope, u, vt, xnt, win, ups)
 
 
 def k4_kernel(slots, block_in, gtok_in, gwin_in, gwout_in, small_in, tiny_in, win_ref, gain_ref,
@@ -1736,10 +1786,10 @@
     gain = gain[None]
     xnt, ups, win, wout, smalls, vecs, gains, masks, live, u, g, v, vt, slope, dl, kq = k1(
         tokens, grad_out, w_in, w_out, w_x.T, w_dt, gain, lengths, conv_w.T, conv_b[None], dt_bias[None], skip[None])
-    m, mt, dg, gwdt, ups, dv, part, stat = k2(dl, kq, smalls, vecs, masks, live, v, g, ups, wout, states)
+    acc, mt, dg, gwdt, ups, dv, part, stat = k2(dl, kq, smalls, vecs, masks, live, v, g, ups, wout, states)
     sums = k3(
-        part, stat, smalls, vecs, gains, gwdt, masks, tokens, grad_out, m, mt, dg, dv, slope, u, vt, xnt,
-        win.reshape(groups, ways * own_d, 2 * channels), wout.reshape(groups, own_e, model), ups)
+        part, stat, smalls, vecs, gains, gwdt, masks, tokens, grad_out, acc, mt, dg, dv, slope, u, vt, xnt,
+        win.reshape(groups, ways * own_d, 2 * channels), ups)
     block_out, grad_tokens, grad_gain, grad_win, convw, convb, gwx, gwdt, dtb, dskip, grad_wout, mean, peak = k4(
         float(groups * ways * length * inner), *sums, w_in, gain, rank + 2 * states)
     return (

time: 286 us -> 278 us (0.972)
  Pallas kernels: 286 us -> 277 us
    pallas_call x1, Pallas kernels: 113 us -> 96.1 us  [k3(): pl.pallas_call(k3_kernel, out_shape=(like((length, model), bf16), like((l...]
    pallas_call x1, Pallas kernels: 66.2 us -> 74.5 us  [k2(): pl.pallas_call(functools.partial(k2_kernel, states), grid=(channels // wi...]
where the time goes in v7:
time: 278 us
  Pallas kernels  277 us (100%)
    pallas_call x1, Pallas kernels, k1(): pl.pallas_call(k1_kernel, out_shape=(like((model, count), bf16), like((co...  102 us
    pallas_call x1, Pallas kernels, k3(): pl.pallas_call(k3_kernel, out_shape=(like((length, model), bf16), like((l...  96.1 us
    pallas_call x1, Pallas kernels, k2(): pl.pallas_call(functools.partial(k2_kernel, states), grid=(channels // wi...  74.5 us

profile of v7, /device:TPU:8, one launch (start us, length us, event | category | flops | bytes accessed | tf_op | source)
XLA Modules:
  0.0 277.7 jit_solution(10145890381105376983)
XLA Ops:
  0.6 101.8 %shard_map.219 = (bf16[2048,1024]{1,0:T(8,128)(2,1)}, bf16[1024,2048]{1,0:T(8,128)(2,1)}, bf16[2048,1024]{1,0:T(8,128)(2,1)}, bf16[512,2048]{1,0:T(8,128)(2,1)},...) custom-call(bf16[1,128,2048]{2,1,0:T(8,128)(2,1)} %tok_ref.3, ...), custom_call_target="tpu_custom_call" | custom-call | tf_op jit(solution)/shard_map/pallas_call | solution.py:686
  102.4 74.5 %shard_map.220 = (bf16[4,128,2048]{2,1,0:T(8,128)(2,1)}, bf16[512,1024]{1,0:T(8,128)(2,1)}, bf16[1024,512]{1,0:T(8,128)(2,1)}, f32[512,128]{1,0:T(8,128)}, bf16[...) custom-call(bf16[1024,128]{1,0:T(8,128)(2,1)} %get-tuple-element.56.dl_ref, ...), custom_call_target="tpu_custom_call" | custom-call | tf_op jit(solution)/shard_map/pallas_call | solution.py:1087
  177.0 96.1 %shard_map.221 = (bf16[128,2048]{1,0:T(8,128)(2,1)}, bf16[128,2048]{1,0:T(8,128)(2,1)}, bf16[64,8192]{1,0:T(8,128)(2,1)}, f32[128,2048]{1,0:T(8,128)}, f32[160,384]{1,0:T(8,128)}, /*index=5*/f32[8,128]{1,0:T(8,128)}) custom-call(f32[1280,128]{1,0:T(8,128)} %get-tuple-element.66.part_ref, f32[8,512]{1,0:T(8,128)} %get-tuple-element.67.stat_ref, ...), custom_call_target="tpu_custom_call" | custom-call | tf_op jit(solution)/shard_map/pallas_call | solution.py:1553
  273.1 4.6 %shard_map.222 = (bf16[1,128,2048]{2,1,0:T(8,128)(2,1)}, bf16[1,128,2048]{2,1,0:T(8,128)(2,1)}, f32[1,64]{1,0:T(1,128)}, f32[64,8192]{1,0:T(8,128)}, f32[4,128]{...) custom-call(bf16[128,2048]{1,0:T(8,128)(2,1)} %get-tuple-element.80., ...), custom_call_target="tpu_custom_call" | custom-call | tf_op jit(solution)/shard_map/pallas_call | solution.py:1628

commit v8 on v7

--- a/solution.py
+++ b/solution.py
@@ -227,6 +227,8 @@
 
 
 UP_HOPS = 2
+LINE1 = bf16
+LINE2 = bf16
 
 
 def k1_kernel(tok_ref, up_ref, w_ref, wout_ref, wx_ref, wdt_ref, gain_ref, lens_ref, convw_ref, convb_ref, dtb_ref, skip_ref,
@@ -456,8 +458,8 @@
     row_hop(xs_ref, 0, 1, normalize)
     for k in range(4, 8):
         relay(k)
+    row_start(up_ref, ups_ref, 4)
     row_hop(xs_ref, 0, 2, normalize)
-    row_start(up_ref, ups_ref, 4)
     for at in range(4):
         rank = flip(c, 1) * 4 + at
         landed(xs_ref.at[rows(rank)], xcr.at[at], sib)
@@ -592,7 +594,9 @@
         put(part_ref.at[far(theirs, p)], sib_ref.at[cut(p)], ss.at[p], sr.at[p], sib)
     for p in range(PIECES):
         landed(sib_ref.at[cut(p)], sr.at[p], sib)
-        base_ref[cut(p), :] = part_ref[far(mine, p), :] + sib_ref[cut(p), :]
+        value = part_ref[far(mine, p), :] + sib_ref[cut(p), :]
+        out_ref[far(mine, p), :] = value
+        base_ref[cut(p), :] = value.astype(base_ref.dtype)
 
         @pl.when(z == 0)
         def _():
@@ -609,7 +613,7 @@
 
         @pl.when(z < 3)
         def _():
-            tor_ref[cut(p), :] = base_ref[cut(p), :] + left_ref[cut(p), :]
+            tor_ref[cut(p), :] = (out_ref[far(mine, p), :] + left_ref[cut(p), :].astype(f32)).astype(tor_ref.dtype)
             put(tor_ref.at[cut(p)], left_ref.at[cut(p)], rs.at[p], lr.at[p], right)
 
     def from_right(p):
@@ -617,7 +621,7 @@
 
         @pl.when(z > 0)
         def _():
-            tol_ref[cut(p), :] = base_ref[cut(p), :] + right_ref[cut(p), :]
+            tol_ref[cut(p), :] = (out_ref[far(mine, p), :] + right_ref[cut(p), :].astype(f32)).astype(tol_ref.dtype)
             put(tol_ref.at[cut(p)], right_ref.at[cut(p)], ls.at[p], rr.at[p], left)
 
     @pl.when(z == 1)
@@ -643,15 +647,13 @@
             from_left(p)
 
     for p in range(PIECES):
-        out_ref[far(mine, p), :] = base_ref[cut(p), :]
-
         @pl.when(z > 0)
         def _():
-            out_ref[far(mine, p), :] += left_ref[cut(p), :]
+            out_ref[far(mine, p), :] += left_ref[cut(p), :].astype(f32)
 
         @pl.when(z < 3)
         def _():
-            out_ref[far(mine, p), :] += right_ref[cut(p), :]
+            out_ref[far(mine, p), :] += right_ref[cut(p), :].astype(f32)
 
         put(out_ref.at[far(mine, p)], out_ref.at[far(mine, p)], os_.at[p], or_.at[p], sib)
     late()
@@ -724,7 +726,7 @@
             pltpu.VMEM((groups, ways) + meta.shape, f32),
             pltpu.VMEM((packed, 128), f32),
             pltpu.VMEM((packed, 128), f32),
-        ] + [pltpu.VMEM((packed // 2, 128), f32)] * 6
+        ] + [pltpu.VMEM((packed // 2, 128), f32)] + [pltpu.VMEM((packed // 2, 128), LINE1)] * 5
         + [dma(8), dma(7), dma(7), dma(3), dma(3), dma(8), dma(8), dma(8), dma(8), dma(8), dma(8), dma(7), dma(7), dma(19), dma(19), dma(8), dma(8), dma(4), dma(4)]
         + [dma(PIECES) for _ in range(8)],
         compiler_params=pltpu.CompilerParams(collective_id=0, has_side_effects=True, vmem_limit_bytes=56 * 1024 * 1024),
@@ -811,28 +813,27 @@
         for part in range(0, 2 * wide, 512):
             hot_ref[:, part:part + 512] = jnp.where((row % 32 == col + part // 128) & (row < 96), 1.0, 0.0).astype(bf16)
 
-    lane = lax.broadcasted_iota(jnp.int32, (chunk, 128), 1)
+    lane = lax.broadcasted_iota(jnp.int32, (512, 128), 1)
 
     def spread(i, carry):
-        r = pl.ds(pl.multiple_of(i * chunk, chunk), chunk)
+        r = pl.ds(pl.multiple_of(i * 512, 512), 512)
         value = jnp.where(lane < 2 * states, kq_ref[r, :], 0.0)
         hi = value.astype(bf16).astype(f32)
         mid = (value - hi).astype(bf16).astype(f32)
         low = value - hi - mid
         left = (hi + pltpu.roll(mid, 32, 1) + pltpu.roll(low, 64, 1)).astype(bf16)
-        for part in range(0, 2 * wide, 512):
-            kb_ref[r, part:part + 512] = jnp.dot(left, hot_ref[:, part:part + 512], preferred_element_type=f32)
+        for part in range(0, 2 * wide, 256):
+            kb_ref[r, part:part + 256] = jnp.dot(left, hot_ref[:, part:part + 256], preferred_element_type=f32)
         return carry
 
-    lax.fori_loop(0, count // chunk, spread, 0)
+    lax.fori_loop(0, count // 512, spread, 0)
     cols = (((1,), (1,)), ((), ()))
 
     def gate_step(i, carry):
-        value = ups_ref[i // 2, pl.ds((i % 2) * 2, 2)].reshape(chunk, wout_ref.shape[1])
-        product = lax.dot_general(value, wout_ref[pl.ds(pl.multiple_of(half * width, width), width), :], cols, preferred_element_type=f32)
-        for j in range(chunk // length):
+        product = lax.dot_general(ups_ref[i].reshape(4 * length, wout_ref.shape[1]), wout_ref[pl.ds(pl.multiple_of(half * width, width), width), :], cols, preferred_element_type=f32)
+        for j in range(4):
             for n in both:
-                dm_ref[n, pl.ds(i * (chunk // length) + j, length, stride=8), :] = product[j * length:(j + 1) * length, n * 128:(n + 1) * 128]
+                dm_ref[n, pl.ds(i * 4 + j, length, stride=8), :] = product[j * length:(j + 1) * length, n * 128:(n + 1) * 128]
         return carry
 
     bias = vecs_ref[5:6, :]
@@ -911,7 +912,7 @@
     def _():
         complete()
 
-    lax.fori_loop(0, count // chunk, gate_step, 0)
+    lax.fori_loop(0, 2, gate_step, 0)
 
     def gates(i, carry):
         r = pl.ds(pl.multiple_of(i * 32, 32), 32)
@@ -1591,7 +1592,7 @@
             pltpu.VMEM((3, 8, 128), f32),
             dma(10), dma(14), dma(14), dma(7), dma(7), dma(3), dma(3),
             pltpu.VMEM((packed, 128), f32),
-        ] + [pltpu.VMEM((packed // 2, 128), f32)] * 6 + [dma(PIECES) for _ in range(8)]
+        ] + [pltpu.VMEM((packed // 2, 128), f32)] + [pltpu.VMEM((packed // 2, 128), LINE2)] * 5 + [dma(PIECES) for _ in range(8)]
         + row_scratch(length, model) * 2
         + flat_scratch(512, channels, bf16) * 2 + flat_scratch(128, model, bf16) + flat_scratch(160, 384, f32),
         compiler_params=pltpu.CompilerParams(collective_id=1, has_side_effects=True, vmem_limit_bytes=63400000),

time: 278 us -> 270 us (0.971)
  Pallas kernels: 277 us -> 270 us
    pallas_call x1, Pallas kernels: 102 us -> 95.4 us  [k1(): pl.pallas_call(k1_kernel, out_shape=(like((model, count), bf16), like((co...]
where the time goes in v8:
time: 270 us
  Pallas kernels  270 us (100%)
    pallas_call x1, Pallas kernels, k1(): pl.pallas_call(k1_kernel, out_shape=(like((model, count), bf16), like((co...  95.4 us
    pallas_call x1, Pallas kernels, k3(): pl.pallas_call(k3_kernel, out_shape=(like((length, model), bf16), like((l...  93.8 us
    pallas_call x1, Pallas kernels, k2(): pl.pallas_call(functools.partial(k2_kernel, states), grid=(channels // wi...  75.7 us

profile of v8, /device:TPU:8, one launch (start us, length us, event | category | flops | bytes accessed | tf_op | source)
XLA Modules:
  0.0 270.2 jit_solution(4183602829723268410)
XLA Ops:
  0.6 95.4 %shard_map.219 = (bf16[2048,1024]{1,0:T(8,128)(2,1)}, bf16[1024,2048]{1,0:T(8,128)(2,1)}, bf16[2048,1024]{1,0:T(8,128)(2,1)}, bf16[512,2048]{1,0:T(8,128)(2,1)},...) custom-call(bf16[1,128,2048]{2,1,0:T(8,128)(2,1)} %tok_ref.3, ...), custom_call_target="tpu_custom_call" | custom-call | tf_op jit(solution)/shard_map/pallas_call | solution.py:688
  96.1 75.7 %shard_map.220 = (bf16[4,128,2048]{2,1,0:T(8,128)(2,1)}, bf16[512,1024]{1,0:T(8,128)(2,1)}, bf16[1024,512]{1,0:T(8,128)(2,1)}, f32[512,128]{1,0:T(8,128)}, bf16[...) custom-call(bf16[1024,128]{1,0:T(8,128)(2,1)} %get-tuple-element.56.dl_ref, ...), custom_call_target="tpu_custom_call" | custom-call | tf_op jit(solution)/shard_map/pallas_call | solution.py:1088
  171.8 93.8 %shard_map.221 = (bf16[128,2048]{1,0:T(8,128)(2,1)}, bf16[128,2048]{1,0:T(8,128)(2,1)}, bf16[64,8192]{1,0:T(8,128)(2,1)}, f32[128,2048]{1,0:T(8,128)}, f32[160,384]{1,0:T(8,128)}, /*index=5*/f32[8,128]{1,0:T(8,128)}) custom-call(f32[1280,128]{1,0:T(8,128)} %get-tuple-element.66.part_ref, f32[8,512]{1,0:T(8,128)} %get-tuple-element.67.stat_ref, ...), custom_call_target="tpu_custom_call" | custom-call | tf_op jit(solution)/shard_map/pallas_call | solution.py:1554
  265.6 4.6 %shard_map.222 = (bf16[1,128,2048]{2,1,0:T(8,128)(2,1)}, bf16[1,128,2048]{2,1,0:T(8,128)(2,1)}, f32[1,64]{1,0:T(1,128)}, f32[64,8192]{1,0:T(8,128)}, f32[4,128]{...) custom-call(bf16[128,2048]{1,0:T(8,128)(2,1)} %get-tuple-element.80., ...), custom_call_target="tpu_custom_call" | custom-call | tf_op jit(solution)/shard_map/pallas_call | solution.py:1629

commit v9 on v8

--- a/solution.py
+++ b/solution.py
@@ -276,6 +276,10 @@
         return pl.ds(pl.multiple_of((group * 8 + rank) * depth, depth), depth)
 
     own_e = wout_ref.shape[0]
+    half_w = cols_ref.shape[2] // 2
+
+    def part_w(q):
+        return pl.ds(q * half_w, half_w)
 
     def part_e(group, start=0, size=own_e):
         return pl.ds(pl.multiple_of(group * own_e + start, 16), size)
@@ -296,16 +300,20 @@
         pending.append(put(meta_ref, metas_ref.at[d, j], ms.at[i], mr.at[i], to))
     for i, s in enumerate(steps):
         to = mate(s)
-        pending.append(put(cols_ref.at[rank_of(to)], win_ref.at[block(d, j)], as_.at[i], ar.at[i], to))
+        pending.append(put(cols_ref.at[rank_of(to), :, part_w(0)], win_ref.at[block(d, j), part_w(0)], as_.at[i], ar.at[i], to))
     for i, to in enumerate((xn, yn, dn)):
-        pending.append(put(small_ref, smalls_ref.at[part_e(d)], ps.at[16 + i], pr.at[16 + i], to))
+        pending.append(put(small_ref, smalls_ref.at[part_e(d)], ps.at[32 + i], pr.at[32 + i], to))
     halves = own_e // 2
     pending.append(put(wout_ref, wouts_ref.at[part_e(d)], ws.at[0], wr.at[0], xn))
     pending.append(put(wout_ref, wouts_ref.at[part_e(d)], ws.at[1], wr.at[1], yn))
     own[2].wait()
-    slot = win_ref.at[block(d, j)]
-    pending.append(put(slot, slot, ps.at[7], pr.at[7], xn))
-    pending.append(put(slot, slot, ps.at[15], pr.at[15], yn))
+
+    def own_part(q):
+        slot = win_ref.at[block(d, j), part_w(q)]
+        pending.append(put(slot, slot, ps.at[16 * q + 7], pr.at[16 * q + 7], xn))
+        pending.append(put(slot, slot, ps.at[16 * q + 15], pr.at[16 * q + 15], yn))
+
+    own_part(0)
 
     def row_start(ref, out, base):
         pending.append(put(ref.at[0], out.at[rows(j)], xcs.at[base + z], xcr.at[base + z], sib))
@@ -362,6 +370,7 @@
             def _():
                 sent(out.at[rows(j)], xcs.at[base + at], sib)
 
+    row_start(tok_ref, xs_ref, 0)
     own[5].wait()
     for i, s in enumerate(steps):
         landed(metas_ref.at[d, rank_of(mate(s, -1))], mr.at[i], xn)
@@ -372,25 +381,33 @@
         slots[i] = rank_of(mate(s, -1))
     order = [7] + list(range(7))
 
-    def pass_on(i):
+    def pass_on(i, q):
         src = mate(steps[i], -1)
-        slot = win_ref.at[block(d, slots[i])]
-        landed(slot, ar.at[i], src)
-        pending.append(put(slot, slot, ps.at[i], pr.at[i], xn))
-        pending.append(put(slot, slot, ps.at[8 + i], pr.at[8 + i], yn))
-
-    def relay(k):
+        slot = win_ref.at[block(d, slots[i]), part_w(q)]
+        landed(slot, ar.at[7 * q + i], src)
+        pending.append(put(slot, slot, ps.at[16 * q + i], pr.at[16 * q + i], xn))
+        pending.append(put(slot, slot, ps.at[16 * q + 8 + i], pr.at[16 * q + 8 + i], yn))
+
+    def relay(k, q):
         i = order[k]
-        slot = win_ref.at[block(dx, slots[i])]
-        landed(slot, pr.at[i], xn)
+        slot = win_ref.at[block(dx, slots[i]), part_w(q)]
+        landed(slot, pr.at[16 * q + i], xn)
         if k % 2 == 0:
-            pending.append(put(slot, slot, rs.at[k // 2], rr.at[k // 2], yn))
-        slot = win_ref.at[block(dy, slots[i])]
-        landed(slot, pr.at[8 + i], yn)
+            pending.append(put(slot, slot, rs.at[8 * q + k // 2], rr.at[8 * q + k // 2], yn))
+        slot = win_ref.at[block(dy, slots[i]), part_w(q)]
+        landed(slot, pr.at[16 * q + 8 + i], yn)
         if k % 2 == 1:
-            pending.append(put(slot, slot, rs.at[4 + k // 2], rr.at[4 + k // 2], xn))
-
-    pass_on(0)
+            pending.append(put(slot, slot, rs.at[8 * q + 4 + k // 2], rr.at[8 * q + 4 + k // 2], xn))
+
+    def relayed(q):
+        for k, i in enumerate(order):
+            slot = win_ref.at[block(dd, slots[i]), part_w(q)]
+            if k % 2 == 0:
+                landed(slot, rr.at[8 * q + k // 2], yn)
+            else:
+                landed(slot, rr.at[8 * q + 4 + k // 2], xn)
+
+    pass_on(0, 0)
     for i, (to, at) in enumerate(((xn, dx), (yn, dy), (dn, dd))):
         landed(metas_ref.at[at], qr.at[i], to)
     lens = jnp.concatenate([metas_ref[d, r, 1:2, :] for r in range(8)], axis=0)
@@ -437,7 +454,7 @@
         lax.fori_loop(0, length // 16, body, 0, unroll=4)
 
     for i in range(1, 4):
-        pass_on(i)
+        pass_on(i, 0)
     slot = wouts_ref.at[part_e(dx)]
     landed(slot, wr.at[0], xn)
     slot = wouts_ref.at[part_e(dx, 0, halves)]
@@ -447,31 +464,28 @@
     slot = wouts_ref.at[part_e(dy, halves, halves)]
     pending.append(put(slot, slot, ws.at[3], wr.at[3], xn))
 
-    row_start(tok_ref, xs_ref, 0)
     for i in range(4, 7):
-        pass_on(i)
+        pass_on(i, 0)
     own[0].wait()
     normalize(j)
     row_hop(xs_ref, 0, 0, normalize)
-    for k in range(4):
-        relay(k)
+    for i, s in enumerate(steps):
+        to = mate(s)
+        pending.append(put(cols_ref.at[rank_of(to), :, part_w(1)], win_ref.at[block(d, j), part_w(1)], as_.at[7 + i], ar.at[7 + i], to))
+    own_part(1)
+    for k in range(8):
+        relay(k, 0)
     row_hop(xs_ref, 0, 1, normalize)
-    for k in range(4, 8):
-        relay(k)
+    for i in range(7):
+        pass_on(i, 1)
     row_start(up_ref, ups_ref, 4)
     row_hop(xs_ref, 0, 2, normalize)
     for at in range(4):
         rank = flip(c, 1) * 4 + at
         landed(xs_ref.at[rows(rank)], xcr.at[at], sib)
         normalize(rank)
-    for k, i in enumerate(order):
-        slot = win_ref.at[block(dd, slots[i])]
-        if k % 2 == 0:
-            landed(slot, rr.at[k // 2], yn)
-        else:
-            landed(slot, rr.at[4 + k // 2], xn)
+    relayed(0)
     own += [pltpu.make_async_copy(xnt_ref, xnt_out, own_sem.at[6]), pltpu.make_async_copy(win_ref, win_out, own_sem.at[7])]
-    own[7].start()
     lead = u_ref.shape[1] - count
     u_ref[:, 0:lead, :] = jnp.zeros((tiles, lead, 128), f32)
 
@@ -504,10 +518,12 @@
         return carry
 
     lax.fori_loop(0, count // 32, conv_step, 0, unroll=2)
+    for k in range(8):
+        relay(k, 1)
     for copy in own[3:5]:
         copy.wait()
     for i, (to, at) in enumerate(((xn, dx), (yn, dy), (dn, dd))):
-        landed(smalls_ref.at[part_e(at)], pr.at[16 + i], to)
+        landed(smalls_ref.at[part_e(at)], pr.at[32 + i], to)
     quarter = count // 4
     narrow = smalls_ref[:, 128:256].astype(f32)
     packed = jnp.zeros((quarter, 128), f32)
@@ -527,6 +543,8 @@
         row_hop(ups_ref, 4, 0, None, UP_HOPS)
 
     def between():
+        relayed(1)
+        own[7].start()
         spread(g_ref, 0, width)
         saves[5].start()
 
@@ -727,7 +745,7 @@
             pltpu.VMEM((packed, 128), f32),
             pltpu.VMEM((packed, 128), f32),
         ] + [pltpu.VMEM((packed // 2, 128), f32)] + [pltpu.VMEM((packed // 2, 128), LINE1)] * 5
-        + [dma(8), dma(7), dma(7), dma(3), dma(3), dma(8), dma(8), dma(8), dma(8), dma(8), dma(8), dma(7), dma(7), dma(19), dma(19), dma(8), dma(8), dma(4), dma(4)]
+        + [dma(8), dma(7), dma(7), dma(3), dma(3), dma(8), dma(8), dma(8), dma(8), dma(8), dma(8), dma(14), dma(14), dma(35), dma(35), dma(16), dma(16), dma(4), dma(4)]
         + [dma(PIECES) for _ in range(8)],
         compiler_params=pltpu.CompilerParams(collective_id=0, has_side_effects=True, vmem_limit_bytes=56 * 1024 * 1024),
     )(tokens, upstream, w_in, w_out, w_x, w_dt, gain, lengths, conv_w, conv_b, dt_bias, skip)

time: 270 us -> 267 us (0.989)
  Pallas kernels: 270 us -> 266 us
    pallas_call x1, Pallas kernels: 95.4 us -> 91.9 us  [k1(): pl.pallas_call(k1_kernel, out_shape=(like((model, count), bf16), like((co...]
where the time goes in v9:
time: 267 us
  Pallas kernels  266 us (100%)
    pallas_call x1, Pallas kernels, k3(): pl.pallas_call(k3_kernel, out_shape=(like((length, model), bf16), like((l...  93.8 us
    pallas_call x1, Pallas kernels, k1(): pl.pallas_call(k1_kernel, out_shape=(like((model, count), bf16), like((co...  91.9 us
    pallas_call x1, Pallas kernels, k2(): pl.pallas_call(functools.partial(k2_kernel, states), grid=(channels // wi...  75.8 us

profile of v9, /device:TPU:8, one launch (start us, length us, event | category | flops | bytes accessed | tf_op | source)
XLA Modules:
  0.0 266.8 jit_solution(16899356422188389560)
XLA Ops:
  0.6 91.9 %shard_map.219 = (bf16[2048,1024]{1,0:T(8,128)(2,1)}, bf16[1024,2048]{1,0:T(8,128)(2,1)}, bf16[2048,1024]{1,0:T(8,128)(2,1)}, bf16[512,2048]{1,0:T(8,128)(2,1)},...) custom-call(bf16[1,128,2048]{2,1,0:T(8,128)(2,1)} %tok_ref.3, ...), custom_call_target="tpu_custom_call" | custom-call | tf_op jit(solution)/shard_map/pallas_call | solution.py:706
  92.6 75.8 %shard_map.220 = (bf16[4,128,2048]{2,1,0:T(8,128)(2,1)}, bf16[512,1024]{1,0:T(8,128)(2,1)}, bf16[1024,512]{1,0:T(8,128)(2,1)}, f32[512,128]{1,0:T(8,128)}, bf16[...) custom-call(bf16[1024,128]{1,0:T(8,128)(2,1)} %get-tuple-element.56.dl_ref, ...), custom_call_target="tpu_custom_call" | custom-call | tf_op jit(solution)/shard_map/pallas_call | solution.py:1106
  168.3 93.8 %shard_map.221 = (bf16[128,2048]{1,0:T(8,128)(2,1)}, bf16[128,2048]{1,0:T(8,128)(2,1)}, bf16[64,8192]{1,0:T(8,128)(2,1)}, f32[128,2048]{1,0:T(8,128)}, f32[160,384]{1,0:T(8,128)}, /*index=5*/f32[8,128]{1,0:T(8,128)}) custom-call(f32[1280,128]{1,0:T(8,128)} %get-tuple-element.66.part_ref, f32[8,512]{1,0:T(8,128)} %get-tuple-element.67.stat_ref, ...), custom_call_target="tpu_custom_call" | custom-call | tf_op jit(solution)/shard_map/pallas_call | solution.py:1572
  262.2 4.6 %shard_map.222 = (bf16[1,128,2048]{2,1,0:T(8,128)(2,1)}, bf16[1,128,2048]{2,1,0:T(8,128)(2,1)}, f32[1,64]{1,0:T(1,128)}, f32[64,8192]{1,0:T(8,128)}, f32[4,128]{...) custom-call(bf16[128,2048]{1,0:T(8,128)(2,1)} %get-tuple-element.80., ...), custom_call_target="tpu_custom_call" | custom-call | tf_op jit(solution)/shard_map/pallas_call | solution.py:1647

commit v10 on v9

--- a/solution.py
+++ b/solution.py
@@ -223,7 +223,7 @@
     return device[1] * 4 + device[2]
 
 
-PIECES = 4
+PIECES = 2
 
 
 UP_HOPS = 2
@@ -1239,7 +1239,7 @@
             dst[r, :] = value.astype(dst.dtype)
         return carry
 
-    lax.fori_loop(0, rows // step, body, 0)
+    lax.fori_loop(0, rows // step, body, 0, unroll=2)
 
 
 class Flat:
@@ -1462,13 +1462,11 @@
             dc_ref[n, r, :] = du
             return tuple(sums)
 
-        sums = lax.fori_loop(0, count // 32, conv_step, (jnp.zeros((8, 128), f32),) * 5)
-        smallp[n, 128:160, :] = jnp.zeros((32, 384), f32)
-        for k in range(5):
-            smallp[n, 128 + k:129 + k, 0:128] = jnp.sum(sums[k], axis=0, keepdims=True)
-        smallp[n, 133:134, 0:128] = stat_ref[5:6, lanes]
-        smallp[n, 134:135, 0:128] = stat_ref[6:7, lanes]
-        smallp[n, 0:128, 256:384] = gwdt_ref[n * 128:(n + 1) * 128, :]
+        sums = lax.fori_loop(0, count // 32, conv_step, (jnp.zeros((8, 128), f32),) * 5, unroll=2)
+        tops = jnp.concatenate([jnp.sum(sums[k], axis=0, keepdims=True) for k in range(5)] + [stat_ref[5:6, lanes], stat_ref[6:7, lanes], jnp.zeros((25, 128), f32)], axis=0)
+        smallp[n, 128:160, :] = jnp.zeros((32, 384), bf16)
+        smallp[n, 128:160, 0:128] = tops.astype(bf16)
+        smallp[n, 0:128, 256:384] = gwdt_ref[n * 128:(n + 1) * 128, :].astype(bf16)
 
     def by_row(i, carry):
         r = pl.ds(pl.multiple_of(i * length, length), length)
@@ -1492,10 +1490,10 @@
     weight_rows(up, 0, d)
     vt_copy.wait()
     for n in range(tiles):
-        smallp[n, 0:128, 0:256] = jnp.dot(mt_ref[n * 128:(n + 1) * 128, :], dp_ref[...], preferred_element_type=f32)
+        smallp[n, 0:128, 0:256] = jnp.dot(mt_ref[n * 128:(n + 1) * 128, :], dp_ref[...], preferred_element_type=f32).astype(bf16)
+    flats[0].middle()
     small_flat.start_far()
     small_flat.start_near()
-    flats[0].middle()
     out_row.along(2, row_ref)
 
     def block_step(i, carry):
@@ -1524,7 +1522,7 @@
         gtok_ref[r, :] = (up_ref[0, r, :].astype(f32) + dxx).astype(bf16)
         return carry
 
-    lax.fori_loop(0, length // 16, norm_step, 0)
+    lax.fori_loop(0, length // 16, norm_step, 0, unroll=2)
     outs[1].start()
     small_flat.finish(small_ref)
     outs[4].start()
@@ -1594,7 +1592,7 @@
             pltpu.VMEM((4, 512, channels), bf16),
             pltpu.VMEM((4, 512, channels), bf16),
             pltpu.VMEM((4, 128, model), bf16),
-            pltpu.VMEM((4, 160, 384), f32),
+            pltpu.VMEM((4, 160, 384), bf16),
             pltpu.VMEM((channels, count), bf16),
             pltpu.VMEM((count, 2 * channels), bf16),
             pltpu.VMEM((tiles, count + 32, 128), f32),
@@ -1612,7 +1610,7 @@
             pltpu.VMEM((packed, 128), f32),
         ] + [pltpu.VMEM((packed // 2, 128), f32)] + [pltpu.VMEM((packed // 2, 128), LINE2)] * 5 + [dma(PIECES) for _ in range(8)]
         + row_scratch(length, model) * 2
-        + flat_scratch(512, channels, bf16) * 2 + flat_scratch(128, model, bf16) + flat_scratch(160, 384, f32),
+        + flat_scratch(512, channels, bf16) * 2 + flat_scratch(128, model, bf16) + flat_scratch(160, 384, bf16),
         compiler_params=pltpu.CompilerParams(collective_id=1, has_side_effects=True, vmem_limit_bytes=63400000),
     )(part, stat, smalls, vecs, gains, gwdt, masks, tokens, upstream, acc, mt, dg, dv, slope, u, vt, xnt, win, ups)
 

time: 267 us -> 266 us (level)
  no operation moved by 1% of the time
where the time goes in v10:
time: 266 us
  Pallas kernels  265 us (100%)
    pallas_call x1, Pallas kernels, k3(): pl.pallas_call(k3_kernel, out_shape=(like((length, model), bf16), like((l...  93.3 us
    pallas_call x1, Pallas kernels, k1(): pl.pallas_call(k1_kernel, out_shape=(like((model, count), bf16), like((co...  91.8 us
    pallas_call x1, Pallas kernels, k2(): pl.pallas_call(functools.partial(k2_kernel, states), grid=(channels // wi...  75.8 us

profile of v10, /device:TPU:8, one launch (start us, length us, event | category | flops | bytes accessed | tf_op | source)
XLA Modules:
  0.0 266.1 jit_solution(4599611970900202700)
XLA Ops:
  0.6 91.8 %shard_map.219 = (bf16[2048,1024]{1,0:T(8,128)(2,1)}, bf16[1024,2048]{1,0:T(8,128)(2,1)}, bf16[2048,1024]{1,0:T(8,128)(2,1)}, bf16[512,2048]{1,0:T(8,128)(2,1)},...) custom-call(bf16[1,128,2048]{2,1,0:T(8,128)(2,1)} %tok_ref.3, ...), custom_call_target="tpu_custom_call" | custom-call | tf_op jit(solution)/shard_map/pallas_call | solution.py:706
  92.4 75.8 %shard_map.220 = (bf16[4,128,2048]{2,1,0:T(8,128)(2,1)}, bf16[512,1024]{1,0:T(8,128)(2,1)}, bf16[1024,512]{1,0:T(8,128)(2,1)}, f32[512,128]{1,0:T(8,128)}, bf16[...) custom-call(bf16[1024,128]{1,0:T(8,128)(2,1)} %get-tuple-element.56.dl_ref, ...), custom_call_target="tpu_custom_call" | custom-call | tf_op jit(solution)/shard_map/pallas_call | solution.py:1106
  168.2 93.3 %shard_map.221 = (bf16[128,2048]{1,0:T(8,128)(2,1)}, bf16[128,2048]{1,0:T(8,128)(2,1)}, bf16[64,8192]{1,0:T(8,128)(2,1)}, f32[128,2048]{1,0:T(8,128)}, f32[160,384]{1,0:T(8,128)}, /*index=5*/f32[8,128]{1,0:T(8,128)}) custom-call(f32[1280,128]{1,0:T(8,128)} %get-tuple-element.66.part_ref, f32[8,512]{1,0:T(8,128)} %get-tuple-element.67.stat_ref, ...), custom_call_target="tpu_custom_call" | custom-call | tf_op jit(solution)/shard_map/pallas_call | solution.py:1570
  261.5 4.6 %shard_map.222 = (bf16[1,128,2048]{2,1,0:T(8,128)(2,1)}, bf16[1,128,2048]{2,1,0:T(8,128)(2,1)}, f32[1,64]{1,0:T(1,128)}, f32[64,8192]{1,0:T(8,128)}, f32[4,128]{...) custom-call(bf16[128,2048]{1,0:T(8,128)(2,1)} %get-tuple-element.80., ...), custom_call_target="tpu_custom_call" | custom-call | tf_op jit(solution)/shard_map/pallas_call | solution.py:1645
